TPU v7x, 32 devices: a whole 2x2x4 slice. The times are simulated.
32 devices in a mesh: ctx: 16 (over z, y, core), fsdp: 2 (over x).
Axes of the slice: x: 2, y: 2, z: 4, core: 2. Of those that a mesh axis runs over, the one named last changes fastest.
Arguments:
- hidden_in: bfloat16 [2, 4096, 2048], P('fsdp', 'ctx'), may hold values from -6 to 6
- norm_gain: float32 [2048], P(('ctx', 'fsdp')), may hold values from 0.5 to 1.5
- in_proj: float32 [2048, 8192], P(('ctx', 'fsdp')), may hold values from -0.125 to 0.125
- conv_weight: float32 [4, 4096], P(None, ('ctx', 'fsdp')), may hold values from -3 to 3
- conv_bias: float32 [4096], P(('ctx', 'fsdp')), may hold values from -3 to 3
- state_proj: float32 [4096, 160], P(('ctx', 'fsdp')), may hold values from -0.09375 to 0.09375
- delta_proj: float32 [128, 4096], P(None, ('ctx', 'fsdp')), may hold values from -0.5 to 0.5
- delta_bias: float32 [4096], P(('ctx', 'fsdp')), may hold values from -4 to -2
- decay_log: float32 [16, 4096], P(None, ('ctx', 'fsdp')), may hold values from -9 to -0.5
- skip_gain: float32 [4096], P(('ctx', 'fsdp')), may hold values from 0.03 to 20, as said below
- out_proj: float32 [4096, 2048], P(('ctx', 'fsdp')), may hold values from -0.09375 to 0.09375
- cotangent: bfloat16 [2, 4096, 2048], P('fsdp', 'ctx'), may hold values from -6 to 6
Outputs:
- block_out: bfloat16 [2, 4096, 2048], P('fsdp', 'ctx')
- input_grad: bfloat16 [2, 4096, 2048], P('fsdp', 'ctx')
- norm_gain_grad: float32 [2048], P(('ctx', 'fsdp'))
- in_proj_grad: float32 [2048, 8192], P(('ctx', 'fsdp'))
- conv_weight_grad: float32 [4, 4096], P(None, ('ctx', 'fsdp'))
- conv_bias_grad: float32 [4096], P(('ctx', 'fsdp'))
- state_proj_grad: float32 [4096, 160], P(('ctx', 'fsdp'))
- delta_proj_grad: float32 [128, 4096], P(None, ('ctx', 'fsdp'))
- delta_bias_grad: float32 [4096], P(('ctx', 'fsdp'))
- decay_log_grad: float32 [16, 4096], P(None, ('ctx', 'fsdp'))
- skip_gain_grad: float32 [4096], P(('ctx', 'fsdp'))
- out_proj_grad: float32 [4096, 2048], P(('ctx', 'fsdp'))
Inputs may be any that keep to these rules, and one draw needn't show every extreme that they name: `skip_gain`: positive skip coefficients.
All inputs are finite; a program needn't handle non-finite values.
Results may differ from a plain program's by a relative error of at most 0.012.
The roundings to bfloat16 on the way count: a program that leaves them out, or rounds other values in their place, can miss the bound.
Values may be sent and summed in bfloat16 or wider, within the bound.
A program may use at most 384 MiB of HBM per device.

v0:
```python
import jax
import jax.numpy as jnp
from jax import lax
from jax.sharding import PartitionSpec as P

D = 2048
DI = 4096
STATE = 16
DT_RANK = 128
KW = 4


EPS = 1e-05


def passed_along(shard, axis, by):
    length = lax.axis_size(axis)
    pairs = [(i, i + by) for i in range(length) if 0 <= i + by < length]
    return lax.ppermute(shard, axis, pairs)


def silu_slope(value):
    sigma = jax.nn.sigmoid(value)
    return sigma * (1.0 + value * (1.0 - sigma))


def contract_rows(left, right):
    return lax.dot_general(
        left, right, (((0,), (0,)), ((), ())), preferred_element_type=jnp.float32
    )


def contract_cols(left, right):
    return lax.dot_general(
        left, right, (((1,), (1,)), ((), ())), preferred_element_type=jnp.float32
    )


def shards(
    hidden_in,
    norm_gain,
    in_proj,
    conv_weight,
    conv_bias,
    state_proj,
    delta_proj,
    delta_bias,
    decay_log,
    skip_gain,
    out_proj,
    cotangent,
):
    tokens = hidden_in.shape[1]
    span = 16
    blocks = tokens // span
    hidden = hidden_in.reshape(tokens, D).astype(jnp.float32)
    inv_rms = lax.rsqrt(jnp.mean(hidden * hidden, axis=1, keepdims=True) + EPS)
    unit_rows = hidden * inv_rms
    gain_low = norm_gain.astype(jnp.bfloat16)
    in_low = in_proj.astype(jnp.bfloat16)
    kernel_low = conv_weight.astype(jnp.bfloat16)
    cbias_low = conv_bias.astype(jnp.bfloat16)
    sproj_low = state_proj.astype(jnp.bfloat16)
    dproj_low = delta_proj.astype(jnp.bfloat16)
    dbias_low = delta_bias.astype(jnp.bfloat16)
    decay_low = decay_log.astype(jnp.bfloat16)
    skip_low = skip_gain.astype(jnp.bfloat16)
    oproj_low = out_proj.astype(jnp.bfloat16)
    gain_piece = lax.all_gather(gain_low, ("ctx", "fsdp"), axis=0, tiled=True)
    weight_piece = lax.all_gather(in_low, ("ctx", "fsdp"), axis=0, tiled=True)
    columns = unit_rows
    normed_piece = (columns * gain_piece.astype(jnp.float32)[None, :]).astype(jnp.bfloat16)
    proj_sum = jnp.dot(normed_piece, weight_piece, preferred_element_type=jnp.float32)
    kernel, bias_conv, state_full, delta_full, delta_shift, decay_full, skip_full, out_full = (
        lax.all_gather(kernel_low, ("ctx", "fsdp"), axis=1, tiled=True),
        lax.all_gather(cbias_low, ("ctx", "fsdp"), axis=0, tiled=True),
        lax.all_gather(sproj_low, ("ctx", "fsdp"), axis=0, tiled=True),
        lax.all_gather(dproj_low, ("ctx", "fsdp"), axis=1, tiled=True),
        lax.all_gather(dbias_low, ("ctx", "fsdp"), axis=0, tiled=True),
        lax.all_gather(decay_low, ("ctx", "fsdp"), axis=1, tiled=True),
        lax.all_gather(skip_low, ("ctx", "fsdp"), axis=0, tiled=True),
        lax.all_gather(oproj_low, ("ctx", "fsdp"), axis=0, tiled=True),
    )
    mixed = proj_sum.astype(jnp.bfloat16)
    conv_in = mixed[:, :DI]
    gate_in = mixed[:, DI:].astype(jnp.float32)
    edge_rows = passed_along(conv_in[tokens - (KW - 1) :], "ctx", 1)
    padded = jnp.concatenate([edge_rows, conv_in], axis=0).astype(jnp.float32)

    def convolve(taps, shift_row):
        taps_float = taps.astype(jnp.float32)
        result = jnp.broadcast_to(shift_row.astype(jnp.float32)[None, :], (tokens, DI))
        for offset in range(KW):
            result = result + taps_float[offset][None, :] * padded[offset : offset + tokens]
        return result

    conv_out = convolve(kernel, bias_conv)
    activated = jax.nn.silu(conv_out).astype(jnp.bfloat16)
    act_float = activated.astype(jnp.float32)
    selected = jnp.dot(activated, state_full, preferred_element_type=jnp.float32)
    delta_in = selected[:, :DT_RANK].astype(jnp.bfloat16)
    in_coef = selected[:, DT_RANK : DT_RANK + STATE]
    out_coef = selected[:, DT_RANK + STATE :]
    delta_pre = (
        jnp.dot(delta_in, delta_full, preferred_element_type=jnp.float32)
        + delta_shift.astype(jnp.float32)[None, :]
    )
    delta = jax.nn.softplus(delta_pre)
    decay_rate = -jnp.exp(decay_full.astype(jnp.float32))

    def split(value):
        return value.reshape(blocks, span, value.shape[1])

    def forward_block(running, piece):
        state, elapsed = running
        delta_blk, act_blk, in_blk, out_blk = piece
        first_state = state
        first_elapsed = elapsed
        outputs = []
        elapsed_rows = []
        for position in range(span):
            delta_row = delta_blk[position]
            state = (
                jnp.exp(delta_row[None, :] * decay_rate) * state
                + in_blk[position][:, None] * (delta_row * act_blk[position])[None, :]
            )
            outputs.append(jnp.sum(out_blk[position][:, None] * state, axis=0))
            elapsed = elapsed + delta_row
            elapsed_rows.append(elapsed)
        return (
            (state, elapsed),
            (first_state, first_elapsed, jnp.stack(outputs), jnp.stack(elapsed_rows)),
        )

    empty_state = jnp.zeros((STATE, DI), jnp.float32)
    (local_end, elapsed_end), (block_starts, start_elapsed, local_out, elapsed_all) = lax.scan(
        forward_block,
        (empty_state, jnp.zeros((DI,), jnp.float32)),
        (split(delta), split(act_float), split(in_coef), split(out_coef)),
    )
    total_decay = jnp.exp(decay_rate * elapsed_end[None, :])

    def relay(index, held):
        return passed_along(total_decay * held + local_end, "ctx", 1)

    state_in = lax.fori_loop(0, lax.axis_size("ctx") - 1, relay, empty_state)

    def carried(piece):
        elapsed_blk, out_blk = piece
        decays = jnp.exp(decay_rate[None, :, :] * elapsed_blk[:, None, :])
        return jnp.sum(out_blk[:, :, None] * decays * state_in[None, :, :], axis=1)

    carried_out = lax.map(carried, (elapsed_all, split(out_coef)))
    scanned = (local_out + carried_out).reshape(tokens, DI) + skip_full.astype(jnp.float32)[
        None, :
    ] * act_float
    gate_act = jax.nn.silu(gate_in)
    gated = (scanned * gate_act).astype(jnp.bfloat16)
    block_out = (hidden + jnp.dot(gated, out_full, preferred_element_type=jnp.float32)).astype(
        jnp.bfloat16
    )
    cot_rows = cotangent.reshape(tokens, D)
    kernel_b, bias_b, state_b, delta_b, shift_b, decay_b, skip_b, out_b = (
        lax.all_gather(kernel_low, ("ctx", "fsdp"), axis=1, tiled=True),
        lax.all_gather(cbias_low, ("ctx", "fsdp"), axis=0, tiled=True),
        lax.all_gather(sproj_low, ("ctx", "fsdp"), axis=0, tiled=True),
        lax.all_gather(dproj_low, ("ctx", "fsdp"), axis=1, tiled=True),
        lax.all_gather(dbias_low, ("ctx", "fsdp"), axis=0, tiled=True),
        lax.all_gather(decay_low, ("ctx", "fsdp"), axis=1, tiled=True),
        lax.all_gather(skip_low, ("ctx", "fsdp"), axis=0, tiled=True),
        lax.all_gather(oproj_low, ("ctx", "fsdp"), axis=0, tiled=True),
    )
    conv_back = convolve(kernel_b, bias_b)
    delta_pre_b = (
        jnp.dot(delta_in, delta_b, preferred_element_type=jnp.float32)
        + shift_b.astype(jnp.float32)[None, :]
    )
    delta_back = jax.nn.softplus(delta_pre_b)
    rate_b = -jnp.exp(decay_b.astype(jnp.float32))
    d_gated = contract_cols(cot_rows, out_b)
    d_scanned = d_gated * gate_act
    d_gate = d_gated * scanned * silu_slope(gate_in)
    skip_grad = jnp.sum(d_scanned * act_float, axis=0)

    def adjoint_part(piece):
        elapsed_blk, out_blk, dscan_blk = piece
        decays = jnp.exp(rate_b[None, :, :] * elapsed_blk[:, None, :])
        return jnp.sum(decays * out_blk[:, :, None] * dscan_blk[:, None, :], axis=0)

    local_adjoint = jnp.sum(
        lax.map(adjoint_part, (elapsed_all, split(out_coef), split(d_scanned))), axis=0
    )

    def relay_back(index, held):
        return passed_along(total_decay * held + local_adjoint, "ctx", -1)

    adjoint_end = lax.fori_loop(0, lax.axis_size("ctx") - 1, relay_back, empty_state)
    starts_true = (
        block_starts
        + jnp.exp(rate_b[None, :, :] * start_elapsed[:, None, :]) * state_in[None, :, :]
    )

    def backward_block(running, piece):
        adjoint, rate_sum = running
        start_state, delta_blk, act_blk, in_blk, out_blk, dscan_blk = piece
        states = []
        decays = []
        state = start_state
        for position in range(span):
            decay = jnp.exp(delta_blk[position][None, :] * rate_b)
            state = (
                decay * state
                + in_blk[position][:, None] * (delta_blk[position] * act_blk[position])[None, :]
            )
            decays.append(decay)
            states.append(state)
        delta_rows = [None] * span
        act_rows = [None] * span
        in_rows_grad = [None] * span
        out_rows_grad = [None] * span
        for position in reversed(range(span)):
            previous = states[position - 1] if position > 0 else start_state
            out_rows_grad[position] = jnp.sum(
                dscan_blk[position][None, :] * states[position], axis=1
            )
            adjoint = adjoint + out_blk[position][:, None] * dscan_blk[position][None, :]
            through = adjoint * previous * decays[position]
            coef_sum = jnp.sum(in_blk[position][:, None] * adjoint, axis=0)
            delta_rows[position] = jnp.sum(through * rate_b, axis=0) + act_blk[position] * coef_sum
            act_rows[position] = delta_blk[position] * coef_sum
            in_rows_grad[position] = jnp.sum(
                adjoint * (delta_blk[position] * act_blk[position])[None, :], axis=1
            )
            rate_sum = rate_sum + through * delta_blk[position][None, :]
            adjoint = adjoint * decays[position]
        return (
            (adjoint, rate_sum),
            (
                jnp.stack(delta_rows),
                jnp.stack(act_rows),
                jnp.stack(in_rows_grad),
                jnp.stack(out_rows_grad),
            ),
        )

    (spent, rate_grad), (d_delta, d_act_scan, d_in_coef, d_out_coef) = lax.scan(
        backward_block,
        (adjoint_end, empty_state),
        (
            starts_true,
            split(delta_back),
            split(act_float),
            split(in_coef),
            split(out_coef),
            split(d_scanned),
        ),
        reverse=True,
    )
    decay_grad = rate_grad * rate_b
    d_delta_pre = d_delta.reshape(tokens, DI) * jax.nn.sigmoid(delta_pre_b)
    shift_grad = jnp.sum(d_delta_pre, axis=0)
    d_delta_low = d_delta_pre.astype(jnp.bfloat16)
    dproj_grad = contract_rows(delta_in, d_delta_low)
    d_delta_in = contract_cols(d_delta_low, delta_b)
    d_selected = jnp.concatenate(
        [d_delta_in, d_in_coef.reshape(tokens, STATE), d_out_coef.reshape(tokens, STATE)], axis=1
    ).astype(jnp.bfloat16)
    sproj_grad = contract_rows(activated, d_selected)
    d_activated = (
        d_act_scan.reshape(tokens, DI)
        + skip_b.astype(jnp.float32)[None, :] * d_scanned
        + contract_cols(d_selected, state_b)
    )
    d_conv = d_activated * silu_slope(conv_back)
    cbias_grad = jnp.sum(d_conv, axis=0)
    kernel_grad = jnp.stack(
        [jnp.sum(d_conv * padded[offset : offset + tokens], axis=0) for offset in range(KW)]
    )
    next_rows = passed_along(d_conv[: KW - 1], "ctx", -1)
    grad_padded = jnp.concatenate([d_conv, next_rows], axis=0)
    kernel_bf = kernel_b.astype(jnp.float32)
    d_conv_in = jnp.zeros((tokens, DI), jnp.float32)
    for offset in range(KW):
        d_conv_in = (
            d_conv_in
            + kernel_bf[offset][None, :] * grad_padded[KW - 1 - offset : KW - 1 - offset + tokens]
        )
    d_mixed = jnp.concatenate([d_conv_in, d_gate], axis=1).astype(jnp.bfloat16)
    start = jnp.int32(0)
    unit_grad = jnp.zeros((tokens, D), jnp.float32)
    gain_sum = jnp.zeros((D,), jnp.float32)
    gain_piece = lax.all_gather(gain_low, ("ctx", "fsdp"), axis=0, tiled=True)
    weight_piece = lax.all_gather(in_low, ("ctx", "fsdp"), axis=0, tiled=True)
    normed_grad = contract_cols(d_mixed, weight_piece)
    columns = unit_rows
    unit_grad = lax.dynamic_update_slice_in_dim(
        unit_grad, normed_grad * gain_piece.astype(jnp.float32)[None, :], start, 1
    )
    gain_sum = lax.dynamic_update_slice_in_dim(
        gain_sum, jnp.sum(normed_grad * columns, axis=0), start, 0
    )
    out_grad = contract_rows(gated, cot_rows)
    in_grad = lax.psum_scatter(
        contract_rows(normed_piece, d_mixed), ("ctx", "fsdp"), scatter_dimension=0, tiled=True
    )
    kernel_g, cbias_g, sproj_g, dproj_g, shift_g, decay_g, skip_g, out_g, gain_g = (
        lax.psum_scatter(kernel_grad, ("ctx", "fsdp"), scatter_dimension=1, tiled=True),
        lax.psum_scatter(cbias_grad, ("ctx", "fsdp"), scatter_dimension=0, tiled=True),
        lax.psum_scatter(sproj_grad, ("ctx", "fsdp"), scatter_dimension=0, tiled=True),
        lax.psum_scatter(dproj_grad, ("ctx", "fsdp"), scatter_dimension=1, tiled=True),
        lax.psum_scatter(shift_grad, ("ctx", "fsdp"), scatter_dimension=0, tiled=True),
        lax.psum_scatter(decay_grad, ("ctx", "fsdp"), scatter_dimension=1, tiled=True),
        lax.psum_scatter(skip_grad, ("ctx", "fsdp"), scatter_dimension=0, tiled=True),
        lax.psum_scatter(out_grad, ("ctx", "fsdp"), scatter_dimension=0, tiled=True),
        lax.psum_scatter(gain_sum, ("ctx", "fsdp"), scatter_dimension=0, tiled=True),
    )
    mean_term = jnp.mean(unit_grad * unit_rows, axis=1, keepdims=True)
    d_hidden = inv_rms * (unit_grad - unit_rows * mean_term)
    input_grad = (cot_rows.astype(jnp.float32) + d_hidden).astype(jnp.bfloat16)
    return (
        block_out.reshape(1, tokens, D),
        input_grad.reshape(1, tokens, D),
        gain_g,
        in_grad,
        kernel_g,
        cbias_g,
        sproj_g,
        dproj_g,
        shift_g,
        decay_g,
        skip_g,
        out_g,
    )


def solution(mesh):
    in_specs = (
        P("fsdp", "ctx", None),
        P(("ctx", "fsdp")),
        P(("ctx", "fsdp"), None),
        P(None, ("ctx", "fsdp")),
        P(("ctx", "fsdp")),
        P(("ctx", "fsdp"), None),
        P(None, ("ctx", "fsdp")),
        P(("ctx", "fsdp")),
        P(None, ("ctx", "fsdp")),
        P(("ctx", "fsdp")),
        P(("ctx", "fsdp"), None),
        P("fsdp", "ctx", None),
    )
    out_specs = (
        P("fsdp", "ctx", None),
        P("fsdp", "ctx", None),
        P(("ctx", "fsdp")),
        P(("ctx", "fsdp"), None),
        P(None, ("ctx", "fsdp")),
        P(("ctx", "fsdp")),
        P(("ctx", "fsdp"), None),
        P(None, ("ctx", "fsdp")),
        P(("ctx", "fsdp")),
        P(None, ("ctx", "fsdp")),
        P(("ctx", "fsdp")),
        P(("ctx", "fsdp"), None),
    )
    return jax.shard_map(shards, mesh=mesh, in_specs=in_specs, out_specs=out_specs, check_vma=False)
```

profile of v0, /device:TPU:0, one launch (start us, length us, event | category | flops | bytes accessed | tf_op | source)
XLA Modules:
  0.0 4913.2 jit_solution(17853203591915547859)
XLA Ops:
  12.9 43.8 all-reduce
  57.0 66.9 %all_gather.41 = bf16[4,4096]{1,0:T(4,128)(2,1)S(1)} all-gather(bf16[4,128]{1,0:T(4,128)(2,1)S(1)} %convert_element_type.101), channel_id=1, replica_groups=mesh['ctx'=16,'fsdp'=2] {'ctx','fsdp'}, dimensions={1}, use_global_device_ids=true | all-gather | bytes 33792 | tf_op jit(solution)/shard_map/all_gather | solution.py:75
  124.0 66.4 %all_gather.47 = bf16[16,4096]{1,0:T(8,128)(2,1)S(1)} all-gather(bf16[16,128]{1,0:T(8,128)(2,1)S(1)} %convert_element_type.114), channel_id=1, replica_groups=mesh['ctx'=16,'fsdp'=2] {'ctx','fsdp'}, dimensions={1}, use_global_device_ids=true | all-gather | bytes 135168 | tf_op jit(solution)/shard_map/all_gather | solution.py:80
  190.5 22.9 all-gather.8.cloned.1.call-done
  213.4 15.4 convolution_convert_fusion
  231.1 64.9 %all-gather = bf16[32,1,128]{2,1,0:T(2,128)(2,1)S(1)} all-gather(bf16[1,1,128]{2,1,0:T(2,128)(2,1)S(1)} %convert_bitcast_fusion.2), channel_id=1, replica_groups=mesh['ctx'=16,'fsdp'=2] {'ctx','fsdp'}, dimensions={0}, use_global_device_ids=true | all-gather | bytes 8448 | tf_op jit(solution)/shard_map/all_gather | solution.py:76
  296.0 64.5 %all-gather.2 = bf16[32,1,128]{2,1,0:T(2,128)(2,1)S(1)} all-gather(bf16[1,1,128]{2,1,0:T(2,128)(2,1)S(1)} %convert_bitcast_fusion), channel_id=1, replica_groups=mesh['ctx'=16,'fsdp'=2] {'ctx','fsdp'}, dimensions={0}, use_global_device_ids=true | all-gather | bytes 8448 | tf_op jit(solution)/shard_map/all_gather | solution.py:81
  361.1 64.2 %all-gather.1 = bf16[32,1,128]{2,1,0:T(2,128)(2,1)S(1)} all-gather(bf16[1,1,128]{2,1,0:T(2,128)(2,1)S(1)} %convert_bitcast_fusion.1), channel_id=1, replica_groups=mesh['ctx'=16,'fsdp'=2] {'ctx','fsdp'}, dimensions={0}, use_global_device_ids=true | all-gather | bytes 8448 | tf_op jit(solution)/shard_map/all_gather | solution.py:79
  428.1 21.4 multiply_reduce_fusion.82
  455.6 7.1 compare_select_fusion
  470.8 584.8 %while.90 = (s32[]{:T(128)}, f32[16,4096]{1,0:T(8,128)S(1)}, f32[4096]{0:T(1024)}, f32[16,16,4096]{2,1,0:T(8,128)}, f32[16,4096]{1,0:T(8,128)}, /*index=5*/f32[1...) while((s32[]{:T(128)}, f32[16,4096]{1,0:T(8,128)S(1)}, ...), condition=%wide.region_18.19_spmd.clone, body=%wide.region_1.18_spmd.clone.sunk | while | flops 9441298 | bytes 11361878 | solution.py:136
  569.7 3.3 stack.554
  1056.6 106.4 %while.86 = (s32[]{:T(128)}, f32[16,4096]{1,0:T(8,128)S(1)}, f32[16,4096]{1,0:T(8,128)S(1)}, f32[16,4096]{1,0:T(8,128)S(1)}, s32[]{:T(128)}) while((s32[]{:T(128)}, f32[16,4096]{1,0:T(8,128)S(1)}, f32[16,4096]{1,0:T(8,128)S(1)}, f32[16,4096]{1,0:T(8,128)S(1)}, s32[]{:T(128)}) %tuple.494), condition=%wide.region_20.21_spmd, body=%wide.region_19.20_spmd.sunk | while | flops 131074 | bytes 2097253 | solution.py:146
  1062.6 6.5 collective-permute-start
  1070.3 6.6 collective-permute-start
  1078.0 6.6 collective-permute-start
  1085.8 6.6 collective-permute-start
  1093.5 6.6 collective-permute-start
  1101.2 6.6 collective-permute-start
  1109.0 6.6 collective-permute-start
  1116.7 6.6 collective-permute-start
  1124.4 6.6 collective-permute-start
  1132.2 6.6 collective-permute-start
  1139.9 6.6 collective-permute-start
  1147.6 6.6 collective-permute-start
  1155.4 6.6 collective-permute-start
  1165.5 59.4 %while.87 = (s32[]{:T(128)}, f32[16,16,4096]{2,1,0:T(8,128)}, f32[16,16,16]{2,1,0:T(8,128)}, f32[16,4096]{1,0:T(8,128)S(1)}, f32[16,16,4096]{2,1,0:T(8,128)}, /*index=5*/f32[16,4096]{1,0:T(8,128)S(1)}, s32[]{:T(128)}) while((s32[]{:T(128)}, f32[16,16,4096]{2,1,0:T(8,128)}, f32[16,16,16]{2,1,0:T(8,128)}, f32[16,4096]{1,0:T(8,128)S(1)}, ...), condition=%wide.region_23.24_spmd, body=%wide.region_21.23_spmd.sunk | while | flops 4128770 | bytes 2100321 | solution.py:153
  1227.4 53.8 %while.88 = (s32[]{:T(128)}, f32[16,16,4096]{2,1,0:T(8,128)}, f32[16,4096]{1,0:T(8,128)S(1)}, f32[16,16,4096]{2,1,0:T(8,128)}, f32[16,16,16]{2,1,0:T(8,128)}, /*index=5*/f32[16,16,4096]{2,1,0:T(8,128)}, s32[]{:T(128)}) while((s32[]{:T(128)}, f32[16,16,4096]{2,1,0:T(8,128)}, f32[16,4096]{1,0:T(8,128)S(1)}, f32[16,16,4096]{2,1,0:T(8,128)}, ...), condition=%wide.region_26.27_spmd, body=%wide.region_24.26_spmd.sunk | while | flops 4128770 | bytes 2624609 | solution.py:191
  1283.6 5.0 multiply_add_fusion.48
  1288.6 128.0 %while.89 = (s32[]{:T(128)}, f32[16,4096]{1,0:T(8,128)S(1)}, f32[16,4096]{1,0:T(8,128)S(1)}, f32[16,4096]{1,0:T(8,128)S(1)}, s32[]{:T(128)}) while((s32[]{:T(128)}, f32[16,4096]{1,0:T(8,128)S(1)}, f32[16,4096]{1,0:T(8,128)S(1)}, f32[16,4096]{1,0:T(8,128)S(1)}, s32[]{:T(128)}) %tuple.532), condition=%wide.region_29.30_spmd, body=%wide.region_28.29_spmd.sunk | while | flops 131074 | bytes 2097253 | solution.py:197
  1290.0 6.3 collective-permute-done.1
  1297.6 7.1 collective-permute-done.1
  1306.1 6.4 collective-permute-done.1
  1313.8 7.8 collective-permute-done.1
  1323.0 7.3 collective-permute-done.1
  1331.6 7.3 collective-permute-done.1
  1340.2 7.3 collective-permute-done.1
  1348.9 7.3 collective-permute-done.1
  1357.5 7.3 collective-permute-done.1
  1366.1 7.3 collective-permute-done.1
  1374.8 7.3 collective-permute-done.1
  1383.4 7.3 collective-permute-done.1
  1392.0 7.3 collective-permute-done.1
  1400.6 7.3 collective-permute-done.1
  1409.3 7.3 collective-permute-done.1
  1422.7 774.8 %while.91 = (s32[]{:T(128)}, f32[16,4096]{1,0:T(8,128)S(1)}, f32[16,4096]{1,0:T(8,128)}, f32[16,16,4096]{2,1,0:T(8,128)}, f32[16,16,4096]{2,1,0:T(8,128)}, /*ind...) while((s32[]{:T(128)}, f32[16,4096]{1,0:T(8,128)S(1)}, ...), condition=%wide.region_95.96_spmd.clone, body=%wide.region_30.95_spmd.clone.sunk | while | flops 32636432 | bytes 31237844 | solution.py:246
  2199.4 4.2 add.943
  2204.0 4.1 fusion.150
  2211.1 5.9 fusion.113
  2219.1 5.4 fusion.98
  2225.8 7.0 collective-permute-done.3
  2232.9 5.3 multiply_reduce_fusion.86
  2241.2 3.4 fusion.137
  2248.4 13.2 fusion.133
  2262.8 25.8 fusion.119
  2288.7 9.4 fusion.122
  2298.1 16.2 fusion.129
  2314.3 49.1 all-reduce.5
  2369.0 17.2 reduce-scatter.19.cloned.1.call-done
  2387.8 131.0 %reduce-scatter.15.cloned.1.call-done = f32[16,128]{1,0:T(8,128)} async-done(((f32[16,4096]{1,0:T(8,128)}), f32[16,128]{1,0:T(8,128)}) %reduce-scatter.15.cloned.1.call-update) | async-done | bytes 8208 | tf_op jit(solution)/shard_map/reduce_scatter | solution.py:312
  2518.8 136.2 %reduce-scatter.13.cloned.1.call-done = f32[128,128]{1,0:T(8,128)} async-done(((f32[128,4096]{1,0:T(8,128)}), f32[128,128]{1,0:T(8,128)}) %reduce-scatter.13.cloned.1.call-update) | async-done | bytes 65552 | tf_op jit(solution)/shard_map/reduce_scatter | solution.py:310
  2654.9 137.9 %reduce-scatter.11.cloned.1.call-done = f32[128,160]{0,1:T(8,128)} async-done(((f32[4096,160]{0,1:T(8,128)}), f32[128,160]{0,1:T(8,128)}) %reduce-scatter.11.cloned.1.call-update) | async-done | bytes 81936 | tf_op jit(solution)/shard_map/reduce_scatter | solution.py:309
  2792.8 704.8 %reduce-scatter.17.cloned.1.call-done = f32[128,2048]{1,0:T(8,128)} async-done(((f32[4096,2048]{1,0:T(8,128)}), f32[128,2048]{1,0:T(8,128)}) %reduce-scatter.17.cloned.1.call-update) | async-done | bytes 1048592 | tf_op jit(solution)/shard_map/reduce_scatter | solution.py:314
  3497.7 1408.3 %reduce-scatter.9.cloned.1.call-done = f32[64,8192]{1,0:T(8,128)} async-done(((f32[2048,8192]{1,0:T(8,128)}), f32[64,8192]{1,0:T(8,128)}) %reduce-scatter.9.cloned.1.call-update) | async-done | bytes 2097168 | tf_op jit(solution)/shard_map/reduce_scatter | solution.py:303
  (5073 shorter events, 1546.6 us)
Async XLA Ops:
  7.2 49.4 %copy-start.20 = (bf16[1,256,2048]{2,1,0:T(8,128)(2,1)S(1)}, bf16[1,256,2048]{2,1,0:T(8,128)(2,1)}, u32[]{:S(2)}) copy-start(bf16[1,256,2048]{2,1,0:T(8,128)(2,1)} %param.24) | copy-start | bytes 3145732
  7.2 49.7 %copy-start.143 = (f32[4,128]{1,0:T(4,128)S(1)}, f32[4,128]{1,0:T(4,128)}, u32[]{:S(2)}) copy-start(f32[4,128]{1,0:T(4,128)} %param.27) | copy-start | bytes 6148
  7.2 116.7 %copy-start.145 = (f32[128]{0:T(128)S(1)}, f32[128]{0:T(128)}, u32[]{:S(2)}) copy-start(f32[128]{0:T(128)} %param.28) | copy-start | bytes 1540
  7.3 116.7 %copy-start.146 = (f32[128]{0:T(128)S(1)}, f32[128]{0:T(128)}, u32[]{:S(2)}) copy-start(f32[128]{0:T(128)} %param.33) | copy-start | bytes 1540
  7.3 116.7 %copy-start.142 = (f32[16,128]{1,0:T(8,128)S(1)}, f32[16,128]{1,0:T(8,128)}, u32[]{:S(2)}) copy-start(f32[16,128]{1,0:T(8,128)} %param.32) | copy-start | bytes 24580
  7.3 206.1 %all-gather.8.cloned.1.call-start = ((), (), s32[]{:S(2)}) async-start(), calls=%async_computation.6 | async-start | bytes 34603008 | tf_op jit(solution)/shard_map/all_gather | solution.py:70
  10.1 417.9 %all-gather.14.cloned.1.call-start = ((), (), s32[]{:S(2)}) async-start(), calls=%async_computation.9 | async-start | bytes 17301504 | tf_op jit(solution)/shard_map/all_gather | solution.py:82
  11.1 438.4 %all-gather.10.cloned.1.call-start = ((), (), s32[]{:S(2)}) async-start(), calls=%async_computation.7 | async-start | bytes 1351680 | tf_op jit(solution)/shard_map/all_gather | solution.py:77
  11.8 443.8 %all-gather.12.cloned.1.call-start = ((), (), s32[]{:S(2)}) async-start(), calls=%async_computation.8 | async-start | bytes 1081344 | tf_op jit(solution)/shard_map/all_gather | solution.py:78
  12.5 2373.7 %reduce-scatter.19.cloned.1.call-start = ((), (), s32[]{:S(2)}) async-start(), calls=%async_computation.15 | async-start | bytes 2162688
  56.6 172.2 %copy-start.118 = (f32[2048]{0:T(1024)}, f32[2048]{0:T(1024)S(1)}, u32[]{:S(2)}) copy-start(f32[2048]{0:T(1024)S(1)} %convert_element_type.104) | copy-start | bytes 24580
  57.0 171.9 %copy-start.126 = (f32[256]{0:T(256)}, f32[256]{0:T(256)S(1)}, u32[]{:S(2)}) copy-start(f32[256]{0:T(256)S(1)} %add_rsqrt_fusion) | copy-start | bytes 3076
  123.9 304.1 %copy-start.130 = (f32[1,4096]{1,0:T(1,128)}, f32[1,4096]{1,0:T(1,128)S(1)}, u32[]{:S(2)}) copy-start(f32[1,4096]{1,0:T(1,128)S(1)} %get-tuple-element.1100) | copy-start | bytes 49156
  123.9 304.1 %copy-start.132 = (f32[1,4096]{1,0:T(1,128)}, f32[1,4096]{1,0:T(1,128)S(1)}, u32[]{:S(2)}) copy-start(f32[1,4096]{1,0:T(1,128)S(1)} %get-tuple-element.1101) | copy-start | bytes 49156
  123.9 304.1 %copy-start.134 = (f32[1,4096]{1,0:T(1,128)}, f32[1,4096]{1,0:T(1,128)S(1)}, u32[]{:S(2)}) copy-start(f32[1,4096]{1,0:T(1,128)S(1)} %get-tuple-element.1102) | copy-start | bytes 49156
  124.0 304.1 %copy-start.136 = (f32[1,4096]{1,0:T(1,128)}, f32[1,4096]{1,0:T(1,128)S(1)}, u32[]{:S(2)}) copy-start(f32[1,4096]{1,0:T(1,128)S(1)} %get-tuple-element.1103) | copy-start | bytes 49156
  190.4 38.4 copy-start.105
  190.5 40.5 copy-start.147
  228.9 196.5 %collective-permute-start.2 = (bf16[3,4096]{1,0:T(4,128)(2,1)S(1)}, bf16[3,4096]{1,0:T(4,128)(2,1)S(1)}, u32[]{:S(2)}, u32[]{:S(2)}) collective-permute-start(bf16[3,4096]{1,0:T(4,128)(2,1)S(1)} %slice.1419), channel_id=1, source_target_pairs={{0,2},{2,4},{4,6},{6,8},{8,10},{10,12},{12,14},{14,16},{16,18},{18... | collective-permute-start | bytes 73736 | tf_op jit(solution)/shard_map/ppermute | solution.py:19
  231.1 194.4 %slice-start.2 = ((bf16[256,8192]{1,0:T(8,128)(2,1)}), bf16[256,4096]{1,0:T(8,128)(2,1)S(1)}, s32[]{:S(2)}) async-start(bf16[256,8192]{1,0:T(8,128)(2,1)} %copy-done.27), calls=%async_computation.18 | async-start | bytes 4194304 | tf_op jit(solution)/shard_map/slice | solution.py:85
  1056.7 2.4 collective-permute-start
  1059.2 3.4 collective-permute-start
  1062.6 7.6 collective-permute-start
  1070.3 7.7 collective-permute-start
  1078.0 7.7 collective-permute-start
  1085.8 7.7 collective-permute-start
  1093.5 7.7 collective-permute-start
  1101.2 7.7 collective-permute-start
  1109.0 7.7 collective-permute-start
  1116.7 7.7 collective-permute-start
  1124.4 7.7 collective-permute-start
  1132.2 7.7 collective-permute-start
  1139.9 7.7 collective-permute-start
  1147.6 7.7 collective-permute-start
  1155.4 7.7 collective-permute-start
  1288.7 7.6 collective-permute-start.1
  1296.3 8.4 collective-permute-start.1
  1304.8 7.7 collective-permute-start.1
  1312.5 9.1 collective-permute-start.1
  1321.7 8.6 collective-permute-start.1
  1330.3 8.6 collective-permute-start.1
  1338.9 8.6 collective-permute-start.1
  1347.5 8.6 collective-permute-start.1
  1356.2 8.6 collective-permute-start.1
  1364.8 8.6 collective-permute-start.1
  1373.4 8.6 collective-permute-start.1
  1382.1 8.6 collective-permute-start.1
  1390.7 8.6 collective-permute-start.1
  1399.3 8.6 collective-permute-start.1
  1408.0 8.6 collective-permute-start.1
  1440.2 14.9 copy-start.13
  1488.9 14.9 copy-start.13
  1537.4 14.9 copy-start.13
  1730.7 14.9 copy-start.13
  1778.6 14.9 copy-start.13
  1826.9 14.9 copy-start.13
  2224.5 8.3 collective-permute-start.3
  2240.3 278.4 %reduce-scatter.15.cloned.1.call-start = ((), (), s32[]{:S(2)}) async-start(), calls=%async_computation.13 | async-start | bytes 270336 | tf_op jit(solution)/shard_map/reduce_scatter | solution.py:312
  2241.2 413.7 %reduce-scatter.13.cloned.1.call-start = ((), (), s32[]{:S(2)}) async-start(), calls=%async_computation.12 | async-start | bytes 2162688 | tf_op jit(solution)/shard_map/reduce_scatter | solution.py:310
  2244.7 548.1 %reduce-scatter.11.cloned.1.call-start = ((), (), s32[]{:S(2)}) async-start(), calls=%async_computation.11 | async-start | bytes 2703360 | tf_op jit(solution)/shard_map/reduce_scatter | solution.py:309
  2246.8 1250.8 %reduce-scatter.17.cloned.1.call-start = ((), (), s32[]{:S(2)}) async-start(), calls=%async_computation.14 | async-start | bytes 34603008 | tf_op jit(solution)/shard_map/reduce_scatter | solution.py:314
  2261.6 2644.3 %reduce-scatter.9.cloned.1.call-start = ((), (), s32[]{:S(2)}) async-start(), calls=%async_computation.10 | async-start | bytes 69206016 | tf_op jit(solution)/shard_map/reduce_scatter | solution.py:303
  2298.1 16.2 copy-start.141
  2298.1 67.6 %copy-start.50 = (bf16[1,256,2048]{2,1,0:T(8,128)(2,1)S(1)}, bf16[1,256,2048]{2,1,0:T(8,128)(2,1)}, u32[]{:S(2)}) copy-start(bf16[1,256,2048]{2,1,0:T(8,128)(2,1)} %param.35) | copy-start | bytes 3145732
  (1689 other events, 15439.6 us)
Sparse Core Ops, SparseCore 0:
  11.7 201.6 all-gather.7
  217.0 113.4 all-gather.13
  333.9 47.8 all-gather.9
  385.1 47.8 all-gather.11
  2240.4 145.7 reduce-scatter.18
  2389.0 129.7 reduce-scatter.14
  2521.6 133.2 reduce-scatter.12
  2657.9 134.8 reduce-scatter.10
  2795.8 701.8 reduce-scatter.16
  3500.5 1405.3 reduce-scatter.8
where the time goes:
time: 4950 us; the launch traced here: 4910 us
  waiting for transfers between devices  2690 us (54%)
  other arithmetic  856 us (17%)
  local copies, waits for them, and re-layouts  669 us (14%)
  blocking collectives  420 us (8%)
  matrix products  124 us (3%)
  starting transfers between devices  112 us (2%)
    reduce_scatter x1, waiting for transfers between devices, shards(): lax.psum_scatter(contract_rows(normed_piece, d_mixed), ('ctx', 'fsdp'), s...  1410 us
    reduce_scatter x1, waiting for transfers between devices, shards(): lax.psum_scatter(out_grad, ('ctx', 'fsdp'), scatter_dimension=0, tiled=True)  705 us
    reduce_sum x64, other arithmetic, backward_block(): jnp.sum(through * rate_b, axis=0) + act_blk[position] * coef_sum  154 us
    mul x240, other arithmetic, forward_block(): delta_row * act_blk[position]  145 us
    reduce_scatter x1, waiting for transfers between devices, shards(): lax.psum_scatter(sproj_grad, ('ctx', 'fsdp'), scatter_dimension=0, tiled=...  138 us
    reduce_scatter x1, waiting for transfers between devices, shards(): lax.psum_scatter(dproj_grad, ('ctx', 'fsdp'), scatter_dimension=1, tiled=...  136 us
    reduce_sum x80, other arithmetic, forward_block(): outputs.append(jnp.sum(out_blk[position][:, None] * state, axis=0))  136 us
    ppermute x32, waiting for transfers between devices, passed_along(): return lax.ppermute(shard, axis, pairs)  132 us

commit v1 on v0

v1 whole, which is shorter than its diff:
```python
import functools

import jax
import jax.numpy as jnp
import numpy as np
from jax import lax
from jax.experimental import pallas as pl
from jax.experimental.pallas import tpu as pltpu
from jax.sharding import PartitionSpec as P

D = 2048
DI = 4096
STATE = 16
DT_RANK = 128
KW = 4
EPS = 1e-05
LOG2E = 1.4426950408889634
STEPS = 16
MESH = pl.DeviceIdType.MESH
BF16 = jnp.bfloat16
F32 = jnp.float32


class Grid:
    def __init__(self, ctx, fsdp):
        self.ctx, self.fsdp = ctx, fsdp
        self.planes = ctx // 4
        self.members = 4 * fsdp
        self.devices = ctx * fsdp

    def here(self):
        c, f = lax.axis_index("ctx"), lax.axis_index("fsdp")
        return c // 4, c % 4, f

    def at(self, z, q, f):
        return {"ctx": z * 4 + q, "fsdp": f}

    def member(self, z, j):
        return self.at(z, j // self.fsdp, j % self.fsdp)


def remote(src, dst, send, recv, where):
    return pltpu.make_async_remote_copy(
        src_ref=src, dst_ref=dst, send_sem=send, recv_sem=recv, device_id=where, device_id_type=MESH
    )


def greet(places):
    barrier = pltpu.get_barrier_semaphore()
    for place in places:
        pl.semaphore_signal(barrier, inc=1, device_id=place, device_id_type=MESH)
    pl.semaphore_wait(barrier, len(places))


def comm_call(kernel, outs, scratch, ident, name, args, vmem=None, in_vmem=()):
    spaces = [pl.BlockSpec(memory_space=pltpu.VMEM if i in in_vmem else pl.ANY) for i in range(len(args))]
    return pl.pallas_call(
        kernel,
        in_specs=spaces,
        out_specs=[pl.BlockSpec(memory_space=pl.ANY)] * len(outs),
        out_shape=outs,
        scratch_shapes=scratch,
        compiler_params=pltpu.CompilerParams(
            collective_id=ident, has_side_effects=True, vmem_limit_bytes=vmem or 16 * 2**20
        ),
        name=name,
    )(*args)


def gather_kernel(grid, n_ref, c_ref, wi_ref, wo_ref, sm_ref, n_all, c_all, wi_all, wo_all, sm_all,
                  local, n_send, n_recv, c_send, c_recv, a_send, a_recv, z_send, z_recv):
    z, q, f = grid.here()
    F, C, Z = grid.fsdp, grid.members, grid.planes
    me = q * F + f
    opposite, twin = q ^ 2, q ^ 1
    plane = [grid.member(z, lax.rem(me + d, C)) for d in range(1, C)]
    barrier = pltpu.get_barrier_semaphore()
    for place in plane:
        pl.semaphore_signal(barrier, inc=1, device_id=place, device_id_type=MESH)

    @pl.when(z > 0)
    def _():
        pl.semaphore_signal(barrier, inc=1, device_id=grid.at(z - 1, q, f), device_id_type=MESH)

    @pl.when(z < Z - 1)
    def _():
        pl.semaphore_signal(barrier, inc=1, device_id=grid.at(z + 1, q, f), device_id_type=MESH)

    inner = jnp.where((z > 0) & (z < Z - 1), 2, 1)
    pl.semaphore_wait(barrier, C - 1 + inner)

    mine = [
        pltpu.make_async_copy(n_ref, n_all.at[me], local.at[0]),
        pltpu.make_async_copy(c_ref, c_all.at[me], local.at[1]),
        pltpu.make_async_copy(wi_ref.at[me], wi_all.at[z * C + me], local.at[2]),
        pltpu.make_async_copy(wo_ref, wo_all.at[z], local.at[3]),
        pltpu.make_async_copy(sm_ref, sm_all.at[z], local.at[4]),
    ]
    for copy in mine:
        copy.start()
    sends = []

    def push(copy):
        copy.start()
        sends.append(copy)

    for d in range(1, C):
        j = lax.rem(me + d, C)
        push(remote(wi_ref.at[j], wi_all.at[z * C + me], a_send.at[d], a_recv.at[d], grid.member(z, j)))

    n_sent, c_sent = [0], [0]

    def push_n(block, src, where):
        push(remote(src, n_all.at[block], n_send.at[n_sent[0]], n_recv.at[block], where))
        n_sent[0] += 1

    def push_c(block, src, where):
        push(remote(src, c_all.at[block], c_send.at[c_sent[0]], c_recv.at[block], where))
        c_sent[0] += 1

    def arrived(ref, sems, block):
        remote(ref.at[block], ref.at[block], n_send.at[0], sems.at[block], grid.at(z, twin, f)).wait_recv()

    others = [lax.rem(f + d, F) for d in range(1, F)]
    for g in others:
        push_n(me, n_ref, grid.at(z, q, g))
    push_c(me, c_ref, grid.at(z, opposite, f))
    push_n(me, n_ref, grid.at(z, opposite, f))
    for g in others:
        push_c(me, c_ref, grid.at(z, q, g))
    push_n(me, n_ref, grid.at(z, twin, f))
    push_c(me, c_ref, grid.at(z, twin, f))

    def line_send(src_of, dst, k, step):
        block_right, block_left = z - step, z + step
        right = remote(src_of(block_right), dst(block_right), z_send.at[k, 0, step], z_recv.at[k, 0, step], grid.at(z + 1, q, f))
        left = remote(src_of(block_left), dst(block_left), z_send.at[k, 1, step], z_recv.at[k, 1, step], grid.at(z - 1, q, f))
        return right, left, (z < Z - 1) & (block_right >= 0), (z > 0) & (block_left <= Z - 1)

    def line_start(src_of, dst, k, step):
        right, left, to_right, to_left = line_send(src_of, dst, k, step)

        @pl.when(to_right)
        def _():
            right.start()

        @pl.when(to_left)
        def _():
            left.start()

    def line_done(src_of, dst, k, step):
        right, left, to_right, to_left = line_send(src_of, dst, k, step)

        @pl.when(to_right)
        def _():
            right.wait_send()

        @pl.when(to_left)
        def _():
            left.wait_send()

    def line_arrived(dst, k, step):
        from_left, from_right = z - 1 - step, z + 1 + step

        @pl.when(from_left >= 0)
        def _():
            remote(dst(from_left), dst(from_left), z_send.at[k, 0, step], z_recv.at[k, 0, step], grid.at(z - 1, q, f)).wait_recv()

        @pl.when(from_right <= Z - 1)
        def _():
            remote(dst(from_right), dst(from_right), z_send.at[k, 1, step], z_recv.at[k, 1, step], grid.at(z + 1, q, f)).wait_recv()

    lines = [
        (lambda b: wi_all.at[pl.ds(b * C, C)], lambda b: wi_all.at[pl.ds(b * C, C)]),
        (lambda b: wo_all.at[b], lambda b: wo_all.at[b]),
        (lambda b: sm_all.at[b], lambda b: sm_all.at[b]),
    ]
    line_start(lambda b: sm_ref, lines[2][1], 2, 0)
    mine[2].wait()
    for d in range(1, C):
        back = lax.rem(me + C - d, C)
        remote(wi_ref.at[me], wi_all.at[z * C + back], a_send.at[d], a_recv.at[d], grid.member(z, back)).wait_recv()
    line_start(*lines[0], 0, 0)
    line_start(lambda b: wo_ref, lines[1][1], 1, 0)
    for g in others:
        block = q * F + g
        arrived(n_all, n_recv, block)
        push_n(block, n_all.at[block], grid.at(z, opposite, f))
        push_n(block, n_all.at[block], grid.at(z, twin, f))
    arrived(c_all, c_recv, opposite * F + f)
    for g in others:
        push_c(opposite * F + f, c_all.at[opposite * F + f], grid.at(z, q, g))
    push_c(opposite * F + f, c_all.at[opposite * F + f], grid.at(z, twin, f))
    for g in others:
        arrived(c_all, c_recv, q * F + g)
        push_c(q * F + g, c_all.at[q * F + g], grid.at(z, twin, f))
    for g in [f] + others:
        block = opposite * F + g
        arrived(n_all, n_recv, block)
        push_n(block, n_all.at[block], grid.at(z, twin, f))
    for g in others:
        block = opposite * F + g
        arrived(c_all, c_recv, block)
        push_c(block, c_all.at[block], grid.at(z, twin, f))
    for step in range(Z - 1):
        for k in (2, 0, 1):
            line_arrived(lines[k][1], k, step)
            if step < Z - 2:
                line_start(*lines[k], k, step + 1)
    for side in (twin, twin ^ 2):
        for g in [f] + others:
            arrived(n_all, n_recv, side * F + g)
            arrived(c_all, c_recv, side * F + g)
    for i in (0, 1, 3, 4):
        mine[i].wait()
    for copy in sends:
        copy.wait_send()
    line_done(lambda b: sm_ref, lines[2][1], 2, 0)
    line_done(lambda b: wo_ref, lines[1][1], 1, 0)
    line_done(*lines[0], 0, 0)
    for step in range(1, Z - 1):
        for k in range(3):
            line_done(*lines[k], k, step)


def gather_all(grid, normed, cot, wi, wo, small):
    F, C, Z = grid.fsdp, grid.members, grid.planes
    tokens = normed.shape[0]
    dma = pltpu.SemaphoreType.DMA
    outs = [
        jax.ShapeDtypeStruct((C, tokens, D), BF16),
        jax.ShapeDtypeStruct((C, tokens, D), BF16),
        jax.ShapeDtypeStruct((Z * C,) + wi.shape[1:], BF16),
        jax.ShapeDtypeStruct((Z,) + wo.shape, BF16),
        jax.ShapeDtypeStruct((Z,) + small.shape, BF16),
    ]
    count = (F - 1) + F + 2 * F
    scratch = [dma((5,)), dma((count,)), dma((C,)), dma((count,)), dma((C,)), dma((C,)), dma((C,)), dma((3, 2, Z)), dma((3, 2, Z))]
    return comm_call(functools.partial(gather_kernel, grid), outs, scratch, 1, "gather_weights_and_tokens", (normed, cot, wi, wo, small))


def plane_sum_kernel(grid, part_ref, out_ref, send_buf, recv_buf, result, send, recv, out_send, out_recv, own):
    z, q, f = grid.here()
    C = grid.members
    me = q * grid.fsdp + f
    rows = recv_buf.shape[1]
    greet([grid.member(z, lax.rem(me + d, C)) for d in range(1, C)])
    lane = lax.broadcasted_iota(jnp.int32, (rows, 128), 1)

    def packed(v):
        high = v.astype(BF16).astype(F32)
        return high + pltpu.roll(v - high, 32, 1)

    @pl.loop(0, C)
    def _(k):
        at = pl.ds(pl.multiple_of(k * rows, 16), rows)
        send_buf[k, :, 0:128] = part_ref[at, 0:128].astype(BF16)
        send_buf[k, :, 128:256] = packed(part_ref[at, 128:256]).astype(BF16)

    copies = []
    for d in range(1, C):
        j = lax.rem(me + d, C)
        copy = remote(send_buf.at[j], recv_buf.at[d], send.at[d], recv.at[d], grid.member(z, j))
        copy.start()
        copies.append(copy)
    low = send_buf[me, :, 0:128].astype(F32)
    high = send_buf[me, :, 128:256].astype(F32)
    for d in range(1, C):
        copies[d - 1].wait_recv()
        low = low + recv_buf[d, :, 0:128].astype(F32)
        high = high + recv_buf[d, :, 128:256].astype(F32)
    total = jnp.where(lane < 32, high + pltpu.roll(high, 96, 1), 0.0)
    result[:, 0:128] = low.astype(BF16)
    result[:, 128:256] = packed(total).astype(BF16)
    for copy in copies:
        copy.wait_send()
    mine = pltpu.make_async_copy(result, out_ref.at[me], own)
    mine.start()
    copies = []
    for d in range(1, C):
        j = lax.rem(me + d, C)
        copy = remote(result, out_ref.at[me], out_send.at[d], out_recv.at[d], grid.member(z, j))
        copy.start()
        copies.append(copy)
    mine.wait()
    for d in range(1, C):
        back = lax.rem(me + C - d, C)
        remote(result, out_ref.at[back], out_send.at[d], out_recv.at[d], grid.member(z, back)).wait_recv()
    for copy in copies:
        copy.wait_send()


def plane_sum(grid, part, ident):
    C = grid.members
    rows = part.shape[0] // C
    dma = pltpu.SemaphoreType.DMA
    out = comm_call(
        functools.partial(plane_sum_kernel, grid),
        [jax.ShapeDtypeStruct((C, rows, 256), BF16)],
        [pltpu.VMEM((C, rows, 256), BF16), pltpu.VMEM((C, rows, 256), BF16), pltpu.VMEM((rows, 256), BF16)]
        + [dma((C,))] * 4 + [dma],
        ident, "plane_sum", (part,), vmem=40 * 2**20, in_vmem=(0,),
    )[0]
    return out.reshape(C * rows, 256)


def line_gather_kernel(grid, count, *refs):
    z, q, f = grid.here()
    Z = grid.planes
    ins, outs = refs[:count], refs[count:2 * count]
    local, send, recv = refs[2 * count:]
    greet([grid.at(lax.rem(z + d, Z), q, f) for d in range(1, Z)])
    copies = []
    for i in range(count):
        mine = pltpu.make_async_copy(ins[i], outs[i].at[z], local.at[i])
        mine.start()
        copies.append(mine)
    pushes = []
    for i in range(count):
        for d in range(1, Z):
            copy = remote(ins[i], outs[i].at[z], send.at[i, d], recv.at[i, d], grid.at(lax.rem(z + d, Z), q, f))
            copy.start()
            pushes.append(copy)
    for mine in copies:
        mine.wait()
    for i in range(count):
        for d in range(1, Z):
            back = lax.rem(z + Z - d, Z)
            remote(ins[i], outs[i].at[back], send.at[i, d], recv.at[i, d], grid.at(back, q, f)).wait_recv()
    for copy in pushes:
        copy.wait_send()


def line_gather(grid, arrays, ident, name):
    dma = pltpu.SemaphoreType.DMA
    n, Z = len(arrays), grid.planes
    return comm_call(
        functools.partial(line_gather_kernel, grid, n),
        [jax.ShapeDtypeStruct((Z,) + a.shape, a.dtype) for a in arrays],
        [dma((n,)), dma((n, Z)), dma((n, Z))], ident, name, tuple(arrays),
    )


def twin_swap_kernel(grid, count, *refs):
    z, q, f = grid.here()
    ins, outs = refs[:count], refs[count:2 * count]
    send, recv = refs[2 * count:]
    twin = grid.at(z, q ^ 1, f)
    greet([twin])
    copies = [remote(ins[i], outs[i], send.at[i], recv.at[i], twin) for i in range(count)]
    for copy in copies:
        copy.start()
    for copy in copies:
        copy.wait()


def twin_swap(grid, arrays, ident):
    dma = pltpu.SemaphoreType.DMA
    n = len(arrays)
    return comm_call(
        functools.partial(twin_swap_kernel, grid, n),
        [jax.ShapeDtypeStruct(a.shape, a.dtype) for a in arrays],
        [dma((n,)), dma((n,))], ident, "twin_swap", tuple(arrays),
    )


def owners_kernel(grid, planes_in, lines_in, *refs):
    z, q, f = grid.here()
    C, Z, N = grid.members, grid.planes, grid.devices
    me = q * grid.fsdp + f
    lin = z * C + me
    total = 1 + planes_in + lines_in
    ins, outs = refs[:total], refs[total:2 * total]
    local, w_send, w_recv, p_send, p_recv, l_send, l_recv = refs[2 * total:]
    barrier = pltpu.get_barrier_semaphore()

    def place(d):
        other = lax.rem(lin + d, N)
        return other, grid.member(other // C, lax.rem(other, C))

    @pl.loop(1, N)
    def _(d):
        pl.semaphore_signal(barrier, inc=1, device_id=place(d)[1], device_id_type=MESH)

    pl.semaphore_wait(barrier, N - 1)

    def weight(d):
        other, where = place(d)
        return remote(ins[0].at[other], outs[0].at[lin], w_send.at[d], w_recv.at[d], where)

    @pl.loop(1, N)
    def _(d):
        weight(d).start()

    mine = [pltpu.make_async_copy(ins[0].at[lin], outs[0].at[lin], local.at[0])]
    pushes, waits = [], []
    for i in range(planes_in):
        mine.append(pltpu.make_async_copy(ins[1 + i].at[me], outs[1 + i].at[me], local.at[1 + i]))
        for d in range(1, C):
            j, back = lax.rem(me + d, C), lax.rem(me + C - d, C)
            pushes.append(remote(ins[1 + i].at[j], outs[1 + i].at[me], p_send.at[i, d], p_recv.at[i, d], grid.member(z, j)))
            waits.append(remote(ins[1 + i].at[me], outs[1 + i].at[back], p_send.at[i, d], p_recv.at[i, d], grid.member(z, back)))
    for i in range(lines_in):
        k = 1 + planes_in + i
        mine.append(pltpu.make_async_copy(ins[k].at[z], outs[k].at[z], local.at[k]))
        for d in range(1, Z):
            j, back = lax.rem(z + d, Z), lax.rem(z + Z - d, Z)
            pushes.append(remote(ins[k].at[j], outs[k].at[z], l_send.at[i, d], l_recv.at[i, d], grid.at(j, q, f)))
            waits.append(remote(ins[k].at[z], outs[k].at[back], l_send.at[i, d], l_recv.at[i, d], grid.at(back, q, f)))
    for copy in pushes + mine:
        copy.start()
    for copy in mine:
        copy.wait()
    for copy in waits:
        copy.wait_recv()
    for copy in pushes:
        copy.wait_send()

    @pl.loop(1, N)
    def _(d):
        back = lax.rem(lin + N - d, N)
        remote(ins[0].at[lin], outs[0].at[back], w_send.at[d], w_recv.at[d], grid.member(back // C, lax.rem(back, C))).wait_recv()
        weight(d).wait_send()


def to_owners(grid, weight, plane_arrays, line_arrays, ident):
    dma = pltpu.SemaphoreType.DMA
    C, Z, N = grid.members, grid.planes, grid.devices
    p, l = len(plane_arrays), len(line_arrays)
    args = (weight,) + tuple(plane_arrays) + tuple(line_arrays)
    return comm_call(
        functools.partial(owners_kernel, grid, p, l),
        [jax.ShapeDtypeStruct(a.shape, a.dtype) for a in args],
        [dma((1 + p + l,)), dma((N,)), dma((N,)), dma((p, C)), dma((p, C)), dma((l, Z)), dma((l, Z))],
        ident, "to_owners", args,
    )

def spread(coef_ref, fan_ref, splat, tc):
    c = coef_ref[...].reshape(8 * tc, 128)
    for k in range(0, 2 * STATE, 4):
        l = pl.ds(k * 128, 512)
        splat[:, l] = jnp.dot(c, fan_ref[:, l], preferred_element_type=F32)

def rows8(t):
    return pl.ds(pl.multiple_of(t * 8, 8), 8)

def ends_kernel(cd, tc, delta_ref, w_ref, ds_ref, coef_ref, rate_ref, fan_ref, hs_ref, cum_ref, e_ref, g_ref, tot_ref, p_scr, splat):
    ch = pl.program_id(1)
    tiles = cd // 128
    @pl.when(ch == 0)
    def _():
        e_ref[...] = jnp.zeros_like(e_ref)
        g_ref[...] = jnp.zeros_like(g_ref)
        tot_ref[...] = jnp.zeros_like(tot_ref)
        p_scr[...] = jnp.ones_like(p_scr)
    hs_ref[...] = e_ref[...].reshape(hs_ref.shape)
    cum_ref[...] = tot_ref[...].reshape(cum_ref.shape)
    spread(coef_ref, fan_ref, splat, tc)
    group = 4
    for tile in range(tiles):
        lanes = pl.ds(tile * 128, 128)
        for n0 in range(0, STATE, group):
            rates = [rate_ref[(n0 + i) * 8:(n0 + i + 1) * 8, lanes] for i in range(group)]
            def body(t, carry):
                hs, ps, gs = carry
                tok = pl.ds(pl.multiple_of(t * 8, 8), 8)
                d, w, s = delta_ref[t, :, lanes], w_ref[t, :, lanes], ds_ref[t, :, lanes]
                nh, np_, ng = [], [], []
                for i in range(group):
                    a = jnp.exp2(d * rates[i])
                    cin = splat[rows8(t), pl.ds((n0 + i) * 128, 128)]
                    cout = splat[rows8(t), pl.ds((STATE + n0 + i) * 128, 128)]
                    nh.append(a * hs[i] + cin * w)
                    p = ps[i] * a
                    np_.append(p)
                    ng.append(gs[i] + p * (cout * s))
                return tuple(nh), tuple(np_), tuple(ng)
            rows = [pl.ds((n0 + i) * 8, 8) for i in range(group)]
            init = (tuple(e_ref[0, r, lanes] for r in rows), tuple(p_scr[r, lanes] for r in rows), tuple(g_ref[0, r, lanes] for r in rows))
            hs, ps, gs = lax.fori_loop(0, tc, body, init, unroll=tc)
            for i, r in enumerate(rows):
                e_ref[0, r, lanes] = hs[i]
                p_scr[r, lanes] = ps[i]
                g_ref[0, r, lanes] = gs[i]
        def total(t, acc):
            return acc + delta_ref[t, :, lanes]
        tot_ref[0, :, lanes] = lax.fori_loop(0, tc, total, tot_ref[0, :, lanes], unroll=tc)

def scan_ends(delta, w, ds, coef, rate, fan, tc=STEPS, vmem=48 * 2**20):
    tokens, members, cd = delta.shape
    sg, nch = members // 8, tokens // tc
    rows = STATE * 8
    tok = lambda width: pl.BlockSpec((tc, 8, width), lambda s, c: (c, s, 0))
    keep = lambda r: pl.BlockSpec((1, r, cd), lambda s, c: (s, 0, 0))
    return pl.pallas_call(
        functools.partial(ends_kernel, cd, tc),
        grid=(sg, nch),
        in_specs=[tok(cd), tok(cd), tok(cd), pl.BlockSpec((tc, 8, 128), lambda s, c: (c, s, 0)), pl.BlockSpec((rows, cd), lambda s, c: (0, 0)), pl.BlockSpec(fan.shape, lambda s, c: (0, 0))],
        out_specs=[pl.BlockSpec((1, 1, rows, cd), lambda s, c: (s, c, 0, 0)), pl.BlockSpec((1, 1, 8, cd), lambda s, c: (s, c, 0, 0)), keep(rows), keep(rows), keep(8)],
        out_shape=[jax.ShapeDtypeStruct((sg, nch, rows, cd), F32), jax.ShapeDtypeStruct((sg, nch, 8, cd), F32),
                   jax.ShapeDtypeStruct((sg, rows, cd), F32), jax.ShapeDtypeStruct((sg, rows, cd), F32), jax.ShapeDtypeStruct((sg, 8, cd), F32)],
        scratch_shapes=[pltpu.VMEM((rows, cd), F32), pltpu.VMEM((tc * 8, 2 * STATE * 128), F32)],
        compiler_params=pltpu.CompilerParams(vmem_limit_bytes=vmem),
        name="segment_ends",
    )(delta, w, ds, coef, rate, fan)

def sweep_kernel(cd, tc, delta_ref, w_ref, ds_ref, coef_ref, rate_ref, fan_ref, fold_ref, hs_ref, cum_ref, sin_ref, gin_ref,
                 y_ref, a_ref, s_ref, dc_ref, rs_ref, hist, h_scr, g_scr, splat, acc_in, acc_out):
    ch = pl.program_id(1)
    tiles = cd // 128
    @pl.when(ch == 0)
    def _():
        rs_ref[...] = jnp.zeros_like(rs_ref)
        g_scr[...] = gin_ref[0]
    spread(coef_ref, fan_ref, splat, tc)
    at = [pl.ds(tile * 128, 128) for tile in range(tiles)]
    nt = [(n, i) for n in range(STATE) for i in range(tiles)]

    for n0 in range(0, STATE, 4):
        pairs = [(n, i) for n in range(n0, n0 + 4) for i in range(tiles)]
        init = tuple(hs_ref[0, 0, pl.ds(n * 8, 8), at[i]] + jnp.exp2(cum_ref[0, 0, :, at[i]] * rate_ref[pl.ds(n * 8, 8), at[i]]) * sin_ref[0, pl.ds(n * 8, 8), at[i]] for n, i in pairs)
        def forward(t, hs, n0=n0, pairs=pairs):
            d = [delta_ref[t, :, l] for l in at]
            w = [w_ref[t, :, l] for l in at]
            s = [ds_ref[t, :, l] for l in at]
            y = [None] * tiles if n0 == 0 else [y_ref[t, :, l] for l in at]
            out = []
            for n in range(n0, n0 + 4):
                cin = splat[rows8(t), pl.ds(n * 128, 128)]
                cout = splat[rows8(t), pl.ds((STATE + n) * 128, 128)]
                acc = None
                for i in range(tiles):
                    r = pl.ds(n * 8, 8)
                    old = hs[len(out)]
                    hist[t, r, at[i]] = old
                    h = jnp.exp2(d[i] * rate_ref[r, at[i]]) * old + cin * w[i]
                    out.append(h)
                    y[i] = cout * h if n == 0 else y[i] + cout * h
                    acc = s[i] * h if i == 0 else acc + s[i] * h
                acc_out[rows8(t), pl.ds(n * 128, 128)] = acc
            for i in range(tiles):
                y_ref[t, :, at[i]] = y[i]
            return tuple(out)
        lax.fori_loop(0, tc, forward, init, unroll=tc)

    for n0 in range(0, STATE, 2):
        pairs = [(n, i) for n in range(n0, n0 + 2) for i in range(tiles)]
        init = (tuple(g_scr[pl.ds(n * 8, 8), at[i]] for n, i in pairs), tuple(rs_ref[0, pl.ds(n * 8, 8), at[i]] for n, i in pairs))
        def backward(k, carry, n0=n0, pairs=pairs):
            gs, rs = carry
            t = tc - 1 - k
            d = [delta_ref[t, :, l] for l in at]
            w = [w_ref[t, :, l] for l in at]
            s = [ds_ref[t, :, l] for l in at]
            da = [None] * tiles if n0 == 0 else [a_ref[t, :, l] for l in at]
            cs = [None] * tiles if n0 == 0 else [s_ref[t, :, l] for l in at]
            ng, nr = [], []
            for n in range(n0, n0 + 2):
                cin = splat[rows8(t), pl.ds(n * 128, 128)]
                cout = splat[rows8(t), pl.ds((STATE + n) * 128, 128)]
                acc = None
                for i in range(tiles):
                    r = pl.ds(n * 8, 8)
                    rate = rate_ref[r, at[i]]
                    j = len(ng)
                    a = jnp.exp2(d[i] * rate)
                    g = gs[j] + cout * s[i]
                    ga = g * a
                    ng.append(ga)
                    th = ga * hist[t, r, at[i]]
                    da[i] = th * rate if n == 0 else da[i] + th * rate
                    cs[i] = cin * g if n == 0 else cs[i] + cin * g
                    acc = g * w[i] if i == 0 else acc + g * w[i]
                    nr.append(rs[j] + th * d[i])
                acc_in[rows8(t), pl.ds(n * 128, 128)] = acc
            for i in range(tiles):
                a_ref[t, :, at[i]] = da[i]
                s_ref[t, :, at[i]] = cs[i]
            return tuple(ng), tuple(nr)
        gs, rs = lax.fori_loop(0, tc, backward, init, unroll=tc)
        for j, (n, i) in enumerate(pairs):
            g_scr[pl.ds(n * 8, 8), at[i]] = gs[j]
            rs_ref[0, pl.ds(n * 8, 8), at[i]] = rs[j]
    sums = jnp.dot(acc_in[...].astype(BF16), fold_ref[0], preferred_element_type=F32) + jnp.dot(acc_out[...].astype(BF16), fold_ref[1], preferred_element_type=F32)
    dc_ref[...] = sums.reshape(tc, 8, 128)

def scan_sweep(delta, w, ds, coef, rate, fan, fold, hs, cum, s_in, g_in, tc=STEPS, vmem=56 * 2**20):
    tokens, members, cd = delta.shape
    sg, nch = members // 8, tokens // tc
    rows = STATE * 8
    tok = lambda width: pl.BlockSpec((tc, 8, width), lambda s, c: (nch - 1 - c, s, 0))
    keep = lambda r: pl.BlockSpec((1, r, cd), lambda s, c: (s, 0, 0))
    cf = pl.BlockSpec((tc, 8, 128), lambda s, c: (nch - 1 - c, s, 0))
    f32 = F32
    return pl.pallas_call(
        functools.partial(sweep_kernel, cd, tc),
        grid=(sg, nch),
        in_specs=[tok(cd), tok(cd), tok(cd), cf, pl.BlockSpec((rows, cd), lambda s, c: (0, 0)), pl.BlockSpec(fan.shape, lambda s, c: (0, 0)), pl.BlockSpec(fold.shape, lambda s, c: (0, 0, 0)),
                  pl.BlockSpec((1, 1, rows, cd), lambda s, c: (s, nch - 1 - c, 0, 0)), pl.BlockSpec((1, 1, 8, cd), lambda s, c: (s, nch - 1 - c, 0, 0)), keep(rows), keep(rows)],
        out_specs=[tok(cd), tok(cd), tok(cd), cf, keep(rows)],
        out_shape=[jax.ShapeDtypeStruct(delta.shape, f32)] * 3 + [jax.ShapeDtypeStruct((tokens, members, 128), f32), jax.ShapeDtypeStruct((sg, rows, cd), f32)],
        scratch_shapes=[pltpu.VMEM((tc, rows, cd), f32), pltpu.VMEM((rows, cd), f32), pltpu.VMEM((rows, cd), f32), pltpu.VMEM((tc * 8, 2 * STATE * 128), f32), pltpu.VMEM((tc * 8, STATE * 128), f32), pltpu.VMEM((tc * 8, STATE * 128), f32)],
        compiler_params=pltpu.CompilerParams(vmem_limit_bytes=vmem),
        name="segment_sweep",
    )(delta, w, ds, coef, rate, fan, fold, hs, cum, s_in, g_in)


def rounded(value):
    return lax.reduce_precision(value, 8, 7)


def silu_slope(value):
    sigma = jax.nn.sigmoid(value)
    return sigma * (1.0 + value * (1.0 - sigma))


def contract_rows(left, right):
    return lax.dot_general(left, right, (((0,), (0,)), ((), ())), preferred_element_type=F32)


def contract_cols(left, right):
    return lax.dot_general(left, right, (((1,), (1,)), ((), ())), preferred_element_type=F32)


def dot(left, right):
    return jnp.dot(left, right, preferred_element_type=F32)


def spread_tables():
    fan = np.zeros((128, 2 * STATE * 128), np.float32)
    for k in range(2 * STATE):
        fan[k, k * 128:(k + 1) * 128] = 1
        fan[2 * STATE + k, k * 128:(k + 1) * 128] = 1
    fold = np.zeros((2, STATE * 128, 128), np.float32)
    for n in range(STATE):
        fold[0, n * 128:(n + 1) * 128, n] = 1
        fold[1, n * 128:(n + 1) * 128, STATE + n] = 1
    return jnp.asarray(fan, BF16), jnp.asarray(fold, BF16)


def shards(grid, hidden_in, norm_gain, in_proj, conv_weight, conv_bias, state_proj, delta_proj, delta_bias,
           decay_log, skip_gain, out_proj, cotangent):
    F, C, Z = grid.fsdp, grid.members, grid.planes
    tokens = hidden_in.shape[1]
    rows = in_proj.shape[0]
    block = out_proj.shape[0]
    chans = Z * block
    z, q, f = grid.here()

    hidden = hidden_in.reshape(tokens, D).astype(F32)
    cot_rows = cotangent.reshape(tokens, D)
    inv_rms = lax.rsqrt(jnp.mean(hidden * hidden, axis=1, keepdims=True) + EPS)
    unit = hidden * inv_rms
    gain_rows = rounded(norm_gain)
    gain_tile = jnp.broadcast_to(jnp.pad(gain_rows, (0, 128 - rows))[None, :], (8, 128))
    gains = everyone(grid, gain_tile)[:, 0, :rows].reshape(D)
    normed = (unit * gains[None, :]).astype(BF16)

    in_low = rounded(in_proj).astype(BF16)
    wi = in_low.reshape(rows, 2, Z, C, block).transpose(3, 0, 1, 2, 4).reshape(C, rows, 2 * chans)
    small = jnp.concatenate(
        [conv_weight, conv_bias[None], delta_bias[None], skip_gain[None], decay_log, jnp.zeros((9, block), F32), delta_proj, state_proj.T], axis=0
    ).astype(BF16)
    normed_all, cot_all, wi_all, wo_all, small_all = gather_all(grid, normed, cot_rows, wi, out_proj.astype(BF16), small)
    count = C * tokens
    normed_all = normed_all.reshape(count, D)
    cot_all = cot_all.reshape(count, D)
    w_in = wi_all.reshape(D, 2 * chans)
    w_out = wo_all.reshape(chans, D)
    small_all = small_all.transpose(1, 0, 2).reshape(small.shape[0], chans)
    taps = small_all[:KW].astype(F32)
    conv_shift = small_all[KW].astype(F32)
    delta_shift = small_all[KW + 1].astype(F32)
    skip = small_all[KW + 2].astype(F32)
    decay_rate = -jnp.exp(small_all[KW + 3:KW + 3 + STATE].astype(F32))
    w_delta = small_all[32:32 + DT_RANK]
    w_state = small_all[32 + DT_RANK:]
    rate8 = jnp.repeat(decay_rate * LOG2E, 8, axis=0)

    def by_step(value):
        return value.reshape(C, tokens, -1).transpose(1, 0, 2)

    def by_member(value):
        return value.transpose(1, 0, 2).reshape(count, -1)

    mixed = by_step(dot(normed_all, w_in).astype(BF16))
    conv_in = mixed[:, :, :chans]
    gate = mixed[:, :, chans:].astype(F32)
    edge_rows = -(-(KW - 1) * F // 16) * 16
    tail = conv_in[tokens - (KW - 1):, C - F:].reshape((KW - 1) * F, chans)
    tails = line_gather(grid, [jnp.pad(tail, ((0, edge_rows - (KW - 1) * F), (0, 0)))], 3, "conv_edges")[0]
    before = lax.dynamic_index_in_dim(tails, jnp.maximum(z - 1, 0), 0, False)[: (KW - 1) * F]
    before = jnp.where(z > 0, before, jnp.zeros_like(before)).reshape(KW - 1, F, chans)
    edge = jnp.concatenate([before, conv_in[tokens - (KW - 1):, : C - F]], axis=1)
    padded = jnp.concatenate([edge, conv_in], axis=0).astype(F32)
    conv_out = jnp.broadcast_to(conv_shift, (tokens, C, chans))
    for k in range(KW):
        conv_out = conv_out + taps[k] * padded[k:k + tokens]
    act = rounded(jax.nn.silu(conv_out))
    act_rows = lax.optimization_barrier(act.astype(BF16).reshape(count, chans))
    pad_lanes = 256 - DT_RANK - 2 * STATE
    selected = contract_cols(act_rows, jnp.pad(w_state, ((0, pad_lanes), (0, 0))))
    selected = plane_sum(grid, selected, 4)
    delta_in = selected[:, :DT_RANK]
    coef = selected[:, DT_RANK:].reshape(tokens, C, 128)
    delta_pre = (dot(delta_in, w_delta) + delta_shift).reshape(tokens, C, chans)
    delta = jax.nn.softplus(delta_pre)
    drive = delta * act
    gate_act = jax.nn.silu(gate)
    d_gated = lax.optimization_barrier(by_step(contract_cols(cot_all, w_out)))
    d_scanned = d_gated * gate_act

    fan, fold = spread_tables()
    starts, elapsed, ends, adjoints, totals = scan_ends(delta, drive, d_scanned, coef, rate8, fan)
    def by_segment(value):
        groups = C // 8
        value = value.reshape(groups, -1, 8, chans).transpose(0, 2, 1, 3)
        return value.reshape(4, F, -1, chans)

    def by_sublane(value):
        return value.reshape(C // 8, 8, STATE, chans).transpose(0, 2, 1, 3).reshape(C // 8, STATE * 8, chans)

    totals = by_segment(totals)
    kept, ends, adjoints = jnp.exp(decay_rate * totals), by_segment(ends), by_segment(adjoints)
    end = ends[0]
    for c in range(1, 4):
        end = kept[c] * end + ends[c]
    adj = adjoints[3]
    for c in reversed(range(3)):
        adj = kept[c] * adj + adjoints[c]
    flat = [end.reshape(F * STATE, chans), adj.reshape(F * STATE, chans), jnp.broadcast_to(jnp.sum(totals, axis=0), (F, 8, chans)).reshape(F * 8, chans)]
    all_end, all_adj, all_tot = line_gather(grid, flat, 5, "segment_states")
    plane_kept = jnp.exp(decay_rate * all_tot.reshape(Z, F, 8, chans)[:, :, :1])
    all_end, all_adj = all_end.reshape(Z, F, STATE, chans), all_adj.reshape(Z, F, STATE, chans)
    state = jnp.zeros((F, STATE, chans), F32)
    adj = state
    for p in range(Z - 1):
        state = jnp.where(p < z, plane_kept[p] * state + all_end[p], state)
    for p in reversed(range(1, Z)):
        adj = jnp.where(p > z, plane_kept[p] * adj + all_adj[p], adj)
    before_state, after_adj = [], []
    for c in range(4):
        before_state.append(state)
        state = kept[c] * state + ends[c]
    for c in reversed(range(4)):
        after_adj.append(adj)
        adj = kept[c] * adj + adjoints[c]
    after_adj.reverse()

    y, d_delta_a, coef_sum, d_coef, rate_sum = scan_sweep(
        delta, drive, d_scanned, coef, rate8, fan, fold, starts, elapsed, by_sublane(jnp.stack(before_state)), by_sublane(jnp.stack(after_adj))
    )
    decay_grad = rate_sum.reshape(C // 8, STATE, 8, chans).sum(axis=(0, 2)) * decay_rate
    scanned = y + skip * act
    gated = (scanned * gate_act).astype(BF16)
    d_gate = d_gated * scanned * silu_slope(gate)
    skip_grad = jnp.sum(d_scanned * act, axis=(0, 1))
    d_delta_pre = (d_delta_a * (1.0 / LOG2E) + act * coef_sum) * jax.nn.sigmoid(delta_pre)
    shift_grad = jnp.sum(d_delta_pre, axis=(0, 1))
    d_delta_low = d_delta_pre.astype(BF16).reshape(count, chans)
    dproj_grad = contract_rows(delta_in, d_delta_low)
    d_delta_in = contract_cols(d_delta_low, w_delta)
    d_selected = plane_sum(grid, jnp.concatenate([d_delta_in, d_coef.reshape(count, 128)], axis=1), 6)
    d_selected = d_selected[:, :DT_RANK + 2 * STATE]
    sproj_grad = contract_rows(d_selected, act_rows)
    d_activated = delta * coef_sum + skip * d_scanned + dot(d_selected, w_state).reshape(tokens, C, chans)
    d_conv = d_activated * silu_slope(conv_out)
    cbias_grad = jnp.sum(d_conv, axis=(0, 1))
    kernel_grad = jnp.stack([jnp.sum(d_conv * padded[k:k + tokens], axis=(0, 1)) for k in range(KW)])
    head = d_conv[:KW - 1, :F].reshape((KW - 1) * F, chans)
    head_rows = -(-(KW - 1) * F // 8) * 8
    heads = line_gather(grid, [jnp.pad(head, ((0, head_rows - (KW - 1) * F), (0, 0)))], 7, "conv_grad_edges")[0]
    after = lax.dynamic_index_in_dim(heads, jnp.minimum(z + 1, Z - 1), 0, False)[: (KW - 1) * F]
    after = jnp.where(z < Z - 1, after, jnp.zeros_like(after)).reshape(KW - 1, F, chans)
    edge_grad = jnp.concatenate([d_conv[:KW - 1, F:], after], axis=1)
    grad_padded = jnp.concatenate([d_conv, edge_grad], axis=0)
    d_conv_in = jnp.zeros((tokens, C, chans), F32)
    for k in range(KW):
        d_conv_in = d_conv_in + taps[k] * grad_padded[KW - 1 - k:KW - 1 - k + tokens]
    d_mixed = by_member(jnp.concatenate([d_conv_in, d_gate], axis=2).astype(BF16))
    gated = by_member(lax.optimization_barrier(gated))

    in_part = contract_rows(normed_all, d_mixed).astype(BF16).reshape(Z * C, rows, 2 * chans)
    out_part = contract_rows(gated, cot_all).astype(BF16).reshape(Z, block, D)
    half = D // 2
    core = q % 2
    w_out_mine = lax.dynamic_slice_in_dim(w_out, core * half, half, 1)
    w_out_twin = lax.dynamic_slice_in_dim(w_out, (1 - core) * half, half, 1)
    w_in_mine = lax.dynamic_slice_in_dim(w_in, core * half, half, 0)
    w_in_twin = lax.dynamic_slice_in_dim(w_in, (1 - core) * half, half, 0)
    twin_out = dot(gated, w_out_twin).astype(BF16)
    twin_in = contract_cols(d_mixed, w_in_twin).astype(BF16)
    from_out, from_in = twin_swap(grid, [twin_out, twin_in], 8)
    part_out = (dot(gated, w_out_mine) + from_out.astype(F32)).astype(BF16).reshape(C, tokens, half)
    part_in = (contract_cols(d_mixed, w_in_mine) + from_in.astype(F32)).astype(BF16).reshape(C, tokens, half)

    fine = jnp.concatenate([kernel_grad, cbias_grad[None], shift_grad[None], skip_grad[None], decay_grad, jnp.zeros((9, chans), F32)], axis=0)
    fine = fine.reshape(32, Z, block).transpose(1, 0, 2)
    coarse = jnp.concatenate([dproj_grad, sproj_grad], axis=0).astype(BF16)
    coarse = coarse.reshape(-1, Z, block).transpose(1, 0, 2)
    got = to_owners(grid, in_part, [part_out, part_in], [out_part, coarse, fine], 9)
    in_grad = got[0].astype(F32).reshape(Z, C, rows, 2, Z, block).sum(axis=0)
    in_grad = in_grad.transpose(1, 2, 3, 0, 4).reshape(rows, 2 * DI)

    def owned(value):
        value = value.astype(F32).reshape(2, 2, F, tokens, half).sum(axis=(0, 2))
        return jnp.concatenate([value[0], value[1]], axis=1)

    block_out = (hidden + owned(got[1])).astype(BF16)
    d_unit = owned(got[2]) * gains[None, :]
    out_grad = got[3].astype(F32).sum(axis=0)
    coarse = got[4].astype(F32).sum(axis=0)
    fine = got[5].sum(axis=0)
    gain_grad = jnp.sum(rounded(in_proj) * in_grad, axis=1) / gain_rows
    mean_term = jnp.mean(d_unit * unit, axis=1, keepdims=True)
    input_grad = (cot_rows.astype(F32) + inv_rms * (d_unit - unit * mean_term)).astype(BF16)
    return (
        block_out.reshape(1, tokens, D),
        input_grad.reshape(1, tokens, D),
        gain_grad,
        in_grad,
        fine[:KW],
        fine[KW],
        coarse[DT_RANK:].T,
        coarse[:DT_RANK],
        fine[KW + 1],
        fine[KW + 3:KW + 3 + STATE],
        fine[KW + 2],
        out_grad,
    )


def everyone_kernel(grid, in_ref, out_ref, local, send, recv):
    z, q, f = grid.here()
    C, N = grid.members, grid.devices
    lin = z * C + q * grid.fsdp + f
    barrier = pltpu.get_barrier_semaphore()

    def copy(d):
        other = lax.rem(lin + d, N)
        where = grid.member(other // C, lax.rem(other, C))
        return remote(in_ref, out_ref.at[lin], send.at[d], recv.at[d], where), where

    @pl.loop(1, N)
    def _(d):
        pl.semaphore_signal(barrier, inc=1, device_id=copy(d)[1], device_id_type=MESH)

    pl.semaphore_wait(barrier, N - 1)

    @pl.loop(1, N)
    def _(d):
        copy(d)[0].start()

    mine = pltpu.make_async_copy(in_ref, out_ref.at[lin], local)
    mine.start()
    mine.wait()

    @pl.loop(1, N)
    def _(d):
        back = lax.rem(lin + N - d, N)
        remote(in_ref, out_ref.at[back], send.at[d], recv.at[d], grid.member(back // C, lax.rem(back, C))).wait_recv()
        copy(d)[0].wait_send()


def everyone(grid, value):
    dma = pltpu.SemaphoreType.DMA
    N = grid.devices
    return comm_call(
        functools.partial(everyone_kernel, grid),
        [jax.ShapeDtypeStruct((N,) + value.shape, value.dtype)],
        [dma, dma((N,)), dma((N,))], 10, "gather_gain", (value,),
    )[0]


def solution(mesh):
    grid = Grid(mesh.shape["ctx"], mesh.shape["fsdp"])
    both = ("ctx", "fsdp")
    tokens, flat, by_row, by_col = P("fsdp", "ctx", None), P(both), P(both, None), P(None, both)
    in_specs = (tokens, flat, by_row, by_col, flat, by_row, by_col, flat, by_col, flat, by_row, tokens)
    out_specs = (tokens, tokens, flat, by_row, by_col, flat, by_row, by_col, flat, by_col, flat, by_row)
    return jax.shard_map(functools.partial(shards, grid), mesh=mesh, in_specs=in_specs, out_specs=out_specs, check_vma=False)
```

time: 4950 us -> 761 us (0.15)
  waiting for transfers between devices: 2690 us -> 0 us
  other arithmetic: 856 us -> 62.6 us
  local copies, waits for them, and re-layouts: 669 us -> 61 us
  Pallas kernels: 0 us -> 518 us
  blocking collectives: 420 us -> 0 us
  starting transfers between devices: 112 us -> 0 us
    reduce_scatter x5 -> x0, waiting for transfers between devices: 2520 us -> none  [the longest x1 1410 us: shards(): lax.psum_scatter(contract_rows(normed_piece, d_mixed), ('ctx', 'fsdp'), s...]
    pallas_call x0 -> x11, Pallas kernels: none -> 518 us  [the longest x9 431 us: comm_call(): pl.pallas_call(kernel, in_specs=spaces, out_specs=[pl.BlockSpec(memory_sp...]
    reduce_sum x275 -> x12, other arithmetic: 499 us -> 27.5 us  [the longest x1 7.35 us: shards(): in_grad = got[0].astype(F32).reshape(Z, C, rows, 2, Z, block).sum(axis=0)]
    all_gather x5 -> x0, blocking collectives: 327 us -> none  [the longest x1 66.9 us: shards(): lax.all_gather(kernel_low, ('ctx', 'fsdp'), axis=1, tiled=True)]
    mul x769 -> x2, other arithmetic: 244 us -> 0.03 us  [the longest x1 0.02 us: shards(): rate_sum.reshape(C // 8, STATE, 8, chans).sum(axis=(0, 2)) * decay_rate]
    slice x86 -> x23, local copies, waits for them, and re-layouts: 198 us -> 7.75 us  [the longest x1 1.88 us: shards(): conv_in = mixed[:, :, :chans]]
    another operation x108 -> x0, local copies, waits for them, and re-layouts: 186 us -> none  [the longest x16 53.4 us: forward_block(): jnp.stack(elapsed_rows)]
    mul x128 -> x2, local copies, waits for them, and re-layouts: 161 us -> 0.08 us  [the longest x1 0.07 us: shards(): normed = (unit * gains[None, :]).astype(BF16)]
where the time goes in v1:
time: 761 us; the launch traced here: 753 us
  Pallas kernels  518 us (68%)
  matrix products  109 us (14%)
  other arithmetic  62.6 us (8%)
  local copies, waits for them, and re-layouts  61 us (8%)
    pallas_call x9, Pallas kernels, comm_call(): pl.pallas_call(kernel, in_specs=spaces, out_specs=[pl.BlockSpec(memory_sp...  431 us
    pallas_call x1, Pallas kernels, scan_sweep(): pl.pallas_call(functools.partial(sweep_kernel, cd, tc), grid=(sg, nch), i...  62.2 us
    dot_general x4, matrix products, contract_rows(): lax.dot_general(left, right, (((0,), (0,)), ((), ())), preferred_element_...  39.4 us
    dot_general x5, matrix products, dot(): return jnp.dot(left, right, preferred_element_type=F32)  39 us
    dot_general x5, matrix products, contract_cols(): lax.dot_general(left, right, (((1,), (1,)), ((), ())), preferred_element_...  30.7 us
    pallas_call x1, Pallas kernels, scan_ends(): pl.pallas_call(functools.partial(ends_kernel, cd, tc), grid=(sg, nch), in...  25.4 us
    unnamed x118, local copies, waits for them, and re-layouts  22 us

profile of v1, /device:TPU:0, one launch (start us, length us, event | category | flops | bytes accessed | tf_op | source)
XLA Modules:
  0.0 753.3 jit_solution(552516048101767967)
XLA Ops:
  1.3 11.2 %gather_gain.1 = f32[32,8,128]{2,1,0:T(8,128)S(1)} custom-call(f32[8,128]{1,0:T(8,128)S(1)} %broadcast_in_dim.54.in_ref), custom_call_target="tpu_custom_call" | custom-call | tf_op jit(solution)/shard_map/gather_gain/pallas_call | solution.py:57
  12.6 1.5 fusion.34
  14.2 1.5 fusion.32.n_ref
  16.4 0.9 convert_bitcast_fusion.3
  20.5 1.8 fusion.47
  22.5 1.4 copy.146
  23.9 1.8 reshape.404.wi_ref
  25.7 1.3 convert_element_type.138.wo_ref
  27.0 157.3 %gather_weights_and_tokens.1 = (bf16[8,256,2048]{2,1,0:T(8,128)(2,1)S(1)}, bf16[8,256,2048]{2,1,0:T(8,128)(2,1)S(1)}, bf16[32,64,1024]{2,1,0:T(8,128)(2,1)S(1)},...) custom-call(bf16[256,2048]{1,0:T(8,128)(2,1)S(1)} %fusion.32.n_ref, bf16[256,2048]{1,0:T(8,128)(2,1)S(1)} %bitcast.275, ...), custom_call_target="tpu_custom_call" | custom-call | tf_op jit(solution)/shard_map/gather_weights_and_tokens/pallas_call | solution.py:57
  184.3 9.1 %convolution_convert_fusion.1 = bf16[2048,1024]{1,0:T(8,128)(2,1)S(1)} fusion(bf16[2048,2048]{1,0:T(8,128)(2,1)S(1)} %bitcast.290, bf16[2048,1024]{1,0:T(8,128)(2,1)S(1)} %bitcast.291), kind=kOutput, calls=%fused_computation.55 | convolution fusion | flops 8592031744 | bytes 16777216 | tf_op jit(solution)/shard_map/dot_general | solution.py:626
  193.5 2.3 copy.145
  195.8 2.1 copy-done.27
  197.9 5.7 conv_edges.1
  203.7 1.9 slice.320
  205.6 1.5 slice.319
  208.5 12.8 %fusion.29 = f32[256,8,512]{2,1,0:T(8,128)} fusion(bf16[512,2048,1]{1,0,2:T(8,128)(2,1)S(1)} %bitcast.294, bf16[8,256,2048]{2,1,0:T(8,128)(2,1)S(1)} %copy-done.16), kind=kOutput, calls=%fused_computation.64 | convolution fusion | flops 4294967296 | bytes 14680064 | tf_op jit(solution)/shard_map/dot_general | solution.py:622
  221.9 7.0 multiply_reduce_fusion
  228.9 1.2 convert_bitcast_fusion.1
  230.1 1.0 fusion.81
  232.3 29.8 %plane_sum.2 = bf16[8,256,256]{2,1,0:T(8,128)(2,1)S(1)} custom-call(f32[2048,256]{1,0:T(8,128)S(1)} %fusion.58.part_ref), custom_call_target="tpu_custom_call" | custom-call | tf_op jit(solution)/shard_map/plane_sum/pallas_call | solution.py:57
  262.4 18.2 %fusion.76 = (f32[256,8,512]{2,1,0:T(8,128)}, f32[256,8,512]{2,1,0:T(8,128)}, f32[2048,512]{1,0:T(8,128)}) fusion(f32[256,8,512]{2,1,0:T(8,128)} %copy-done.25, f32[512]{0:T(512)S(1)} %bitcast.353, bf16[128,512]{0,1:T(8,128)(2,1)S(1)} %bitcast.327, bf16[2048,256]{1,0:T(8,128)(2,1)S(1)} %bitcast.272), kind=kOutput, calls=%fused_computation.181 | convolution fusion | flops 282066944 | bytes 17434624 | tf_op jit(solution)/shard_map/dot_general | solution.py:626
  280.7 25.4 %segment_ends.1 = (f32[1,16,128,512]{3,2,1,0:T(8,128)}, f32[1,16,8,512]{3,2,1,0:T(8,128)S(1)}, f32[1,128,512]{2,1,0:T(8,128)S(1)}, f32[1,128,512]{2,1,0:T(8,128)S(1)}, f32[1,8,512]{2,1,0:T(8,128)S(1)}) custom-call(f32[256,8,512]{2,1,0:T(8,128)} %get-tuple-element.85.delta_ref, f32[256,8,512]{2,1,0:T(8,128)} %get-tuple-element.84.w_ref, ...), custom_call_target="tpu_custom_call" | custom-call | tf_op jit(solution)/shard_map/segment_ends/pallas_call | solution.py:495
  308.1 17.8 %segment_states.1 = (f32[4,32,512]{2,1,0:T(8,128)S(1)}, f32[4,32,512]{2,1,0:T(8,128)S(1)}, f32[4,16,512]{2,1,0:T(8,128)S(1)}) custom-call(f32[32,512]{1,0:T(8,128)S(1)} %get-tuple-element.123.refs_0_, f32[32,512]{1,0:T(8,128)S(1)} %get-tuple-element.122.refs_1_, f32[16,512]{1,0:T(8,128)S(1)} %broadcast_bitcast_fusion.1.refs_2_), custom_call_target="tpu_custom_call" | custom-call | tf_op jit(solution)/shard_map/segment_states/pallas_call | solution.py:57
  326.8 1.1 multiply_add_fusion.2
  328.7 1.0 multiply_add_fusion.5
  329.7 0.9 copy.148
  330.6 62.2 %segment_sweep.1 = (f32[256,8,512]{2,1,0:T(8,128)}, f32[256,8,512]{2,1,0:T(8,128)}, f32[256,8,512]{2,1,0:T(8,128)}, f32[256,8,128]{2,1,0:T(8,128)}, f32[1,128,512]{2,1,0:T(8,128)}) custom-call(f32[256,8,512]{2,1,0:T(8,128)} %get-tuple-element.85.delta_ref, f32[256,8,512]{2,1,0:T(8,128)} %get-tuple-element.84.w_ref, f32[256,8,512]{2,1,0:T(8,128)} %get-tuple-element.72.ds_ref, ...), custom_call_target="tpu_custom_call" | custom-call | tf_op jit(solution)/shard_map/segment_sweep/pallas_call | solution.py:595
  392.8 1.0 bitcast_reduce_fusion
  393.9 12.1 %multiply_convert_fusion = (bf16[256,8,512]{2,1,0:T(8,128)(2,1)}, bf16[256,8,512]{2,1,0:T(8,128)(2,1)}, f32[512]{0:T(512)}, bf16[256,8,512]{2,1,0:T(8,128)(2,1)S(1)}) fusion(f32[256,8,512]{2,1,0:T(8,128)} %get-tuple-element.54, f32[512]{0:T(512)S(1)} %bitcast.351, bf16[256,8,1024]{2,1,0:T(8,128)(2,1)} %bitcast.303, f32[256,8,512]{2,1,0:T(8,128)S(1)} %copy-done.26, ...), kind=kLoop, calls=%fused_computation.48 | loop fusion | flops 32505344 | bytes 33560576 | tf_op jit(solution)/shard_map/convert_element_type | solution.py:755
  406.8 29.6 %plane_sum.3 = bf16[8,256,256]{2,1,0:T(8,128)(2,1)S(1)} custom-call(f32[2048,256]{1,0:T(8,128)S(1)} %pad_maximum_fusion.part_ref), custom_call_target="tpu_custom_call" | custom-call | tf_op jit(solution)/shard_map/plane_sum/pallas_call | solution.py:57
  436.6 6.9 multiply_multiply_fusion
  443.5 2.0 copy-done.29
  445.5 5.7 conv_grad_edges.1
  451.2 1.0 slice.354
  452.2 3.0 maximum_maximum_fusion
  455.2 1.0 copy-done.30
  456.2 5.4 multiply_reduce_fusion.1
  462.0 4.3 copy.102
  466.3 2.6 convolution_convert_fusion.4
  468.9 2.1 fusion.46
  471.8 4.3 copy.98
  476.1 7.6 %convolution_convert_fusion.2.refs_1_ = bf16[2048,1024]{1,0:T(8,128)(2,1)S(1)} fusion(bf16[2048,1024]{1,0:T(8,128)(2,1)} %bitcast.309, bf16[2048,1024]{1,0:T(8,128)(2,1)} %bitcast.292, s32[]{:T(128)S(6)} %select_n.143), kind=kOutput, calls=%fused_computation.56 | convolution fusion | flops 4297064448 | bytes 10485764 | tf_op jit(solution)/shard_map/dot_general | solution.py:622
  484.4 0.9 copy-done.23
  485.3 2.3 convolution_convert_fusion.refs_0_
  487.6 13.2 %twin_swap.1 = (bf16[2048,1024]{1,0:T(8,128)(2,1)S(1)}, bf16[2048,1024]{1,0:T(8,128)(2,1)S(1)}) custom-call(bf16[2048,1024]{1,0:T(8,128)(2,1)S(1)} %convolution_convert_fusion.refs_0_, bf16[2048,1024]{1,0:T(8,128)(2,1)S(1)} %convolution_convert_fusion.2.refs_1_), custom_call_target="tpu_custom_call" | custom-call | tf_op jit(solution)/shard_map/twin_swap/pallas_call | solution.py:57
  500.9 2.0 copy-done.18
  502.9 2.1 copy-done.20
  504.9 8.9 %add_convert_fusion = bf16[2048,1024]{1,0:T(8,128)(2,1)S(1)} fusion(bf16[2048,1024]{1,0:T(8,128)(2,1)} %copy-done.20, bf16[2048,1024]{1,0:T(8,128)(2,1)} %bitcast.310, bf16[2048,1024]{1,0:T(8,128)(2,1)} %bitcast.293, s32[]{:T(128)S(6)} %select_n.142), kind=kOutput, calls=%fused_computation.4 | convolution fusion | flops 4301258752 | bytes 14680068 | tf_op jit(solution)/shard_map/dot_general | solution.py:622
  513.9 2.5 add_convert_fusion.1
  516.4 14.4 %bitcast_convert_fusion.1 = bf16[512,2048]{1,0:T(8,128)(2,1)S(1)} fusion(bf16[8,256,2048]{2,1,0:T(8,128)(2,1)} %copy-done.15, bf16[256,8,512]{2,1,0:T(8,128)(2,1)S(1)} %copy-done.36), kind=kOutput, calls=%fused_computation.29 | convolution fusion | flops 4296015872 | bytes 12582912 | tf_op jit(solution)/shard_map/dot_general | solution.py:618
  530.8 20.3 %bitcast_convert_fusion = bf16[2048,1024]{1,0:T(8,128)(2,1)S(1)} fusion(bf16[8,256,2048]{2,1,0:T(8,128)(2,1)} %copy-done.14, bf16[8,256,1024]{2,0,1:T(8,128)(2,1)} %copy-done.31), kind=kOutput, calls=%fused_computation.3 | convolution fusion | flops 8592031744 | bytes 16777216 | tf_op jit(solution)/shard_map/dot_general | solution.py:618
  551.1 160.4 %to_owners.1 = (bf16[32,64,1024]{2,1,0:T(8,128)(2,1)S(1)}, bf16[8,256,1024]{2,1,0:T(8,128)(2,1)S(1)}, bf16[8,256,1024]{2,1,0:T(8,128)(2,1)S(1)}, bf16[4,128,2048...) custom-call(bf16[32,64,1024]{2,1,0:T(8,128)(2,1)S(1)} %bitcast.269, ...), custom_call_target="tpu_custom_call" | custom-call | tf_op jit(solution)/shard_map/to_owners/pallas_call | solution.py:57
  711.5 1.9 copy-done.1
  713.5 2.0 copy-done.3
  715.5 1.9 copy-done.5
  718.8 9.2 %reshape.450 = f32[4,8,64,2,4,128]{5,4,3,2,1,0:T(4,128)} reshape(bf16[32,64,1024]{2,1,0:T(8,128)(2,1)} %copy-done.1) | data formatting | bytes 12582912 | tf_op jit(solution)/shard_map/reshape | solution.py:802
  727.9 7.3 reduce_sum.178
  735.3 3.0 copy.105
  738.3 2.9 multiply_reduce_fusion.5
  741.7 0.9 convert_reduce_fusion
  743.0 0.9 copy-done.32
  745.2 0.9 convert_reduce_fusion.1
  746.3 2.2 fusion.40
  748.5 1.4 convert_reduce_fusion.2
  (184 shorter events, 21.6 us)
Async XLA Ops:
  12.6 3.8 copy-start.46
  14.2 2.2 copy-start.48
  22.2 4.8 copy-start.7
  184.3 9.2 %copy-start.14 = (bf16[8,256,2048]{2,1,0:T(8,128)(2,1)}, bf16[8,256,2048]{2,1,0:T(8,128)(2,1)S(1)}, u32[]{:S(2)}) copy-start(bf16[8,256,2048]{2,1,0:T(8,128)(2,1)S(1)} %get-tuple-element.38) | copy-start | bytes 25165828
  184.3 9.2 %copy-start.15 = (bf16[8,256,2048]{2,1,0:T(8,128)(2,1)}, bf16[8,256,2048]{2,1,0:T(8,128)(2,1)S(1)}, u32[]{:S(2)}) copy-start(bf16[8,256,2048]{2,1,0:T(8,128)(2,1)S(1)} %get-tuple-element.41) | copy-start | bytes 25165828
  184.3 9.2 %copy-start.17 = (bf16[32,64,1024]{2,1,0:T(8,128)(2,1)}, bf16[32,64,1024]{2,1,0:T(8,128)(2,1)S(1)}, u32[]{:S(2)}) copy-start(bf16[32,64,1024]{2,1,0:T(8,128)(2,1)S(1)} %get-tuple-element.40) | copy-start | bytes 12582916
  184.3 9.2 %copy-start.21 = (bf16[4,128,2048]{2,1,0:T(8,128)(2,1)}, bf16[4,128,2048]{2,1,0:T(8,128)(2,1)S(1)}, u32[]{:S(2)}) copy-start(bf16[4,128,2048]{2,1,0:T(8,128)(2,1)S(1)} %get-tuple-element.42) | copy-start | bytes 6291460
  195.8 2.1 copy-start.27
  203.7 4.0 copy-start.16
  205.5 3.0 copy-start.22
  207.7 14.3 %copy-start.24 = (f32[259,8,512]{2,1,0:T(8,128)}, f32[259,8,512]{2,1,0:T(8,128)S(1)}, u32[]{:S(2)}) copy-start(f32[259,8,512]{2,1,0:T(8,128)S(1)} %maximum_convert_fusion) | copy-start | bytes 12730372
  221.9 40.4 %copy-start.53 = (f32[1,4,128]{2,0,1:T(1,128)}, f32[1,4,128]{2,0,1:T(1,128)S(1)}, u32[]{:S(2)}) copy-start(f32[1,4,128]{2,0,1:T(1,128)S(1)} %get-tuple-element.102) | copy-start | bytes 6148
  228.9 2.2 copy-start.25
  230.1 1.5 copy-start.33
  262.3 18.3 %copy-start.44 = (bf16[128,4,128]{0,2,1:T(8,128)(2,1)}, bf16[128,4,128]{0,2,1:T(8,128)(2,1)S(1)}, u32[]{:S(2)}) copy-start(bf16[128,4,128]{0,2,1:T(8,128)(2,1)S(1)} %copy.87) | copy-start | bytes 393220
  262.4 18.4 %copy-start.2 = (bf16[128,4096]{1,0:T(8,128)(2,1)S(1)}, bf16[128,4096]{1,0:T(8,128)(2,1)}, u32[]{:S(2)}) copy-start(bf16[128,4096]{1,0:T(8,128)(2,1)} %constant.89.clone.fan_ref) | copy-start | bytes 3145732
  280.6 25.5 %copy-start = (bf16[256,8,128]{2,1,0:T(8,128)(2,1)}, bf16[256,8,128]{2,1,0:T(8,128)(2,1)S(1)}, u32[]{:S(2)}) copy-start(bf16[256,8,128]{2,1,0:T(8,128)(2,1)S(1)} %slice_bitcast_fusion.coef_ref) | copy-start | bytes 1572868
  280.7 25.4 %copy-start.8 = (f32[128,512]{1,0:T(8,128)}, f32[128,512]{1,0:T(8,128)S(1)}, u32[]{:S(2)}) copy-start(f32[128,512]{1,0:T(8,128)S(1)} %broadcast_bitcast_fusion.rate_ref) | copy-start | bytes 786436
  306.2 0.7 copy-start.11
  307.2 0.7 copy-start.41
  330.6 63.2 %copy-start.26 = (f32[256,8,512]{2,1,0:T(8,128)S(1)}, f32[256,8,512]{2,1,0:T(8,128)}, u32[]{:S(2)}) copy-start(f32[256,8,512]{2,1,0:T(8,128)} %copy-done.25) | copy-start | bytes 12582916
  330.6 63.2 %copy-start.52 = (f32[1,4,128]{2,0,1:T(1,128)S(1)}, f32[1,4,128]{2,0,1:T(1,128)}, u32[]{:S(2)}) copy-start(f32[1,4,128]{2,0,1:T(1,128)} %get-tuple-element.101) | copy-start | bytes 6148
  330.6 63.2 %copy-start.54 = (f32[1,4,128]{2,0,1:T(1,128)S(1)}, f32[1,4,128]{2,0,1:T(1,128)}, u32[]{:S(2)}) copy-start(f32[1,4,128]{2,0,1:T(1,128)} %copy-done.53) | copy-start | bytes 6148
  393.8 12.1 %copy-start.45 = (bf16[128,4,128]{0,2,1:T(8,128)(2,1)S(1)}, bf16[128,4,128]{0,2,1:T(8,128)(2,1)}, u32[]{:S(2)}) copy-start(bf16[128,4,128]{0,2,1:T(8,128)(2,1)} %copy-done.44) | copy-start | bytes 393220
  393.9 12.8 %copy-start.42 = (f32[256,8,128]{2,1,0:T(8,128)S(1)}, f32[256,8,128]{2,1,0:T(8,128)}, u32[]{:S(2)}) copy-start(f32[256,8,128]{2,1,0:T(8,128)} %get-tuple-element.53) | copy-start | bytes 3145732
  405.9 30.5 %copy-start.28 = (bf16[256,8,512]{2,1,0:T(8,128)(2,1)}, bf16[256,8,512]{2,1,0:T(8,128)(2,1)S(1)}, u32[]{:S(2)}) copy-start(bf16[256,8,512]{2,1,0:T(8,128)(2,1)S(1)} %get-tuple-element.90) | copy-start | bytes 6291460
  406.6 29.8 %copy-start.43 = (bf16[160,4,128]{2,0,1:T(8,128)(2,1)S(1)}, bf16[160,4,128]{2,0,1:T(8,128)(2,1)}, u32[]{:S(2)}) copy-start(bf16[160,4,128]{2,0,1:T(8,128)(2,1)} %get-tuple-element.99) | copy-start | bytes 491524
  443.5 2.0 copy-start.29
  451.2 4.0 slice-start
  452.2 3.0 slice-start.1
  452.2 4.0 copy-start.30
  456.2 5.4 copy-start.50
  456.2 5.4 copy-start.51
  466.3 4.8 copy-start.37
  466.3 4.8 copy-start.38
  471.8 4.3 copy-start.31
  476.1 7.6 %copy-start.35 = (bf16[256,8,512]{2,1,0:T(8,128)(2,1)S(1)}, bf16[256,8,512]{2,1,0:T(8,128)(2,1)}, u32[]{:S(2)}) copy-start(bf16[256,8,512]{2,1,0:T(8,128)(2,1)} %get-tuple-element.86) | copy-start | bytes 6291460
  483.7 1.6 copy-start.23
  484.4 3.2 copy-start.39
  500.9 2.0 copy-start.18
  502.9 2.1 copy-start.20
  504.9 8.9 %copy-start.19 = (bf16[2048,1024]{1,0:T(8,128)(2,1)S(1)}, bf16[2048,1024]{1,0:T(8,128)(2,1)}, u32[]{:S(2)}) copy-start(bf16[2048,1024]{1,0:T(8,128)(2,1)} %copy-done.18) | copy-start | bytes 12582916
  504.9 9.0 %copy-start.40 = (bf16[8,256,512]{2,1,0:T(8,128)(2,1)S(1)}, bf16[8,256,512]{2,1,0:T(8,128)(2,1)}, u32[]{:S(2)}) copy-start(bf16[8,256,512]{2,1,0:T(8,128)(2,1)} %copy-done.39) | copy-start | bytes 6291460
  513.9 2.5 copy-start.36
  711.5 2.0 copy-start.1
  713.5 2.0 copy-start.3
  715.5 2.0 copy-start.5
  717.4 0.7 copy-start.9
  718.1 0.6 copy-start.12
  735.3 3.0 copy-start.34
  738.3 2.9 copy-start.55
  738.3 3.4 copy-start.6
  742.6 1.2 copy-start.32
  742.7 1.2 copy-start.47
  742.7 1.2 copy-start.49
  742.7 2.5 copy-start.4
  746.3 3.6 copy-start.10
  746.3 4.9 copy-start.13

commit v2 on v1

v2 whole, which is shorter than its diff:
```python
import functools

import jax
import jax.numpy as jnp
import numpy as np
from jax import lax
from jax.experimental import pallas as pl
from jax.experimental.pallas import tpu as pltpu
from jax.sharding import PartitionSpec as P

D = 2048
DI = 4096
STATE = 16
DT_RANK = 128
KW = 4
EPS = 1e-05
LOG2E = 1.4426950408889634
STEPS = 16
MESH = pl.DeviceIdType.MESH
BF16 = jnp.bfloat16
F32 = jnp.float32


class Grid:
    def __init__(self, ctx, fsdp):
        self.ctx, self.fsdp = ctx, fsdp
        self.planes = ctx // 4
        self.members = 4 * fsdp
        self.devices = ctx * fsdp

    def here(self):
        c, f = lax.axis_index("ctx"), lax.axis_index("fsdp")
        return c // 4, c % 4, f

    def at(self, z, q, f):
        return {"ctx": z * 4 + q, "fsdp": f}

    def member(self, z, j):
        return self.at(z, j // self.fsdp, j % self.fsdp)


def remote(src, dst, send, recv, where):
    return pltpu.make_async_remote_copy(
        src_ref=src, dst_ref=dst, send_sem=send, recv_sem=recv, device_id=where, device_id_type=MESH
    )


def greet(places):
    barrier = pltpu.get_barrier_semaphore()
    for place in places:
        pl.semaphore_signal(barrier, inc=1, device_id=place, device_id_type=MESH)
    pl.semaphore_wait(barrier, len(places))


def comm_call(kernel, outs, scratch, ident, name, args, vmem=None, in_vmem=()):
    spaces = [pl.BlockSpec(memory_space=pltpu.VMEM if i in in_vmem else pl.ANY) for i in range(len(args))]
    return pl.pallas_call(
        kernel,
        in_specs=spaces,
        out_specs=[pl.BlockSpec(memory_space=pl.ANY)] * len(outs),
        out_shape=outs,
        scratch_shapes=scratch,
        compiler_params=pltpu.CompilerParams(
            collective_id=ident, has_side_effects=True, vmem_limit_bytes=vmem or 16 * 2**20
        ),
        name=name,
    )(*args)


def gather_kernel(grid, rows, h_ref, g_ref, c_ref, wi_ref, sm_ref, n_all, c_all, wi_all, sm_all, gain_out,
                  gain_buf, gains, n_low, local, g_send, g_recv, n_send, n_recv, c_send, c_recv, a_send, a_recv,
                  z_send, z_recv, s_send, s_recv):
    z, q, f = grid.here()
    F, C, Z, N = grid.fsdp, grid.members, grid.planes, grid.devices
    me = q * F + f
    lin = z * C + me
    opposite, twin = q ^ 2, q ^ 1
    barrier = pltpu.get_barrier_semaphore()

    def other(d):
        to = lax.rem(lin + d, N)
        return grid.member(to // C, lax.rem(to, C))

    @pl.loop(1, N)
    def _(d):
        pl.semaphore_signal(barrier, inc=1, device_id=other(d), device_id_type=MESH)

    pl.semaphore_wait(barrier, N - 1)

    def gain_copy(d):
        return remote(g_ref, gain_buf.at[lin], g_send.at[d], g_recv.at[d], other(d))

    @pl.loop(1, N)
    def _(d):
        gain_copy(d).start()

    sends = []

    def push(copy):
        copy.start()
        sends.append(copy)

    def block_of(i):
        return lax.rem(me + C - i, C)

    def line_pair(step, i):
        right, left = z - step, z + step
        if step == 0 and i == 0:
            src_right = src_left = wi_ref.at[me]
        else:
            src_right, src_left = wi_all.at[right * C + block_of(i)], wi_all.at[left * C + block_of(i)]
        return (
            (z < Z - 1) & (right >= 0),
            remote(src_right, wi_all.at[right * C + block_of(i)], z_send.at[0, step, i], z_recv.at[0, step, i], grid.at(z + 1, q, f)),
            (z > 0) & (left <= Z - 1),
            remote(src_left, wi_all.at[left * C + block_of(i)], z_send.at[1, step, i], z_recv.at[1, step, i], grid.at(z - 1, q, f)),
        )

    def line_start(step, i):
        to_right, right, to_left, left = line_pair(step, i)

        @pl.when(to_right)
        def _():
            right.start()

        @pl.when(to_left)
        def _():
            left.start()

    def line_done(step, i):
        to_right, right, to_left, left = line_pair(step, i)

        @pl.when(to_right)
        def _():
            right.wait_send()

        @pl.when(to_left)
        def _():
            left.wait_send()

    def line_arrived(step, i):
        from_left, from_right = z - 1 - step, z + 1 + step

        @pl.when(from_left >= 0)
        def _():
            ref = wi_all.at[from_left * C + block_of(i)]
            remote(ref, ref, z_send.at[0, step, i], z_recv.at[0, step, i], grid.at(z - 1, q, f)).wait_recv()

        @pl.when(from_right <= Z - 1)
        def _():
            ref = wi_all.at[from_right * C + block_of(i)]
            remote(ref, ref, z_send.at[1, step, i], z_recv.at[1, step, i], grid.at(z + 1, q, f)).wait_recv()

    line_start(0, 0)
    for d in range(1, C):
        j = lax.rem(me + d, C)
        push(remote(wi_ref.at[j], wi_all.at[lin], a_send.at[d], a_recv.at[d], grid.member(z, j)))
    for d in range(1, Z):
        push(remote(sm_ref, sm_all.at[z], s_send.at[d], s_recv.at[d], grid.at(lax.rem(z + d, Z), q, f)))

    n_sent, c_sent = [0], [0]

    def push_n(block, src, where):
        push(remote(src, n_all.at[block], n_send.at[n_sent[0]], n_recv.at[block], where))
        n_sent[0] += 1

    def push_c(block, src, where):
        push(remote(src, c_all.at[block], c_send.at[c_sent[0]], c_recv.at[block], where))
        c_sent[0] += 1

    def arrived(ref, sems, block):
        remote(ref.at[block], ref.at[block], n_send.at[0], sems.at[block], grid.at(z, twin, f)).wait_recv()

    others = [lax.rem(f + d, F) for d in range(1, F)]
    push_c(me, c_ref, grid.at(z, opposite, f))

    gain_buf[lin] = g_ref[...]

    @pl.loop(1, N)
    def _(d):
        back = lax.rem(lin + N - d, N)
        remote(g_ref, gain_buf.at[back], g_send.at[d], g_recv.at[d], grid.member(back // C, lax.rem(back, C))).wait_recv()

    per = max(1, 128 // rows)
    for chunk in range(D // 128):
        gain = gain_buf[chunk * per]
        for k in range(1, per):
            gain = gain + gain_buf[chunk * per + k]
        gains[:, chunk * 128:(chunk + 1) * 128] = gain

    @pl.loop(0, h_ref.shape[0] // 16)
    def _(r):
        at = pl.ds(pl.multiple_of(r * 16, 16), 16)
        hidden = h_ref[at, :].astype(F32)
        scale = lax.rsqrt(jnp.mean(hidden * hidden, axis=1, keepdims=True) + EPS)
        n_low[at, :] = (hidden * scale * gains[0:1, :]).astype(BF16)

    for g in others:
        push_n(me, n_low, grid.at(z, q, g))
    push_n(me, n_low, grid.at(z, opposite, f))
    for g in others:
        push_c(me, c_ref, grid.at(z, q, g))
    push_n(me, n_low, grid.at(z, twin, f))
    push_c(me, c_ref, grid.at(z, twin, f))
    mine = [
        pltpu.make_async_copy(n_low, n_all.at[me], local.at[0]),
        pltpu.make_async_copy(c_ref, c_all.at[me], local.at[1]),
        pltpu.make_async_copy(wi_ref.at[me], wi_all.at[lin], local.at[2]),
        pltpu.make_async_copy(sm_ref, sm_all.at[z], local.at[3]),
        pltpu.make_async_copy(gains, gain_out, local.at[4]),
    ]
    for copy in mine:
        copy.start()
    for d in range(1, C):
        back = block_of(d)
        remote(wi_ref.at[me], wi_all.at[z * C + back], a_send.at[d], a_recv.at[d], grid.member(z, back)).wait_recv()
        line_start(0, d)
    mine[2].wait()

    def pass_on(step, blocks):
        for i in blocks:
            line_arrived(step, i)
            if step < Z - 2:
                line_start(step + 1, i)

    pass_on(0, range(C // 2))
    for g in others:
        block = q * F + g
        arrived(n_all, n_recv, block)
        push_n(block, n_all.at[block], grid.at(z, opposite, f))
        push_n(block, n_all.at[block], grid.at(z, twin, f))
    arrived(c_all, c_recv, opposite * F + f)
    for g in others:
        push_c(opposite * F + f, c_all.at[opposite * F + f], grid.at(z, q, g))
    push_c(opposite * F + f, c_all.at[opposite * F + f], grid.at(z, twin, f))
    pass_on(0, range(C // 2, C))
    for step in range(1, Z - 2):
        pass_on(step, range(C))
    for g in others:
        arrived(c_all, c_recv, q * F + g)
        push_c(q * F + g, c_all.at[q * F + g], grid.at(z, twin, f))
    for g in [f] + others:
        block = opposite * F + g
        arrived(n_all, n_recv, block)
        push_n(block, n_all.at[block], grid.at(z, twin, f))
    for g in others:
        block = opposite * F + g
        arrived(c_all, c_recv, block)
        push_c(block, c_all.at[block], grid.at(z, twin, f))
    pass_on(Z - 2, range(C))
    for side in (twin, twin ^ 2):
        for g in [f] + others:
            arrived(n_all, n_recv, side * F + g)
            arrived(c_all, c_recv, side * F + g)
    for d in range(1, Z):
        back = lax.rem(z + Z - d, Z)
        remote(sm_ref, sm_all.at[back], s_send.at[d], s_recv.at[d], grid.at(back, q, f)).wait_recv()
    for i in (0, 1, 3, 4):
        mine[i].wait()
    for copy in sends:
        copy.wait_send()
    for step in range(Z - 1):
        for i in range(C):
            line_done(step, i)

    @pl.loop(1, N)
    def _(d):
        gain_copy(d).wait_send()


def gather_all(grid, hidden, gain_tile, cot, wi, small):
    F, C, Z, N = grid.fsdp, grid.members, grid.planes, grid.devices
    tokens, rows = hidden.shape[0], wi.shape[1]
    dma = pltpu.SemaphoreType.DMA
    outs = [
        jax.ShapeDtypeStruct((C, tokens, D), BF16),
        jax.ShapeDtypeStruct((C, tokens, D), BF16),
        jax.ShapeDtypeStruct((Z * C,) + wi.shape[1:], BF16),
        jax.ShapeDtypeStruct((Z,) + small.shape, BF16),
        jax.ShapeDtypeStruct((8, D), F32),
    ]
    count = (F - 1) + F + 2 * F
    scratch = [pltpu.VMEM((N, 8, 128), F32), pltpu.VMEM((8, D), F32), pltpu.VMEM((tokens, D), BF16)]
    scratch += [dma((5,)), dma((N,)), dma((N,)), dma((count,)), dma((C,)), dma((count,)), dma((C,)), dma((C,)), dma((C,))]
    scratch += [dma((2, Z, C)), dma((2, Z, C)), dma((Z,)), dma((Z,))]
    return comm_call(
        functools.partial(gather_kernel, grid, rows), outs, scratch, 1, "gather_weights_and_tokens",
        (hidden, gain_tile, cot, wi, small), in_vmem=(0, 1),
    )


def plane_sum_kernel(grid, part_ref, out_ref, send_buf, recv_buf, result, send, recv, out_send, out_recv, own):
    z, q, f = grid.here()
    C = grid.members
    me = q * grid.fsdp + f
    rows = recv_buf.shape[1]
    greet([grid.member(z, lax.rem(me + d, C)) for d in range(1, C)])
    lane = lax.broadcasted_iota(jnp.int32, (rows, 128), 1)

    def packed(v):
        high = v.astype(BF16).astype(F32)
        return high + pltpu.roll(v - high, 32, 1)

    @pl.loop(0, C)
    def _(k):
        at = pl.ds(pl.multiple_of(k * rows, 16), rows)
        send_buf[k, :, 0:128] = part_ref[at, 0:128].astype(BF16)
        send_buf[k, :, 128:256] = packed(part_ref[at, 128:256]).astype(BF16)

    copies = []
    for d in range(1, C):
        j = lax.rem(me + d, C)
        copy = remote(send_buf.at[j], recv_buf.at[d], send.at[d], recv.at[d], grid.member(z, j))
        copy.start()
        copies.append(copy)
    low = send_buf[me, :, 0:128].astype(F32)
    high = send_buf[me, :, 128:256].astype(F32)
    for d in range(1, C):
        copies[d - 1].wait_recv()
        low = low + recv_buf[d, :, 0:128].astype(F32)
        high = high + recv_buf[d, :, 128:256].astype(F32)
    total = jnp.where(lane < 32, high + pltpu.roll(high, 96, 1), 0.0)
    result[:, 0:128] = low.astype(BF16)
    result[:, 128:256] = packed(total).astype(BF16)
    for copy in copies:
        copy.wait_send()
    mine = pltpu.make_async_copy(result, out_ref.at[me], own)
    mine.start()
    copies = []
    for d in range(1, C):
        j = lax.rem(me + d, C)
        copy = remote(result, out_ref.at[me], out_send.at[d], out_recv.at[d], grid.member(z, j))
        copy.start()
        copies.append(copy)
    mine.wait()
    for d in range(1, C):
        back = lax.rem(me + C - d, C)
        remote(result, out_ref.at[back], out_send.at[d], out_recv.at[d], grid.member(z, back)).wait_recv()
    for copy in copies:
        copy.wait_send()


def plane_sum(grid, part, ident):
    C = grid.members
    rows = part.shape[0] // C
    dma = pltpu.SemaphoreType.DMA
    out = comm_call(
        functools.partial(plane_sum_kernel, grid),
        [jax.ShapeDtypeStruct((C, rows, 256), BF16)],
        [pltpu.VMEM((C, rows, 256), BF16), pltpu.VMEM((C, rows, 256), BF16), pltpu.VMEM((rows, 256), BF16)]
        + [dma((C,))] * 4 + [dma],
        ident, "plane_sum", (part,), vmem=40 * 2**20, in_vmem=(0,),
    )[0]
    return out.reshape(C * rows, 256)


def line_gather_kernel(grid, count, *refs):
    z, q, f = grid.here()
    Z = grid.planes
    ins, outs = refs[:count], refs[count:2 * count]
    local, send, recv = refs[2 * count:]
    greet([grid.at(lax.rem(z + d, Z), q, f) for d in range(1, Z)])
    copies = []
    for i in range(count):
        mine = pltpu.make_async_copy(ins[i], outs[i].at[z], local.at[i])
        mine.start()
        copies.append(mine)
    pushes = []
    for i in range(count):
        for d in range(1, Z):
            copy = remote(ins[i], outs[i].at[z], send.at[i, d], recv.at[i, d], grid.at(lax.rem(z + d, Z), q, f))
            copy.start()
            pushes.append(copy)
    for mine in copies:
        mine.wait()
    for i in range(count):
        for d in range(1, Z):
            back = lax.rem(z + Z - d, Z)
            remote(ins[i], outs[i].at[back], send.at[i, d], recv.at[i, d], grid.at(back, q, f)).wait_recv()
    for copy in pushes:
        copy.wait_send()


def line_gather(grid, arrays, ident, name):
    dma = pltpu.SemaphoreType.DMA
    n, Z = len(arrays), grid.planes
    return comm_call(
        functools.partial(line_gather_kernel, grid, n),
        [jax.ShapeDtypeStruct((Z,) + a.shape, a.dtype) for a in arrays],
        [dma((n,)), dma((n, Z)), dma((n, Z))], ident, name, tuple(arrays),
    )


def owners_kernel(grid, planes_in, lines_in, *refs):
    z, q, f = grid.here()
    C, Z = grid.members, grid.planes
    me = q * grid.fsdp + f
    total = 1 + planes_in + lines_in
    ins, outs = refs[:total], refs[total:2 * total]
    slots, own, result, local, w_send, w_recv, r_send, r_recv, p_send, p_recv, l_send, l_recv = refs[2 * total:]
    greet([grid.member(z, lax.rem(me + d, C)) for d in range(1, C)] + [grid.at(lax.rem(z + d, Z), q, f) for d in range(1, Z)])
    load = pltpu.make_async_copy(ins[0].at[z], own, local.at[0])
    load.start()
    weights, mine, pushes, waits = [], [], [], []
    for d in range(1, Z):
        j = lax.rem(z + d, Z)
        weights.append(remote(ins[0].at[j], slots.at[d], w_send.at[d], w_recv.at[d], grid.at(j, q, f)))
    for copy in weights:
        copy.start()
    for i in range(planes_in):
        mine.append(pltpu.make_async_copy(ins[1 + i].at[me], outs[1 + i].at[me], local.at[1 + i]))
        for d in range(1, C):
            j, back = lax.rem(me + d, C), lax.rem(me + C - d, C)
            pushes.append(remote(ins[1 + i].at[j], outs[1 + i].at[me], p_send.at[i, d], p_recv.at[i, d], grid.member(z, j)))
            waits.append(remote(ins[1 + i].at[me], outs[1 + i].at[back], p_send.at[i, d], p_recv.at[i, d], grid.member(z, back)))
    for i in range(lines_in):
        k = 1 + planes_in + i
        mine.append(pltpu.make_async_copy(ins[k].at[z], outs[k].at[z], local.at[k]))
        for d in range(1, Z):
            j, back = lax.rem(z + d, Z), lax.rem(z + Z - d, Z)
            pushes.append(remote(ins[k].at[j], outs[k].at[z], l_send.at[i, d], l_recv.at[i, d], grid.at(j, q, f)))
            waits.append(remote(ins[k].at[z], outs[k].at[back], l_send.at[i, d], l_recv.at[i, d], grid.at(back, q, f)))
    for copy in pushes + mine:
        copy.start()
    load.wait()
    for copy in weights:
        copy.wait_recv()

    @pl.loop(0, C)
    def _(j):
        value = own[j].astype(F32)
        for d in range(1, Z):
            value = value + slots[d, j].astype(F32)
        result[j] = value.astype(BF16)

    mine.append(pltpu.make_async_copy(result.at[me], outs[0].at[me], local.at[0]))
    mine[-1].start()
    for d in range(1, C):
        j, back = lax.rem(me + d, C), lax.rem(me + C - d, C)
        copy = remote(result.at[j], outs[0].at[me], r_send.at[d], r_recv.at[d], grid.member(z, j))
        copy.start()
        pushes.append(copy)
        waits.append(remote(result.at[me], outs[0].at[back], r_send.at[d], r_recv.at[d], grid.member(z, back)))
    for copy in mine:
        copy.wait()
    for copy in waits:
        copy.wait_recv()
    for copy in pushes + weights:
        copy.wait_send()


def to_owners(grid, weight, plane_arrays, line_arrays, ident):
    dma = pltpu.SemaphoreType.DMA
    C, Z = grid.members, grid.planes
    p, l = len(plane_arrays), len(line_arrays)
    args = (weight,) + tuple(plane_arrays) + tuple(line_arrays)
    part = weight.shape[1:]
    outs = [jax.ShapeDtypeStruct(part, BF16)] + [jax.ShapeDtypeStruct(a.shape, a.dtype) for a in args[1:]]
    return comm_call(
        functools.partial(owners_kernel, grid, p, l), outs,
        [pltpu.VMEM((Z,) + part, BF16), pltpu.VMEM(part, BF16), pltpu.VMEM(part, BF16)]
        + [dma((1 + p + l,)), dma((Z,)), dma((Z,)), dma((C,)), dma((C,)), dma((p, C)), dma((p, C)), dma((l, Z)), dma((l, Z))],
        ident, "to_owners", args,
    )


def place_kernel(grid, *refs):
    z, _, _ = grid.here()
    Z = grid.planes
    for d in range(Z):
        refs[Z][lax.rem(z + Z - d, Z)] = refs[d][...]


def in_place_order(grid, pieces):
    Z = grid.planes
    return pl.pallas_call(
        functools.partial(place_kernel, grid),
        in_specs=[pl.BlockSpec(memory_space=pltpu.VMEM)] * Z,
        out_specs=pl.BlockSpec(memory_space=pltpu.VMEM),
        out_shape=jax.ShapeDtypeStruct((Z,) + pieces[0].shape, pieces[0].dtype),
        compiler_params=pltpu.CompilerParams(vmem_limit_bytes=16 * 2**20),
        name="in_place_order",
    )(*pieces)

def spread(coef_ref, fan_ref, splat, tc):
    c = coef_ref[...].reshape(8 * tc, 128)
    for k in range(0, 2 * STATE, 4):
        l = pl.ds(k * 128, 512)
        splat[:, l] = jnp.dot(c, fan_ref[:, l], preferred_element_type=F32)

def rows8(t):
    return pl.ds(pl.multiple_of(t * 8, 8), 8)

def ends_kernel(cd, tc, delta_ref, w_ref, ds_ref, coef_ref, rate_ref, fan_ref, e_ref, g_ref, tot_ref, p_scr, splat):
    ch = pl.program_id(1)
    tiles = cd // 128
    @pl.when(ch == 0)
    def _():
        e_ref[...] = jnp.zeros_like(e_ref)
        g_ref[...] = jnp.zeros_like(g_ref)
        tot_ref[...] = jnp.zeros_like(tot_ref)
        p_scr[...] = jnp.ones_like(p_scr)
    spread(coef_ref, fan_ref, splat, tc)
    group = 4
    for tile in range(tiles):
        lanes = pl.ds(tile * 128, 128)
        for n0 in range(0, STATE, group):
            rates = [rate_ref[(n0 + i) * 8:(n0 + i + 1) * 8, lanes] for i in range(group)]
            def body(t, carry):
                hs, ps, gs = carry
                tok = pl.ds(pl.multiple_of(t * 8, 8), 8)
                d, w, s = delta_ref[t, :, lanes], w_ref[t, :, lanes], ds_ref[t, :, lanes]
                nh, np_, ng = [], [], []
                for i in range(group):
                    a = jnp.exp2(d * rates[i])
                    cin = splat[rows8(t), pl.ds((n0 + i) * 128, 128)]
                    cout = splat[rows8(t), pl.ds((STATE + n0 + i) * 128, 128)]
                    nh.append(a * hs[i] + cin * w)
                    p = ps[i] * a
                    np_.append(p)
                    ng.append(gs[i] + p * (cout * s))
                return tuple(nh), tuple(np_), tuple(ng)
            rows = [pl.ds((n0 + i) * 8, 8) for i in range(group)]
            init = (tuple(e_ref[0, r, lanes] for r in rows), tuple(p_scr[r, lanes] for r in rows), tuple(g_ref[0, r, lanes] for r in rows))
            hs, ps, gs = lax.fori_loop(0, tc, body, init, unroll=tc)
            for i, r in enumerate(rows):
                e_ref[0, r, lanes] = hs[i]
                p_scr[r, lanes] = ps[i]
                g_ref[0, r, lanes] = gs[i]
        def total(t, acc):
            return acc + delta_ref[t, :, lanes]
        tot_ref[0, :, lanes] = lax.fori_loop(0, tc, total, tot_ref[0, :, lanes], unroll=tc)

def scan_ends(delta, w, ds, coef, rate, fan, tc=STEPS, vmem=48 * 2**20):
    tokens, members, cd = delta.shape
    sg, nch = members // 8, tokens // tc
    rows = STATE * 8
    tok = lambda width: pl.BlockSpec((tc, 8, width), lambda s, c: (c, s, 0))
    keep = lambda r: pl.BlockSpec((1, r, cd), lambda s, c: (s, 0, 0))
    return pl.pallas_call(
        functools.partial(ends_kernel, cd, tc),
        grid=(sg, nch),
        in_specs=[tok(cd), tok(cd), tok(cd), pl.BlockSpec((tc, 8, 128), lambda s, c: (c, s, 0)), pl.BlockSpec((rows, cd), lambda s, c: (0, 0)), pl.BlockSpec(fan.shape, lambda s, c: (0, 0))],
        out_specs=[keep(rows), keep(rows), keep(8)],
        out_shape=[jax.ShapeDtypeStruct((sg, rows, cd), F32), jax.ShapeDtypeStruct((sg, rows, cd), F32), jax.ShapeDtypeStruct((sg, 8, cd), F32)],
        scratch_shapes=[pltpu.VMEM((rows, cd), F32), pltpu.VMEM((tc * 8, 2 * STATE * 128), F32)],
        compiler_params=pltpu.CompilerParams(vmem_limit_bytes=vmem),
        name="segment_ends",
    )(delta, w, ds, coef, rate, fan)

def forward_kernel(cd, tc, delta_ref, w_ref, ds_ref, coef_ref, rate_ref, fan_ref, fold_ref, sin_ref,
                   y_ref, hist_ref, dc_ref, h_scr, splat, acc_out):
    ch = pl.program_id(1)
    tiles = cd // 128

    @pl.when(ch == 0)
    def _():
        h_scr[...] = sin_ref[0]

    spread(coef_ref, fan_ref, splat, tc)
    at = [pl.ds(tile * 128, 128) for tile in range(tiles)]
    group = 4
    for n0 in range(0, STATE, group):
        pairs = [(n, i) for n in range(n0, n0 + group) for i in range(tiles)]
        init = tuple(h_scr[pl.ds(n * 8, 8), at[i]] for n, i in pairs)

        def forward(t, hs, n0=n0):
            d = [delta_ref[t, :, l] for l in at]
            w = [w_ref[t, :, l] for l in at]
            s = [ds_ref[t, :, l] for l in at]
            y = [None] * tiles if n0 == 0 else [y_ref[t, :, l] for l in at]
            out = []
            for n in range(n0, n0 + group):
                r = pl.ds(n * 8, 8)
                cin = splat[rows8(t), pl.ds(n * 128, 128)]
                cout = splat[rows8(t), pl.ds((STATE + n) * 128, 128)]
                acc = None
                for i in range(tiles):
                    old = hs[len(out)]
                    hist_ref[0, t, r, at[i]] = old
                    h = jnp.exp2(d[i] * rate_ref[r, at[i]]) * old + cin * w[i]
                    out.append(h)
                    y[i] = cout * h if n == 0 else y[i] + cout * h
                    acc = s[i] * h if i == 0 else acc + s[i] * h
                acc_out[rows8(t), pl.ds(n * 128, 128)] = acc
            for i in range(tiles):
                y_ref[t, :, at[i]] = y[i]
            return tuple(out)

        hs = lax.fori_loop(0, tc, forward, init, unroll=tc)
        for j, (n, i) in enumerate(pairs):
            h_scr[pl.ds(n * 8, 8), at[i]] = hs[j]
    sums = jnp.dot(acc_out[...].astype(BF16), fold_ref[1], preferred_element_type=F32)
    dc_ref[...] = sums.reshape(tc, 8, 128)


def scan_forward(delta, w, ds, coef, rate, fan, fold, s_in, tc=STEPS, vmem=56 * 2**20):
    tokens, members, cd = delta.shape
    sg, nch = members // 8, tokens // tc
    rows = STATE * 8
    tok = lambda width: pl.BlockSpec((tc, 8, width), lambda s, c: (c, s, 0))
    keep = lambda r: pl.BlockSpec((1, r, cd), lambda s, c: (s, 0, 0))
    whole = lambda a: pl.BlockSpec(a.shape, lambda s, c: (0,) * a.ndim)
    return pl.pallas_call(
        functools.partial(forward_kernel, cd, tc),
        grid=(sg, nch),
        in_specs=[tok(cd), tok(cd), tok(cd), tok(128), whole(rate), whole(fan), whole(fold), keep(rows)],
        out_specs=[tok(cd), pl.BlockSpec((1, tc, rows, cd), lambda s, c: (s, c, 0, 0)), tok(128)],
        out_shape=[jax.ShapeDtypeStruct(delta.shape, F32), jax.ShapeDtypeStruct((sg, tokens, rows, cd), F32), jax.ShapeDtypeStruct((tokens, members, 128), F32)],
        scratch_shapes=[pltpu.VMEM((rows, cd), F32), pltpu.VMEM((tc * 8, 2 * STATE * 128), F32), pltpu.VMEM((tc * 8, STATE * 128), F32)],
        compiler_params=pltpu.CompilerParams(vmem_limit_bytes=vmem),
        cost_estimate=pl.CostEstimate(flops=30 * 10**9, bytes_accessed=90 * 10**6, transcendentals=0),
        name="scan_forward",
    )(delta, w, ds, coef, rate, fan, fold, s_in)


def backward_kernel(cd, tc, delta_ref, w_ref, ds_ref, coef_ref, rate_ref, fan_ref, fold_ref, hist_ref, dout_ref, gin_ref,
                    a_ref, s_ref, dc_ref, rs_ref, g_scr, splat, acc_in):
    ch = pl.program_id(1)
    tiles = cd // 128

    @pl.when(ch == 0)
    def _():
        rs_ref[...] = jnp.zeros_like(rs_ref)
        g_scr[...] = gin_ref[0]

    spread(coef_ref, fan_ref, splat, tc)
    at = [pl.ds(tile * 128, 128) for tile in range(tiles)]
    group = 2
    for n0 in range(0, STATE, group):
        pairs = [(n, i) for n in range(n0, n0 + group) for i in range(tiles)]
        init = (tuple(g_scr[pl.ds(n * 8, 8), at[i]] for n, i in pairs), tuple(rs_ref[0, pl.ds(n * 8, 8), at[i]] for n, i in pairs))

        def backward(k, carry, n0=n0):
            gs, rs = carry
            t = tc - 1 - k
            d = [delta_ref[t, :, l] for l in at]
            w = [w_ref[t, :, l] for l in at]
            s = [ds_ref[t, :, l] for l in at]
            da = [None] * tiles if n0 == 0 else [a_ref[t, :, l] for l in at]
            cs = [None] * tiles if n0 == 0 else [s_ref[t, :, l] for l in at]
            ng, nr = [], []
            for n in range(n0, n0 + group):
                r = pl.ds(n * 8, 8)
                cin = splat[rows8(t), pl.ds(n * 128, 128)]
                cout = splat[rows8(t), pl.ds((STATE + n) * 128, 128)]
                acc = None
                for i in range(tiles):
                    rate = rate_ref[r, at[i]]
                    j = len(ng)
                    a = jnp.exp2(d[i] * rate)
                    g = gs[j] + cout * s[i]
                    ga = g * a
                    ng.append(ga)
                    th = ga * hist_ref[0, t, r, at[i]]
                    da[i] = th * rate if n == 0 else da[i] + th * rate
                    cs[i] = cin * g if n == 0 else cs[i] + cin * g
                    acc = g * w[i] if i == 0 else acc + g * w[i]
                    nr.append(rs[j] + th * d[i])
                acc_in[rows8(t), pl.ds(n * 128, 128)] = acc
            for i in range(tiles):
                a_ref[t, :, at[i]] = da[i]
                s_ref[t, :, at[i]] = cs[i]
            return tuple(ng), tuple(nr)

        gs, rs = lax.fori_loop(0, tc, backward, init, unroll=tc)
        for j, (n, i) in enumerate(pairs):
            g_scr[pl.ds(n * 8, 8), at[i]] = gs[j]
            rs_ref[0, pl.ds(n * 8, 8), at[i]] = rs[j]
    sums = jnp.dot(acc_in[...].astype(BF16), fold_ref[0], preferred_element_type=F32)
    dc_ref[...] = sums.reshape(tc, 8, 128) + dout_ref[...]


def scan_backward(delta, w, ds, coef, rate, fan, fold, hist, dout, g_in, tc=STEPS, vmem=56 * 2**20):
    tokens, members, cd = delta.shape
    sg, nch = members // 8, tokens // tc
    rows = STATE * 8
    tok = lambda width: pl.BlockSpec((tc, 8, width), lambda s, c: (nch - 1 - c, s, 0))
    keep = lambda r: pl.BlockSpec((1, r, cd), lambda s, c: (s, 0, 0))
    whole = lambda a: pl.BlockSpec(a.shape, lambda s, c: (0,) * a.ndim)
    return pl.pallas_call(
        functools.partial(backward_kernel, cd, tc),
        grid=(sg, nch),
        in_specs=[tok(cd), tok(cd), tok(cd), tok(128), whole(rate), whole(fan), whole(fold),
                  pl.BlockSpec((1, tc, rows, cd), lambda s, c: (s, nch - 1 - c, 0, 0)), tok(128), keep(rows)],
        out_specs=[tok(cd), tok(cd), tok(128), keep(rows)],
        out_shape=[jax.ShapeDtypeStruct(delta.shape, F32)] * 2 + [jax.ShapeDtypeStruct((tokens, members, 128), F32), jax.ShapeDtypeStruct((sg, rows, cd), F32)],
        scratch_shapes=[pltpu.VMEM((rows, cd), F32), pltpu.VMEM((tc * 8, 2 * STATE * 128), F32), pltpu.VMEM((tc * 8, STATE * 128), F32)],
        compiler_params=pltpu.CompilerParams(vmem_limit_bytes=vmem),
        cost_estimate=pl.CostEstimate(flops=45 * 10**9, bytes_accessed=90 * 10**6, transcendentals=0),
        name="scan_backward",
    )(delta, w, ds, coef, rate, fan, fold, hist, dout, g_in)


def rounded(value):
    return lax.reduce_precision(value, 8, 7)


def silu_slope(value):
    sigma = jax.nn.sigmoid(value)
    return sigma * (1.0 + value * (1.0 - sigma))


def contract_rows(left, right):
    return lax.dot_general(left, right, (((0,), (0,)), ((), ())), preferred_element_type=F32)


def contract_cols(left, right):
    return lax.dot_general(left, right, (((1,), (1,)), ((), ())), preferred_element_type=F32)


def dot(left, right):
    return jnp.dot(left, right, preferred_element_type=F32)


def along_z(grid, value, d):
    ctx = grid.ctx
    return lax.ppermute(value, "ctx", [(c, (c + 4 * d) % ctx) for c in range(ctx)])


def swap(grid, value, bit):
    return lax.ppermute(value, "ctx", [(c, c ^ bit) for c in range(grid.ctx)])


def spread_tables():
    fan = np.zeros((128, 2 * STATE * 128), np.float32)
    for k in range(2 * STATE):
        fan[k, k * 128:(k + 1) * 128] = 1
        fan[2 * STATE + k, k * 128:(k + 1) * 128] = 1
    fold = np.zeros((2, STATE * 128, 128), np.float32)
    for n in range(STATE):
        fold[0, n * 128:(n + 1) * 128, n] = 1
        fold[1, n * 128:(n + 1) * 128, STATE + n] = 1
    return jnp.asarray(fan, BF16), jnp.asarray(fold, BF16)


def shards(grid, hidden_in, norm_gain, in_proj, conv_weight, conv_bias, state_proj, delta_proj, delta_bias,
           decay_log, skip_gain, out_proj, cotangent):
    F, C, Z = grid.fsdp, grid.members, grid.planes
    tokens = hidden_in.shape[1]
    rows = in_proj.shape[0]
    block = out_proj.shape[0]
    chans = Z * block
    z, q, f = grid.here()

    hidden_low = hidden_in.reshape(tokens, D)
    cot_rows = cotangent.reshape(tokens, D)
    gain_rows = rounded(norm_gain)
    lin = z * C + q * F + f
    slots = 128 // rows
    gain_tile = jnp.where(lax.broadcasted_iota(jnp.int32, (slots, 1), 0) == lin % slots, gain_rows[None, :], 0.0).reshape(1, 128)
    gain_tile = jnp.broadcast_to(gain_tile, (8, 128))
    out_low = out_proj.astype(BF16)
    in_low = rounded(in_proj).astype(BF16)
    wi = in_low.reshape(rows, 2, Z, C, block).transpose(3, 0, 1, 2, 4).reshape(C, rows, 2 * chans)
    small = jnp.concatenate(
        [conv_weight, conv_bias[None], delta_bias[None], skip_gain[None], decay_log, jnp.zeros((9, block), F32), delta_proj, state_proj.T], axis=0
    ).astype(BF16)
    normed_all, cot_all, wi_all, small_all, gains = gather_all(grid, hidden_low, gain_tile, cot_rows, wi, small)
    gains = gains[0]
    count = C * tokens
    normed_all = normed_all.reshape(count, D)
    cot_all = cot_all.reshape(count, D)
    w_in = wi_all.reshape(D, 2 * chans)
    small_all = small_all.transpose(1, 0, 2).reshape(small.shape[0], chans)
    taps = small_all[:KW].astype(F32)
    conv_shift = small_all[KW].astype(F32)
    delta_shift = small_all[KW + 1].astype(F32)
    skip = small_all[KW + 2].astype(F32)
    decay_rate = -jnp.exp(small_all[KW + 3:KW + 3 + STATE].astype(F32))
    w_delta = small_all[32:32 + DT_RANK]
    w_state = small_all[32 + DT_RANK:]
    rate8 = jnp.repeat(decay_rate * LOG2E, 8, axis=0)

    def by_step(value):
        return value.reshape(C, tokens, -1).transpose(1, 0, 2)

    def by_member(value):
        return value.transpose(1, 0, 2).reshape(count, -1)

    mixed = by_step(dot(normed_all, w_in).astype(BF16))
    conv_in = mixed[:, :, :chans]
    gate = mixed[:, :, chans:].astype(F32)
    edge_rows = -(-(KW - 1) * F // 16) * 16
    tail = conv_in[tokens - (KW - 1):, C - F:].reshape((KW - 1) * F, chans)
    tails = line_gather(grid, [jnp.pad(tail, ((0, edge_rows - (KW - 1) * F), (0, 0)))], 3, "conv_edges")[0]
    out_low, tails = lax.optimization_barrier((out_low, tails))
    w_out = [out_low] + [along_z(grid, out_low, d) for d in range(1, Z)]
    before = lax.dynamic_index_in_dim(tails, jnp.maximum(z - 1, 0), 0, False)[: (KW - 1) * F]
    before = jnp.where(z > 0, before, jnp.zeros_like(before)).reshape(KW - 1, F, chans)
    edge = jnp.concatenate([before, conv_in[tokens - (KW - 1):, : C - F]], axis=1)
    padded = jnp.concatenate([edge, conv_in], axis=0).astype(F32)
    conv_out = jnp.broadcast_to(conv_shift, (tokens, C, chans))
    for k in range(KW):
        conv_out = conv_out + taps[k] * padded[k:k + tokens]
    act = rounded(jax.nn.silu(conv_out))
    act_rows = lax.optimization_barrier(act.astype(BF16).reshape(count, chans))
    pad_lanes = 256 - DT_RANK - 2 * STATE
    selected = contract_cols(act_rows, jnp.pad(w_state, ((0, pad_lanes), (0, 0))))
    selected, *w_out = lax.optimization_barrier((plane_sum(grid, selected, 4), *w_out))
    delta_in = selected[:, :DT_RANK]
    coef = selected[:, DT_RANK:].reshape(tokens, C, 128)
    delta_pre = (dot(delta_in, w_delta) + delta_shift).reshape(tokens, C, chans)
    delta = jax.nn.softplus(delta_pre)
    drive = delta * act
    gate_act = jax.nn.silu(gate)
    w_out = in_place_order(grid, w_out).reshape(chans, D)
    d_gated = lax.optimization_barrier(by_step(contract_cols(cot_all, w_out)))
    d_scanned = d_gated * gate_act

    fan, fold = spread_tables()
    ends, adjoints, totals = scan_ends(delta, drive, d_scanned, coef, rate8, fan)
    def by_segment(value):
        groups = C // 8
        value = value.reshape(groups, -1, 8, chans).transpose(0, 2, 1, 3)
        return value.reshape(4, F, -1, chans)

    def by_sublane(value):
        return value.reshape(C // 8, 8, STATE, chans).transpose(0, 2, 1, 3).reshape(C // 8, STATE * 8, chans)

    totals = by_segment(totals)
    kept, ends, adjoints = jnp.exp(decay_rate * totals), by_segment(ends), by_segment(adjoints)
    end = ends[0]
    for c in range(1, 4):
        end = kept[c] * end + ends[c]
    adj = adjoints[3]
    for c in reversed(range(3)):
        adj = kept[c] * adj + adjoints[c]
    flat = [end.reshape(F * STATE, chans), adj.reshape(F * STATE, chans), jnp.broadcast_to(jnp.sum(totals, axis=0), (F, 8, chans)).reshape(F * 8, chans)]
    all_end, all_adj, all_tot = line_gather(grid, flat, 5, "segment_states")
    plane_kept = jnp.exp(decay_rate * all_tot.reshape(Z, F, 8, chans)[:, :, :1])
    all_end, all_adj = all_end.reshape(Z, F, STATE, chans), all_adj.reshape(Z, F, STATE, chans)
    state = jnp.zeros((F, STATE, chans), F32)
    adj = state
    for p in range(Z - 1):
        state = jnp.where(p < z, plane_kept[p] * state + all_end[p], state)
    for p in reversed(range(1, Z)):
        adj = jnp.where(p > z, plane_kept[p] * adj + all_adj[p], adj)
    before_state, after_adj = [], []
    for c in range(4):
        before_state.append(state)
        state = kept[c] * state + ends[c]
    for c in reversed(range(4)):
        after_adj.append(adj)
        adj = kept[c] * adj + adjoints[c]
    after_adj.reverse()

    y, history, d_out_coef = scan_forward(delta, drive, d_scanned, coef, rate8, fan, fold, by_sublane(jnp.stack(before_state)))
    scanned = y + skip * act
    gated = (scanned * gate_act).astype(BF16)
    d_gate = d_gated * scanned * silu_slope(gate)
    gated, d_gate = lax.optimization_barrier((gated, d_gate.astype(BF16)))
    gated, d_gate = by_member(gated), by_member(d_gate)
    half = D // 2
    core = q % 2
    w_out_mine = lax.dynamic_slice_in_dim(w_out, core * half, half, 1)
    w_out_twin = lax.dynamic_slice_in_dim(w_out, (1 - core) * half, half, 1)

    def sent_along_z(part):
        pick = lambda d: lax.dynamic_index_in_dim(part, (z + d) % Z, 0, False)
        return [pick(0)] + [along_z(grid, pick(d), d) for d in range(1, Z)]

    def total(parts):
        return functools.reduce(lambda t, v: t + v.astype(F32), parts[1:], parts[0].astype(F32))

    def twin_summed(mine, twin_part):
        return (mine + swap(grid, twin_part, 1).astype(F32)).astype(BF16).reshape(4, F, tokens, half)

    def other_sequences(total):
        pieces = [lax.dynamic_index_in_dim(total, (f + d) % F, 1, False) for d in range(F)]
        return pieces[:1] + [lax.ppermute(pieces[d], "fsdp", [(g, (g + d) % F) for g in range(F)]) for d in range(1, F)]

    def own_tokens(own):
        own = own.reshape(2, 2, tokens, half)
        keep = lax.dynamic_index_in_dim(own, q // 2, 0, False)
        give = lax.dynamic_index_in_dim(own, 1 - q // 2, 0, False).astype(BF16)
        keep = keep + swap(grid, give, 2).astype(F32)
        final = lax.dynamic_index_in_dim(keep, core, 0, False)
        give = lax.dynamic_index_in_dim(keep, 1 - core, 0, False).astype(BF16)
        return final, swap(grid, give, 1)

    twin_part = dot(gated, w_out_twin).astype(BF16)
    out_part = contract_rows(gated, cot_all).astype(BF16).reshape(Z, block, D)
    gate_part = contract_rows(normed_all, d_gate).astype(BF16).reshape(Z, C * rows, chans)
    out_part, gate_part, chip_out = lax.optimization_barrier((out_part, gate_part, twin_summed(dot(gated, w_out_mine), twin_part)))
    sent_out, sent_gate, sent_tokens = sent_along_z(out_part), sent_along_z(gate_part), other_sequences(chip_out)
    history, _ = lax.optimization_barrier((history, (out_part, gate_part, chip_out)))
    swept = scan_backward(delta, drive, d_scanned, coef, rate8, fan, fold, history, d_out_coef, by_sublane(jnp.stack(after_adj)))
    near = [d for d in range(1, Z) if d != 2]
    (d_delta_a, coef_sum, d_coef, rate_sum), arrived_out, arrived_gate, sent_tokens = lax.optimization_barrier(
        (swept, [sent_out[d] for d in near], [sent_gate[d] for d in near], sent_tokens)
    )
    mixer_own, mixer_twin = own_tokens(total(sent_tokens))
    decay_grad = rate_sum.reshape(C // 8, STATE, 8, chans).sum(axis=(0, 2)) * decay_rate
    skip_grad = jnp.sum(d_scanned * act, axis=(0, 1))
    d_delta_pre = (d_delta_a * (1.0 / LOG2E) + act * coef_sum) * jax.nn.sigmoid(delta_pre)
    shift_grad = jnp.sum(d_delta_pre, axis=(0, 1))
    d_delta_low = d_delta_pre.astype(BF16).reshape(count, chans)
    dproj_grad = contract_rows(delta_in, d_delta_low)
    d_delta_in = contract_cols(d_delta_low, w_delta)
    partial = jnp.concatenate([d_delta_in, d_coef.reshape(count, 128)], axis=1)
    d_selected, far_out = lax.optimization_barrier((plane_sum(grid, partial, 6), sent_out[2]))
    d_selected = d_selected[:, :DT_RANK + 2 * STATE]
    sproj_grad = contract_rows(d_selected, act_rows)
    d_activated = delta * coef_sum + skip * d_scanned + dot(d_selected, w_state).reshape(tokens, C, chans)
    d_conv = d_activated * silu_slope(conv_out)
    cbias_grad = jnp.sum(d_conv, axis=(0, 1))
    kernel_grad = jnp.stack([jnp.sum(d_conv * padded[k:k + tokens], axis=(0, 1)) for k in range(KW)])
    head = d_conv[:KW - 1, :F].reshape((KW - 1) * F, chans)
    head_rows = -(-(KW - 1) * F // 8) * 8
    heads = line_gather(grid, [jnp.pad(head, ((0, head_rows - (KW - 1) * F), (0, 0)))], 7, "conv_grad_edges")[0]
    after = lax.dynamic_index_in_dim(heads, jnp.minimum(z + 1, Z - 1), 0, False)[: (KW - 1) * F]
    after = jnp.where(z < Z - 1, after, jnp.zeros_like(after)).reshape(KW - 1, F, chans)
    edge_grad = jnp.concatenate([d_conv[:KW - 1, F:], after], axis=1)
    grad_padded = jnp.concatenate([d_conv, edge_grad], axis=0)
    d_conv_in = jnp.zeros((tokens, C, chans), F32)
    for k in range(KW):
        d_conv_in = d_conv_in + taps[k] * grad_padded[KW - 1 - k:KW - 1 - k + tokens]
    d_conv_in, far_gate, mixer_own, mixer_twin = lax.optimization_barrier((d_conv_in.astype(BF16), sent_gate[2], mixer_own, mixer_twin))
    d_conv_in = by_member(d_conv_in)
    out_grad = total([sent_out[0], far_out] + arrived_out)
    gate_sum = total([sent_gate[0], far_gate] + arrived_gate).astype(BF16).reshape(C, rows, chans)
    mixer_twin = mixer_twin.astype(F32)
    mixer_out = jnp.where(core == 0, jnp.concatenate([mixer_own, mixer_twin], 1), jnp.concatenate([mixer_twin, mixer_own], 1))
    d_mixed = jnp.concatenate([d_conv_in, d_gate], axis=1)
    w_in_mine = lax.dynamic_slice_in_dim(w_in, core * half, half, 0)
    w_in_twin = lax.dynamic_slice_in_dim(w_in, (1 - core) * half, half, 0)
    from_twin = swap(grid, contract_cols(d_mixed, w_in_twin).astype(BF16), 1)
    conv_part = contract_rows(normed_all, d_conv_in).astype(BF16).reshape(Z, C, rows, chans)
    part_in = (contract_cols(d_mixed, w_in_mine) + from_twin.astype(F32)).astype(BF16).reshape(C, tokens, half)

    fine = jnp.concatenate([kernel_grad, cbias_grad[None], shift_grad[None], skip_grad[None], decay_grad, jnp.zeros((9, chans), F32)], axis=0)
    fine = fine.reshape(32, Z, block).transpose(1, 0, 2)
    coarse = jnp.concatenate([dproj_grad, sproj_grad], axis=0).astype(BF16)
    coarse = coarse.reshape(-1, Z, block).transpose(1, 0, 2)
    got = to_owners(grid, conv_part, [gate_sum, part_in], [coarse, fine], 9)
    in_grad = jnp.stack([got[0], got[1]], axis=0).reshape(2, C, rows, Z, block).transpose(2, 0, 3, 1, 4)
    in_grad = in_grad.reshape(rows, 2 * DI).astype(F32)
    d_normed = got[2].astype(F32).reshape(2, 2, F, tokens, half).sum(axis=(0, 2))
    d_unit = jnp.concatenate([d_normed[0], d_normed[1]], axis=1) * gains[None, :]
    hidden = hidden_low.astype(F32)
    inv_rms = lax.rsqrt(jnp.mean(hidden * hidden, axis=1, keepdims=True) + EPS)
    unit = hidden * inv_rms
    block_out = (hidden + mixer_out).astype(BF16)
    coarse = got[3].astype(F32).sum(axis=0)
    fine = got[4].sum(axis=0)
    gain_grad = jnp.sum(rounded(in_proj) * in_grad, axis=1) / gain_rows
    mean_term = jnp.mean(d_unit * unit, axis=1, keepdims=True)
    input_grad = (cot_rows.astype(F32) + inv_rms * (d_unit - unit * mean_term)).astype(BF16)
    return (
        block_out.reshape(1, tokens, D),
        input_grad.reshape(1, tokens, D),
        gain_grad,
        in_grad,
        fine[:KW],
        fine[KW],
        coarse[DT_RANK:].T,
        coarse[:DT_RANK],
        fine[KW + 1],
        fine[KW + 3:KW + 3 + STATE],
        fine[KW + 2],
        out_grad,
    )


def solution(mesh):
    grid = Grid(mesh.shape["ctx"], mesh.shape["fsdp"])
    both = ("ctx", "fsdp")
    tokens, flat, by_row, by_col = P("fsdp", "ctx", None), P(both), P(both, None), P(None, both)
    in_specs = (tokens, flat, by_row, by_col, flat, by_row, by_col, flat, by_col, flat, by_row, tokens)
    out_specs = (tokens, tokens, flat, by_row, by_col, flat, by_row, by_col, flat, by_col, flat, by_row)
    return jax.shard_map(functools.partial(shards, grid), mesh=mesh, in_specs=in_specs, out_specs=out_specs, check_vma=False)
```

time: 761 us -> 609 us (0.80)
  Pallas kernels: 518 us -> 352 us
  starting transfers between devices: 0 us -> 15.6 us
  matrix products: 109 us -> 96.6 us
  waiting for transfers between devices: 0 us -> 10.6 us
    pallas_call x9 -> x7, Pallas kernels: 431 us -> 247 us  [comm_call(): pl.pallas_call(kernel, in_specs=spaces, out_specs=[pl.BlockSpec(memory_sp...]
    pallas_call x1 -> x3, Pallas kernels: 62.2 us -> 79.5 us  [the longest x1 45.1 us: scan_backward(): pl.pallas_call(functools.partial(backward_kernel, cd, tc), grid=(sg, nch)...]
    ppermute x0 -> x14, starting transfers between devices: none -> 15.6 us  [the longest x9 12.5 us: along_z(): lax.ppermute(value, 'ctx', [(c, (c + 4 * d) % ctx) for c in range(ctx)])]
    ppermute x0 -> x14, waiting for transfers between devices: none -> 10.6 us  [the longest x4 10.6 us: swap(): return lax.ppermute(value, 'ctx', [(c, c ^ bit) for c in range(grid.ctx)])]
    reshape x1 -> x0, local copies, waits for them, and re-layouts: 9.16 us -> none  [shards(): in_grad = got[0].astype(F32).reshape(Z, C, rows, 2, Z, block).sum(axis=0)]
    dot_general x5, matrix products: 39 us -> 31.2 us  [dot(): return jnp.dot(left, right, preferred_element_type=F32)]
    reduce_sum x7 -> x4, other arithmetic: 17.6 us -> 10.7 us  [the longest x1 6.04 us: shards(): shift_grad = jnp.sum(d_delta_pre, axis=(0, 1))]
    dot_general x4 -> x5, matrix products: 39.4 us -> 34.9 us  [contract_rows(): lax.dot_general(left, right, (((0,), (0,)), ((), ())), preferred_element_...]
  transfers between devices with their start and end apart: 0 -> 14, of which waited for: 0 -> 1; matrix products, arithmetic and copies ran while one was open for 0% -> 16% of each run, Pallas kernels for 0% -> 18%
where the time goes in v2:
time: 609 us; the launch traced here: 601 us
  Pallas kernels  352 us (58%)
  matrix products  96.6 us (16%)
  local copies, waits for them, and re-layouts  62.4 us (10%)
  other arithmetic  61.1 us (10%)
  starting transfers between devices  15.6 us (3%)
  waiting for transfers between devices  10.6 us (2%)
    pallas_call x7, Pallas kernels, comm_call(): pl.pallas_call(kernel, in_specs=spaces, out_specs=[pl.BlockSpec(memory_sp...  247 us
    pallas_call x1, Pallas kernels, scan_backward(): pl.pallas_call(functools.partial(backward_kernel, cd, tc), grid=(sg, nch)...  45.1 us
    dot_general x5, matrix products, contract_rows(): lax.dot_general(left, right, (((0,), (0,)), ((), ())), preferred_element_...  34.9 us
    pallas_call x1, Pallas kernels, scan_forward(): pl.pallas_call(functools.partial(forward_kernel, cd, tc), grid=(sg, nch),...  32.3 us
    dot_general x5, matrix products, dot(): return jnp.dot(left, right, preferred_element_type=F32)  31.2 us
    dot_general x5, matrix products, contract_cols(): lax.dot_general(left, right, (((1,), (1,)), ((), ())), preferred_element_...  30.5 us
    pallas_call x1, Pallas kernels, scan_ends(): pl.pallas_call(functools.partial(ends_kernel, cd, tc), grid=(sg, nch), in...  25.1 us
    unnamed x168, local copies, waits for them, and re-layouts  20.8 us
  transfers between devices with their start and end apart: 14, of which 1 were waited for; matrix products, arithmetic and copies ran while one was open for 16% of the time, Pallas kernels for 18%

profile of v2, /device:TPU:0, one launch (start us, length us, event | category | flops | bytes accessed | tf_op | source)
XLA Modules:
  0.0 600.7 jit_solution(3675109292640067457)
XLA Ops:
  5.3 2.1 convert_element_type.197.refs_0_
  7.4 1.9 fusion.44
  9.6 1.4 copy.113
  11.0 1.8 reshape.488.wi_ref
  13.1 95.2 %gather_weights_and_tokens.1 = (bf16[8,256,2048]{2,1,0:T(8,128)(2,1)S(1)}, bf16[8,256,2048]{2,1,0:T(8,128)(2,1)S(1)}, bf16[32,64,1024]{2,1,0:T(8,128)(2,1)S(1)},...) custom-call(bf16[256,2048]{1,0:T(8,128)(2,1)S(1)} %bitcast.294, f32[8,128]{1,0:T(8,128)S(1)} %broadcast_in_dim.77.g_ref, ...), custom_call_target="tpu_custom_call" | custom-call | tf_op jit(solution)/shard_map/gather_weights_and_tokens/pallas_call | solution.py:57
  108.3 3.3 copy-done.14
  111.6 9.1 %convolution_convert_fusion.1 = bf16[2048,1024]{1,0:T(8,128)(2,1)S(1)} fusion(bf16[2048,2048]{1,0:T(8,128)(2,1)S(1)} %bitcast.318, bf16[2048,1024]{1,0:T(8,128)(2,1)S(1)} %bitcast.321), kind=kOutput, calls=%fused_computation.55 | convolution fusion | flops 8592031744 | bytes 16777216 | tf_op jit(solution)/shard_map/dot_general | solution.py:713
  120.8 2.3 copy.112
  123.1 2.0 copy-done.25
  125.1 5.7 conv_edges.1
  130.8 1.5 collective-permute-start.2
  135.2 1.3 slice.311
  136.5 1.7 slice.312
  138.8 1.6 copy.118
  140.5 1.3 maximum_convert_fusion
  141.9 4.8 convert_bitcast_fusion.1
  149.5 1.7 copy.46
  151.2 1.7 copy.44
  152.8 1.6 reshape.536
  154.5 29.6 %plane_sum.2 = bf16[8,256,256]{2,1,0:T(8,128)(2,1)S(1)} custom-call(f32[2048,256]{1,0:T(8,128)S(1)} %fusion.68.part_ref), custom_call_target="tpu_custom_call" | custom-call | tf_op jit(solution)/shard_map/plane_sum/pallas_call | solution.py:57
  186.3 1.7 copy.45
  188.0 2.1 in_place_order.1
  190.1 16.1 %fusion.26 = f32[256,8,512]{2,1,0:T(8,128)} fusion(bf16[512,2048,1]{1,0,2:T(8,128)(2,1)S(1)} %bitcast.301, bf16[8,256,2048]{2,1,0:T(8,128)(2,1)} %copy-done.14), kind=kOutput, calls=%fused_computation.62 | convolution fusion | flops 4294967296 | bytes 14680064 | tf_op jit(solution)/shard_map/dot_general | solution.py:709
  206.3 10.3 %fusion.89 = (f32[256,8,512]{2,1,0:T(8,128)}, f32[256,8,512]{2,1,0:T(8,128)}, f32[512]{0:T(512)}, f32[256,8,512]{2,1,0:T(8,128)}, f32[2048,512]{1,0:T(8,128)}) fusion(f32[256,8,512]{2,1,0:T(8,128)S(1)} %copy-done.19, f32[512]{0:T(512)S(1)} %bitcast.392, f32[256,8,512]{2,1,0:T(8,128)} %fusion.26, bf16[256,8,1024]{2,1,0:T(8,128)(2,1)S(1)} %bitcast.329, ...), kind=kOutput, calls=%fused_computation.209 | convolution fusion | flops 290455040 | bytes 27922432 | tf_op jit(solution)/shard_map/dot_general | solution.py:713
  216.6 25.1 %segment_ends.1 = (f32[1,128,512]{2,1,0:T(8,128)S(1)}, f32[1,128,512]{2,1,0:T(8,128)S(1)}, f32[1,8,512]{2,1,0:T(8,128)S(1)}) custom-call(f32[256,8,512]{2,1,0:T(8,128)} %get-tuple-element.136.delta_ref, f32[256,8,512]{2,1,0:T(8,128)} %get-tuple-element.135.w_ref, f32[256,8,512]{2,1,0:T(8,128)} %get-tuple-element.145.ds_ref, ...), custom_call_target="tpu_custom_call" | custom-call | tf_op jit(solution)/shard_map/segment_ends/pallas_call | solution.py:540
  242.3 18.3 %segment_states.1 = (f32[4,32,512]{2,1,0:T(8,128)S(1)}, f32[4,32,512]{2,1,0:T(8,128)S(1)}, f32[4,16,512]{2,1,0:T(8,128)S(1)}) custom-call(f32[32,512]{1,0:T(8,128)S(1)} %get-tuple-element.182.refs_0_, f32[32,512]{1,0:T(8,128)S(1)} %get-tuple-element.181.refs_1_, f32[16,512]{1,0:T(8,128)S(1)} %broadcast_bitcast_fusion.1.refs_2_), custom_call_target="tpu_custom_call" | custom-call | tf_op jit(solution)/shard_map/segment_states/pallas_call | solution.py:57
  261.7 32.3 %scan_forward.1 = (f32[256,8,512]{2,1,0:T(8,128)}, f32[1,256,128,512]{3,2,1,0:T(8,128)}, f32[256,8,128]{2,1,0:T(8,128)}) custom-call(f32[256,8,512]{2,1,0:T(8,128)} %get-tuple-element.136.delta_ref, f32[256,8,512]{2,1,0:T(8,128)} %get-tuple-element.135.w_ref, f32[256,8,512]{2,1,0:T(8,128)} %get-tuple-element.145.ds_ref, bf16[256,8,128]{2,1,0:T(8,128)(2,1)} %copy-done.5, ...), custom_call_target="tpu_custom_call" | custom-call | flops 30000001024 | bytes 90000000 | tf_op jit(solution)/shard_map/scan_forward/pallas_call | solution.py:604
  294.0 5.8 fusion.10
  301.8 4.3 convolution_convert_fusion
  306.2 15.0 %bitcast_convert_fusion.2 = bf16[512,2048]{1,0:T(8,128)(2,1)S(1)} fusion(bf16[8,256,2048]{2,1,0:T(8,128)(2,1)} %copy-done.14, bf16[256,8,512]{2,1,0:T(8,128)(2,1)S(1)} %get-tuple-element.82), kind=kOutput, calls=%fused_computation.29 | convolution fusion | flops 4296015872 | bytes 12582912 | tf_op jit(solution)/shard_map/dot_general | solution.py:705
  322.5 2.0 copy.54
  324.5 5.8 bitcast_convert_fusion.1
  330.4 5.4 add_convert_fusion.1
  338.1 2.7 collective-permute-start.5
  340.8 3.8 collective-permute-start.7
  344.6 1.8 dynamic-slice_bitcast_fusion
  347.1 45.1 %scan_backward.1 = (f32[256,8,512]{2,1,0:T(8,128)}, f32[256,8,512]{2,1,0:T(8,128)}, f32[256,8,128]{2,1,0:T(8,128)}, f32[1,128,512]{2,1,0:T(8,128)}) custom-call(f32[256,8,512]{2,1,0:T(8,128)} %get-tuple-element.136.delta_ref, f32[256,8,512]{2,1,0:T(8,128)} %get-tuple-element.135.w_ref, f32[256,8,512]{2,1,0:T(8,128)} %get-tuple-element.145.ds_ref, ...), custom_call_target="tpu_custom_call" | custom-call | flops 44999999488 | bytes 90000000 | tf_op jit(solution)/shard_map/scan_backward/pallas_call | solution.py:681
  392.9 2.4 collective-permute-start.10
  395.3 6.0 %fusion.91 = (f32[512]{0:T(512)S(1)}, bf16[256,8,512]{2,1,0:T(8,128)(2,1)S(1)}) fusion(f32[2048,512]{1,0:T(8,128)} %get-tuple-element.190, f32[512]{0:T(512)S(1)} %bitcast.393, f32[256,8,512]{2,1,0:T(8,128)} %get-tuple-element.94, f32[256,8,512]{2,1,0:T(8,128)S(1)} %copy-done.21, f32[256,8,512]{2,1,0:T(8,128)} %get-tuple-element.95), kind=kLoop, calls=%fused_computation.210 | loop fusion | flops 15728128 | bytes 18878464 | tf_op jit(solution)/shard_map/reduce_sum | solution.py:897
  402.8 29.3 %plane_sum.3 = bf16[8,256,256]{2,1,0:T(8,128)(2,1)S(1)} custom-call(f32[2048,256]{1,0:T(8,128)S(1)} %pad_maximum_fusion.5.part_ref), custom_call_target="tpu_custom_call" | custom-call | tf_op jit(solution)/shard_map/plane_sum/pallas_call | solution.py:57
  433.0 2.7 convert_add_fusion
  435.8 1.8 copy-done.28
  437.6 1.7 collective-permute-start.11
  439.3 2.1 multiply_multiply_fusion
  441.4 2.1 copy-done.23
  443.6 6.4 %conv_grad_edges.1 = f32[4,8,512]{2,1,0:T(8,128)S(1)} custom-call(f32[8,512]{1,0:T(8,128)S(1)} %pad.14.refs_0_), custom_call_target="tpu_custom_call" | custom-call | tf_op jit(solution)/shard_map/conv_grad_edges/pallas_call | solution.py:57
  450.1 2.8 maximum_maximum_fusion
  452.9 10.6 %collective-permute-done.11 = bf16[2,256,1024]{2,1,0:T(8,128)(2,1)} collective-permute-done((bf16[2,256,1024]{2,1,0:T(8,128)(2,1)S(1)}, bf16[2,256,1024]{2,1,0:T(8,128)(2,1)}, u32[]{:S(2)}, u32[]{:S(2)}) %collective-permute-start.11) | collective-permute-done | bytes 1048608 | tf_op jit(solution)/shard_map/ppermute | solution.py:722
  463.5 1.7 bitcast_add_fusion
  465.4 7.7 %multiply_reduce_fusion.1 = (f32[512]{0:T(512)S(1)}, f32[512]{0:T(512)S(1)}, f32[512]{0:T(512)S(1)}, f32[512]{0:T(512)S(1)}, f32[512]{0:T(512)S(1)}, /*index=5*/bf16[256,8,512]{2,1,0:T(8,128)(2,1)S(1)}) fusion(f32[256,8,512]{2,1,0:T(8,128)S(1)} %copy-done.24, f32[259,8,512]{2,1,0:T(8,128)} %copy-done.18, f32[512]{0:T(512)S(1)} %bitcast.379, ...), kind=kLoop, calls=%fused_computation.43 | loop fusion | flops 17823232 | bytes 35670016 | tf_op jit(solution)/shard_map/reduce_sum | solution.py:908
  474.9 2.5 copy-done.16
  478.1 6.4 %convolution_convert_fusion.2 = bf16[2048,1024]{1,0:T(8,128)(2,1)} fusion(bf16[2048,512]{1,0:T(8,128)(2,1)S(1)} %bitcast.346, bf16[2048,512]{1,0:T(8,128)(2,1)S(1)} %bitcast.350, bf16[2048,1024]{1,0:T(8,128)(2,1)S(1)} %bitcast.322, s32[]{:T(128)S(6)} %select_n.242), kind=kOutput, calls=%fused_computation.56 | convolution fusion | flops 4305453056 | bytes 10485764 | tf_op jit(solution)/shard_map/dot_general | solution.py:709
  486.2 2.2 fusion.43
  488.5 4.0 copy.64
  493.7 2.4 convolution_convert_fusion.4
  496.1 3.0 fusion.47
  500.2 1.8 fusion.50
  502.0 9.5 %bitcast_convert_fusion = bf16[2048,512]{1,0:T(8,128)(2,1)S(1)} fusion(bf16[8,256,2048]{2,1,0:T(8,128)(2,1)} %copy-done.13, bf16[8,256,512]{2,0,1:T(8,128)(2,1)S(1)} %bitcast.333), kind=kOutput, calls=%fused_computation.27 | convolution fusion | flops 4296015872 | bytes 12582912 | tf_op jit(solution)/shard_map/dot_general | solution.py:705
  511.5 6.6 %add_convert_fusion = bf16[2048,1024]{1,0:T(8,128)(2,1)S(1)} fusion(bf16[2048,1024]{1,0:T(8,128)(2,1)} %collective-permute-done.13, bf16[2048,512]{1,0:T(8,128)(2,1)S(1)} %bitcast.347, bf16[2048,512]{1,0:T(8,128)(2,1)S(1)} %bitcast.351, bf16[2048,1024]{1,0:T(8,128)(2,1)S(1)} %bitcast.323, s32[]{:T(128)S(6)} %select_n.241), kind=kOutput, calls=%fused_computation.2 | convolution fusion | flops 4309647360 | bytes 14680068 | tf_op jit(solution)/shard_map/dot_general | solution.py:709
  518.1 62.6 %to_owners.1 = (bf16[8,64,512]{2,1,0:T(8,128)(2,1)S(1)}, bf16[8,64,512]{2,1,0:T(8,128)(2,1)S(1)}, bf16[8,256,1024]{2,1,0:T(8,128)(2,1)S(1)}, bf16[4,288,128]{2,1,0:T(8,128)(2,1)S(1)}, f32[4,32,128]{2,1,0:T(8,128)S(1)}) custom-call(bf16[4,8,64,512]{3,2,1,0:T(8,128)(2,1)S(1)} %bitcast.300, bf16[8,64,512]{2,1,0:T(8,128)(2,1)S(1)} %bitcast.304, ...), custom_call_target="tpu_custom_call" | custom-call | tf_op jit(solution)/shard_map/to_owners/pallas_call | solution.py:57
  580.8 2.0 copy-done.2
  585.8 4.7 convert_reduce_fusion
  592.7 2.9 multiply_reduce_fusion.5
  597.9 2.3 fusion.34
  (273 shorter events, 38.8 us)
Async XLA Ops:
  111.6 9.1 %copy-start.12 = (f32[8,2048]{1,0:T(8,128)}, f32[8,2048]{1,0:T(8,128)S(1)}, u32[]{:S(2)}) copy-start(f32[8,2048]{1,0:T(8,128)S(1)} %get-tuple-element.108) | copy-start | bytes 196612
  111.6 9.1 %copy-start.13 = (bf16[8,256,2048]{2,1,0:T(8,128)(2,1)}, bf16[8,256,2048]{2,1,0:T(8,128)(2,1)S(1)}, u32[]{:S(2)}) copy-start(bf16[8,256,2048]{2,1,0:T(8,128)(2,1)S(1)} %get-tuple-element.65) | copy-start | bytes 25165828
  111.6 9.1 %copy-start.15 = (bf16[32,64,1024]{2,1,0:T(8,128)(2,1)}, bf16[32,64,1024]{2,1,0:T(8,128)(2,1)S(1)}, u32[]{:S(2)}) copy-start(bf16[32,64,1024]{2,1,0:T(8,128)(2,1)S(1)} %get-tuple-element.66) | copy-start | bytes 12582916
  111.6 73.4 %copy-start.11 = (bf16[4,320,128]{2,1,0:T(8,128)(2,1)}, bf16[4,320,128]{2,1,0:T(8,128)(2,1)S(1)}, u32[]{:S(2)}) copy-start(bf16[4,320,128]{2,1,0:T(8,128)(2,1)S(1)} %get-tuple-element.64) | copy-start | bytes 983044
  130.8 54.3 %collective-permute-start.2 = (bf16[128,2048]{1,0:T(8,128)(2,1)}, bf16[128,2048]{1,0:T(8,128)(2,1)}, u32[]{:S(2)}, u32[]{:S(2)}) collective-permute-start(bf16[128,2048]{1,0:T(8,128)(2,1)} %convert_element_type.197.refs_0_), channel_id=1, source_target_pairs={{0,24},{2,26},{4,28},{6,30},{8,0},{10,2},{12,4},{14,6},{16,8},{18,... | collective-permute-start | bytes 1572872 | tf_op jit(solution)/shard_map/ppermute | solution.py:718
  132.3 52.8 %collective-permute-start.1 = (bf16[128,2048]{1,0:T(8,128)(2,1)}, bf16[128,2048]{1,0:T(8,128)(2,1)}, u32[]{:S(2)}, u32[]{:S(2)}) collective-permute-start(bf16[128,2048]{1,0:T(8,128)(2,1)} %convert_element_type.197.refs_0_), channel_id=1, source_target_pairs={{0,16},{2,18},{4,20},{6,22},{8,24},{10,26},{12,28},{14,30},{16,0},... | collective-permute-start | bytes 1572872 | tf_op jit(solution)/shard_map/ppermute | solution.py:718
  133.1 52.0 %collective-permute-start = (bf16[128,2048]{1,0:T(8,128)(2,1)}, bf16[128,2048]{1,0:T(8,128)(2,1)}, u32[]{:S(2)}, u32[]{:S(2)}) collective-permute-start(bf16[128,2048]{1,0:T(8,128)(2,1)} %convert_element_type.197.refs_0_), channel_id=1, source_target_pairs={{0,8},{2,10},{4,12},{6,14},{8,16},{10,18},{12,20},{14,22},{16,24},... | collective-permute-start | bytes 1572872 | tf_op jit(solution)/shard_map/ppermute | solution.py:718
  138.8 7.8 %copy-start.65 = (f32[1,4,128]{2,0,1:T(1,128)}, f32[1,4,128]{2,0,1:T(1,128)S(1)}, u32[]{:S(2)}) copy-start(f32[1,4,128]{2,0,1:T(1,128)S(1)} %get-tuple-element.186) | copy-start | bytes 6148
  138.8 7.8 %copy-start.67 = (f32[1,4,128]{2,0,1:T(1,128)}, f32[1,4,128]{2,0,1:T(1,128)S(1)}, u32[]{:S(2)}) copy-start(f32[1,4,128]{2,0,1:T(1,128)S(1)} %get-tuple-element.187) | copy-start | bytes 6148
  185.1 31.5 %copy-start.9 = (f32[128,512]{1,0:T(8,128)}, f32[128,512]{1,0:T(8,128)S(1)}, u32[]{:S(2)}) copy-start(f32[128,512]{1,0:T(8,128)S(1)} %broadcast_bitcast_fusion.rate_ref) | copy-start | bytes 786436
  186.3 30.3 %copy-start.5 = (bf16[256,8,128]{2,1,0:T(8,128)(2,1)}, bf16[256,8,128]{2,1,0:T(8,128)(2,1)S(1)}, u32[]{:S(2)}) copy-start(bf16[256,8,128]{2,1,0:T(8,128)(2,1)S(1)} %slice_bitcast_fusion.coef_ref) | copy-start | bytes 1572868
  188.0 18.2 %copy-start.42 = (bf16[2048,256]{0,1:T(8,128)(2,1)}, bf16[2048,256]{0,1:T(8,128)(2,1)S(1)}, u32[]{:S(2)}) copy-start(bf16[2048,256]{0,1:T(8,128)(2,1)S(1)} %copy.45) | copy-start | bytes 3145732
  190.0 16.2 %copy-start.6 = (bf16[4,128,2048]{2,1,0:T(8,128)(2,1)}, bf16[4,128,2048]{2,1,0:T(8,128)(2,1)S(1)}, u32[]{:S(2)}) copy-start(bf16[4,128,2048]{2,1,0:T(8,128)(2,1)S(1)} %in_place_order.1) | copy-start | bytes 6291460
  190.0 16.2 %copy-start.19 = (f32[256,8,512]{2,1,0:T(8,128)S(1)}, f32[256,8,512]{2,1,0:T(8,128)}, u32[]{:S(2)}) copy-start(f32[256,8,512]{2,1,0:T(8,128)} %get-tuple-element.138) | copy-start | bytes 12582916
  190.1 16.2 %copy-start.26 = (bf16[8,256,1024]{2,0,1:T(8,128)(2,1)S(1)}, bf16[8,256,1024]{2,0,1:T(8,128)(2,1)}, u32[]{:S(2)}) copy-start(bf16[8,256,1024]{2,0,1:T(8,128)(2,1)} %copy-done.25) | copy-start | bytes 12582916
  190.1 16.2 %copy-start.60 = (bf16[128,4,128]{0,2,1:T(8,128)(2,1)S(1)}, bf16[128,4,128]{0,2,1:T(8,128)(2,1)}, u32[]{:S(2)}) copy-start(bf16[128,4,128]{0,2,1:T(8,128)(2,1)} %copy.46) | copy-start | bytes 393220
  190.1 16.2 %copy-start.75 = (f32[1,4,128]{2,0,1:T(1,128)S(1)}, f32[1,4,128]{2,0,1:T(1,128)}, u32[]{:S(2)}) copy-start(f32[1,4,128]{2,0,1:T(1,128)} %get-tuple-element.161) | copy-start | bytes 6148
  206.2 10.4 %copy-start.10 = (bf16[128,4096]{1,0:T(8,128)(2,1)S(1)}, bf16[128,4096]{1,0:T(8,128)(2,1)}, u32[]{:S(2)}) copy-start(bf16[128,4096]{1,0:T(8,128)(2,1)} %constant.179.clone.fan_ref) | copy-start | bytes 3145732
  242.0 19.7 %copy-start.40 = (f32[4,2,16,512]{3,2,1,0:T(8,128)}, f32[4,2,16,512]{3,2,1,0:T(8,128)S(1)}, u32[]{:S(2)}) copy-start(f32[4,2,16,512]{3,2,1,0:T(8,128)S(1)} %multiply_exponential_fusion.1) | copy-start | bytes 786436
  242.2 19.5 %copy-start.52 = (f32[1,16,8,512]{3,1,2,0:T(8,128)}, f32[1,16,8,512]{3,1,2,0:T(8,128)S(1)}, u32[]{:S(2)}) copy-start(f32[1,16,8,512]{3,1,2,0:T(8,128)S(1)} %copy.116) | copy-start | bytes 786436
  261.7 32.3 %copy-start.20 = (f32[256,8,512]{2,1,0:T(8,128)S(1)}, f32[256,8,512]{2,1,0:T(8,128)}, u32[]{:S(2)}) copy-start(f32[256,8,512]{2,1,0:T(8,128)} %get-tuple-element.138) | copy-start | bytes 12582916
  261.7 32.3 %copy-start.73 = (f32[1,4,128]{2,0,1:T(1,128)S(1)}, f32[1,4,128]{2,0,1:T(1,128)}, u32[]{:S(2)}) copy-start(f32[1,4,128]{2,0,1:T(1,128)} %get-tuple-element.160) | copy-start | bytes 6148
  301.8 22.7 %slice-start = ((s8[8388608]{0:T(1024)(128)(4,1)}), s8[4194304]{0:T(1024)(128)(4,1)S(1)}, s32[]{:S(2)}) async-start(s8[8388608]{0:T(1024)(128)(4,1)} %bitcast.319), calls=%async_computation | async-start | bytes 8388608
  306.1 15.1 %copy-start.41 = (f32[4,2,16,512]{3,2,1,0:T(8,128)S(1)}, f32[4,2,16,512]{3,2,1,0:T(8,128)}, u32[]{:S(2)}) copy-start(f32[4,2,16,512]{3,2,1,0:T(8,128)} %copy-done.40) | copy-start | bytes 786436
  306.1 15.1 %copy-start.53 = (f32[1,16,8,512]{3,1,2,0:T(8,128)S(1)}, f32[1,16,8,512]{3,1,2,0:T(8,128)}, u32[]{:S(2)}) copy-start(f32[1,16,8,512]{3,1,2,0:T(8,128)} %copy-done.52) | copy-start | bytes 786436
  306.1 15.1 %copy-start.55 = (f32[4,2,16,512]{3,2,1,0:T(8,128)S(1)}, f32[4,2,16,512]{3,2,1,0:T(8,128)}, u32[]{:S(2)}) copy-start(f32[4,2,16,512]{3,2,1,0:T(8,128)} %copy-done.54) | copy-start | bytes 786436
  306.1 18.3 %slice-start.1 = ((s8[8388608]{0:T(1024)(128)(4,1)}), s8[4194304]{0:T(1024)(128)(4,1)S(1)}, s32[]{:S(2)}) async-start(s8[8388608]{0:T(1024)(128)(4,1)} %bitcast.319), calls=%async_computation.1 | async-start | bytes 8388608
  306.1 24.2 %collective-permute-start.3 = (bf16[2048,1024]{1,0:T(8,128)(2,1)}, bf16[2048,1024]{1,0:T(8,128)(2,1)}, u32[]{:S(2)}, u32[]{:S(2)}) collective-permute-start(bf16[2048,1024]{1,0:T(8,128)(2,1)} %convolution_convert_fusion), channel_id=1, source_target_pairs={{0,2},{2,0},{4,6},{6,4},{8,10},{10,8},{12,14},{14,12},{16,18},{18,... | collective-permute-start | bytes 12582920 | tf_op jit(solution)/shard_map/ppermute | solution.py:722
  321.2 14.5 %copy-start.44 = (bf16[512,2048]{1,0:T(8,128)(2,1)}, bf16[512,2048]{1,0:T(8,128)(2,1)S(1)}, u32[]{:S(2)}) copy-start(bf16[512,2048]{1,0:T(8,128)(2,1)S(1)} %bitcast_convert_fusion.2) | copy-start | bytes 6291460
  330.3 6.6 %copy-start.47 = (bf16[2048,512]{1,0:T(8,128)(2,1)}, bf16[2048,512]{1,0:T(8,128)(2,1)S(1)}, u32[]{:S(2)}) copy-start(bf16[2048,512]{1,0:T(8,128)(2,1)S(1)} %bitcast_convert_fusion.1) | copy-start | bytes 6291460
  338.1 54.2 %collective-permute-start.5 = (bf16[128,2048]{1,0:T(8,128)(2,1)}, bf16[128,2048]{1,0:T(8,128)(2,1)}, u32[]{:S(2)}, u32[]{:S(2)}) collective-permute-start(bf16[128,2048]{1,0:T(8,128)(2,1)} %get-tuple-element.154), channel_id=1, source_target_pairs={{0,24},{2,26},{4,28},{6,30},{8,0},{10,2},{12,4},{14,6},{16,8},{18,... | collective-permute-start | bytes 1572872 | tf_op jit(solution)/shard_map/ppermute | solution.py:718
  340.8 52.1 %collective-permute-start.4 = (bf16[128,2048]{1,0:T(8,128)(2,1)}, bf16[128,2048]{1,0:T(8,128)(2,1)}, u32[]{:S(2)}, u32[]{:S(2)}) collective-permute-start(bf16[128,2048]{1,0:T(8,128)(2,1)} %get-tuple-element.155), channel_id=1, source_target_pairs={{0,8},{2,10},{4,12},{6,14},{8,16},{10,18},{12,20},{14,22},{16,24},... | collective-permute-start | bytes 1572872 | tf_op jit(solution)/shard_map/ppermute | solution.py:718
  340.8 54.4 %collective-permute-start.7 = (bf16[512,512]{1,0:T(8,128)(2,1)}, bf16[512,512]{1,0:T(8,128)(2,1)}, u32[]{:S(2)}, u32[]{:S(2)}) collective-permute-start(bf16[512,512]{1,0:T(8,128)(2,1)} %get-tuple-element.151), channel_id=1, source_target_pairs={{0,24},{2,26},{4,28},{6,30},{8,0},{10,2},{12,4},{14,6},{16,8},{18,... | collective-permute-start | bytes 1572872 | tf_op jit(solution)/shard_map/ppermute | solution.py:718
  344.6 50.6 %collective-permute-start.6 = (bf16[512,512]{1,0:T(8,128)(2,1)}, bf16[512,512]{1,0:T(8,128)(2,1)}, u32[]{:S(2)}, u32[]{:S(2)}) collective-permute-start(bf16[512,512]{1,0:T(8,128)(2,1)} %get-tuple-element.152), channel_id=1, source_target_pairs={{0,8},{2,10},{4,12},{6,14},{8,16},{10,18},{12,20},{14,22},{16,24},... | collective-permute-start | bytes 1572872 | tf_op jit(solution)/shard_map/ppermute | solution.py:718
  346.4 48.9 %collective-permute-start.8 = (bf16[4,256,1024]{2,1,0:T(8,128)(2,1)S(1)}, bf16[4,256,1024]{2,1,0:T(8,128)(2,1)}, u32[]{:S(2)}, u32[]{:S(2)}) collective-permute-start(bf16[4,256,1024]{2,1,0:T(8,128)(2,1)S(1)} %get-tuple-element.142), channel_id=1, source_target_pairs={{0,1},{1,0},{2,3},{3,2},{4,5},{5,4},{6,7},{7,6},{8,9},{9,8},{10,11... | collective-permute-start | bytes 6291464 | tf_op jit(solution)/shard_map/ppermute | solution.py:871
  347.1 48.2 %copy-start.21 = (f32[256,8,512]{2,1,0:T(8,128)S(1)}, f32[256,8,512]{2,1,0:T(8,128)}, u32[]{:S(2)}) copy-start(f32[256,8,512]{2,1,0:T(8,128)} %get-tuple-element.138) | copy-start | bytes 12582916
  347.1 48.2 %copy-start.76 = (f32[1,4,128]{2,0,1:T(1,128)S(1)}, f32[1,4,128]{2,0,1:T(1,128)}, u32[]{:S(2)}) copy-start(f32[1,4,128]{2,0,1:T(1,128)} %get-tuple-element.161) | copy-start | bytes 6148
  392.2 39.8 %collective-permute-start.9 = (bf16[128,2048]{1,0:T(8,128)(2,1)S(1)}, bf16[128,2048]{1,0:T(8,128)(2,1)S(1)}, u32[]{:S(2)}, u32[]{:S(2)}) collective-permute-start(bf16[128,2048]{1,0:T(8,128)(2,1)S(1)} %get-tuple-element.153), channel_id=1, source_target_pairs={{0,16},{2,18},{4,20},{6,22},{8,24},{10,26},{12,28},{14,30},{16,0},... | collective-permute-start | bytes 1572872 | tf_op jit(solution)/shard_map/ppermute | solution.py:718
  392.9 81.4 %collective-permute-start.10 = (bf16[512,512]{1,0:T(8,128)(2,1)}, bf16[512,512]{1,0:T(8,128)(2,1)}, u32[]{:S(2)}, u32[]{:S(2)}) collective-permute-start(bf16[512,512]{1,0:T(8,128)(2,1)} %get-tuple-element.150), channel_id=1, source_target_pairs={{0,16},{2,18},{4,20},{6,22},{8,24},{10,26},{12,28},{14,30},{16,0},... | collective-permute-start | bytes 1572872 | tf_op jit(solution)/shard_map/ppermute | solution.py:718
  395.3 7.4 %copy-start.56 = (f32[256,8,128]{2,1,0:T(8,128)S(1)}, f32[256,8,128]{2,1,0:T(8,128)}, u32[]{:S(2)}) copy-start(f32[256,8,128]{2,1,0:T(8,128)} %get-tuple-element.96) | copy-start | bytes 3145732
  402.1 30.9 %copy-start.34 = (bf16[4,256,1024]{2,1,0:T(8,128)(2,1)S(1)}, bf16[4,256,1024]{2,1,0:T(8,128)(2,1)}, u32[]{:S(2)}) copy-start(bf16[4,256,1024]{2,1,0:T(8,128)(2,1)} %get-tuple-element.98) | copy-start | bytes 6291460
  402.8 36.5 %copy-start.37 = (f32[256,8,512]{2,1,0:T(8,128)S(1)}, f32[256,8,512]{2,1,0:T(8,128)}, u32[]{:S(2)}) copy-start(f32[256,8,512]{2,1,0:T(8,128)} %get-tuple-element.94) | copy-start | bytes 12582916
  433.0 6.3 %copy-start.35 = (f32[256,8,512]{2,1,0:T(8,128)S(1)}, f32[256,8,512]{2,1,0:T(8,128)}, u32[]{:S(2)}) copy-start(f32[256,8,512]{2,1,0:T(8,128)} %get-tuple-element.136.delta_ref) | copy-start | bytes 12582916
  433.0 6.3 %copy-start.36 = (f32[256,8,512]{2,1,0:T(8,128)S(1)}, f32[256,8,512]{2,1,0:T(8,128)}, u32[]{:S(2)}) copy-start(f32[256,8,512]{2,1,0:T(8,128)} %get-tuple-element.145.ds_ref) | copy-start | bytes 12582916
  433.0 6.3 %copy-start.64 = (bf16[160,512,1]{1,0,2:T(8,128)(2,1)S(1)}, bf16[160,512,1]{1,0,2:T(8,128)(2,1)}, u32[]{:S(2)}) copy-start(bf16[160,512,1]{1,0,2:T(8,128)(2,1)} %reshape.536) | copy-start | bytes 491524
  433.0 6.3 %copy-start.74 = (f32[1,4,128]{2,0,1:T(1,128)S(1)}, f32[1,4,128]{2,0,1:T(1,128)}, u32[]{:S(2)}) copy-start(f32[1,4,128]{2,0,1:T(1,128)} %get-tuple-element.160) | copy-start | bytes 6148
  437.6 25.9 %collective-permute-start.11 = (bf16[2,256,1024]{2,1,0:T(8,128)(2,1)S(1)}, bf16[2,256,1024]{2,1,0:T(8,128)(2,1)}, u32[]{:S(2)}, u32[]{:S(2)}) collective-permute-start(bf16[2,256,1024]{2,1,0:T(8,128)(2,1)S(1)} %fusion.45), channel_id=1, source_target_pairs={{0,4},{2,6},{4,0},{6,2},{8,12},{10,14},{12,8},{14,10},{16,20},{18,... | collective-permute-start | bytes 3145736 | tf_op jit(solution)/shard_map/ppermute | solution.py:722
  450.0 13.5 %copy-start.29 = (f32[4,256,1024]{2,1,0:T(8,128)S(1)}, f32[4,256,1024]{2,1,0:T(8,128)}, u32[]{:S(2)}) copy-start(f32[4,256,1024]{2,1,0:T(8,128)} %copy-done.28) | copy-start | bytes 12582916
  452.9 12.5 %copy-start.24 = (f32[256,8,512]{2,1,0:T(8,128)S(1)}, f32[256,8,512]{2,1,0:T(8,128)}, u32[]{:S(2)}) copy-start(f32[256,8,512]{2,1,0:T(8,128)} %copy-done.23) | copy-start | bytes 12582916
  452.9 12.5 %copy-start.66 = (f32[1,4,128]{2,0,1:T(1,128)S(1)}, f32[1,4,128]{2,0,1:T(1,128)}, u32[]{:S(2)}) copy-start(f32[1,4,128]{2,0,1:T(1,128)} %copy-done.65) | copy-start | bytes 6148
  452.9 12.5 %copy-start.68 = (f32[1,4,128]{2,0,1:T(1,128)S(1)}, f32[1,4,128]{2,0,1:T(1,128)}, u32[]{:S(2)}) copy-start(f32[1,4,128]{2,0,1:T(1,128)} %copy-done.67) | copy-start | bytes 6148
  452.9 12.5 %copy-start.70 = (f32[1,4,128]{2,0,1:T(1,128)S(1)}, f32[1,4,128]{2,0,1:T(1,128)}, u32[]{:S(2)}) copy-start(f32[1,4,128]{2,0,1:T(1,128)} %get-tuple-element.188) | copy-start | bytes 6148
  452.9 12.5 %copy-start.72 = (f32[1,4,128]{2,0,1:T(1,128)S(1)}, f32[1,4,128]{2,0,1:T(1,128)}, u32[]{:S(2)}) copy-start(f32[1,4,128]{2,0,1:T(1,128)} %get-tuple-element.189) | copy-start | bytes 6148
  465.3 9.0 %collective-permute-start.12 = (bf16[256,1024]{1,0:T(8,128)(2,1)S(1)}, bf16[256,1024]{1,0:T(8,128)(2,1)S(1)}, u32[]{:S(2)}, u32[]{:S(2)}) collective-permute-start(bf16[256,1024]{1,0:T(8,128)(2,1)S(1)} %fusion.63), channel_id=1, source_target_pairs={{0,2},{2,0},{4,6},{6,4},{8,10},{10,8},{12,14},{14,12},{16,18},{18,... | collective-permute-start | bytes 1572872 | tf_op jit(solution)/shard_map/ppermute | solution.py:722
  473.2 11.3 %copy-start.32 = (bf16[256,8,512]{2,1,0:T(8,128)(2,1)}, bf16[256,8,512]{2,1,0:T(8,128)(2,1)S(1)}, u32[]{:S(2)}) copy-start(bf16[256,8,512]{2,1,0:T(8,128)(2,1)S(1)} %get-tuple-element.102) | copy-start | bytes 6291460
  474.3 10.2 %copy-start.58 = (bf16[256,1024]{1,0:T(8,128)(2,1)}, bf16[256,1024]{1,0:T(8,128)(2,1)S(1)}, u32[]{:S(2)}) copy-start(bf16[256,1024]{1,0:T(8,128)(2,1)S(1)} %collective-permute-done.12) | copy-start | bytes 1572868
  474.9 9.6 %copy-start.48 = (bf16[8,256,512]{2,1,0:T(8,128)(2,1)}, bf16[8,256,512]{2,1,0:T(8,128)(2,1)S(1)}, u32[]{:S(2)}) copy-start(bf16[8,256,512]{2,1,0:T(8,128)(2,1)S(1)} %copy.61) | copy-start | bytes 6291460
  484.5 27.0 %collective-permute-start.13 = (bf16[2048,1024]{1,0:T(8,128)(2,1)}, bf16[2048,1024]{1,0:T(8,128)(2,1)}, u32[]{:S(2)}, u32[]{:S(2)}) collective-permute-start(bf16[2048,1024]{1,0:T(8,128)(2,1)} %convolution_convert_fusion.2), channel_id=1, source_target_pairs={{0,2},{2,0},{4,6},{6,4},{8,10},{10,8},{12,14},{14,12},{16,18},{18,... | collective-permute-start | bytes 12582920 | tf_op jit(solution)/shard_map/ppermute | solution.py:722
  486.2 7.2 %copy-start.77 = (f32[512]{0:T(512)S(1)}, f32[512]{0:T(512)}, u32[]{:S(2)}) copy-start(f32[512]{0:T(512)} %get-tuple-element.144) | copy-start | bytes 6148
  486.2 7.4 %copy-start.43 = (bf16[2048,256]{0,1:T(8,128)(2,1)S(1)}, bf16[2048,256]{0,1:T(8,128)(2,1)}, u32[]{:S(2)}) copy-start(bf16[2048,256]{0,1:T(8,128)(2,1)} %copy-done.42) | copy-start | bytes 3145732
  492.5 6.6 %copy-start.59 = (bf16[256,1024]{1,0:T(8,128)(2,1)S(1)}, bf16[256,1024]{1,0:T(8,128)(2,1)}, u32[]{:S(2)}) copy-start(bf16[256,1024]{1,0:T(8,128)(2,1)} %copy-done.58) | copy-start | bytes 1572868
  502.0 9.5 %copy-start.17 = (bf16[32,64,1024]{2,1,0:T(8,128)(2,1)S(1)}, bf16[32,64,1024]{2,1,0:T(8,128)(2,1)}, u32[]{:S(2)}) copy-start(bf16[32,64,1024]{2,1,0:T(8,128)(2,1)} %copy-done.15) | copy-start | bytes 12582916
  502.0 9.5 %copy-start.46 = (bf16[8,256,512]{2,1,0:T(8,128)(2,1)S(1)}, bf16[8,256,512]{2,1,0:T(8,128)(2,1)}, u32[]{:S(2)}) copy-start(bf16[8,256,512]{2,1,0:T(8,128)(2,1)} %copy.54) | copy-start | bytes 6291460
  502.0 9.5 %copy-start.49 = (bf16[8,256,512]{2,1,0:T(8,128)(2,1)S(1)}, bf16[8,256,512]{2,1,0:T(8,128)(2,1)}, u32[]{:S(2)}) copy-start(bf16[8,256,512]{2,1,0:T(8,128)(2,1)} %copy-done.48) | copy-start | bytes 6291460
  (33 other events, 108.1 us)

commit v3 on v2

--- a/solution.py
+++ b/solution.py
@@ -52,12 +52,12 @@
     pl.semaphore_wait(barrier, len(places))
 
 
-def comm_call(kernel, outs, scratch, ident, name, args, vmem=None, in_vmem=()):
+def comm_call(kernel, outs, scratch, ident, name, args, vmem=None, in_vmem=(), out_vmem=False):
     spaces = [pl.BlockSpec(memory_space=pltpu.VMEM if i in in_vmem else pl.ANY) for i in range(len(args))]
     return pl.pallas_call(
         kernel,
         in_specs=spaces,
-        out_specs=[pl.BlockSpec(memory_space=pl.ANY)] * len(outs),
+        out_specs=[pl.BlockSpec(memory_space=pltpu.VMEM if out_vmem else pl.ANY)] * len(outs),
         out_shape=outs,
         scratch_shapes=scratch,
         compiler_params=pltpu.CompilerParams(
@@ -67,8 +67,8 @@
     )(*args)
 
 
-def gather_kernel(grid, rows, h_ref, g_ref, c_ref, wi_ref, sm_ref, n_all, c_all, wi_all, sm_all, gain_out,
-                  gain_buf, gains, n_low, local, g_send, g_recv, n_send, n_recv, c_send, c_recv, a_send, a_recv,
+def gather_kernel(grid, rows, h_ref, g_ref, c_ref, in_ref, sm_ref, n_all, c_all, wi_all, sm_all, gain_out,
+                  gain_buf, gains, n_low, wi_cut, local, g_send, g_recv, n_send, n_recv, c_send, c_recv, a_send, a_recv,
                   z_send, z_recv, s_send, s_recv):
     z, q, f = grid.here()
     F, C, Z, N = grid.fsdp, grid.members, grid.planes, grid.devices
@@ -85,6 +85,12 @@
     def _(d):
         pl.semaphore_signal(barrier, inc=1, device_id=other(d), device_id_type=MESH)
 
+    wi_ref = in_ref
+    if in_ref.dtype == F32:
+        wi_ref, lanes = wi_cut, wi_cut.shape[2] // (2 * Z)
+        for j in range(C):
+            for m in range(2 * Z):
+                wi_cut[j, :, m * lanes:(m + 1) * lanes] = in_ref[:, (m * C + j) * lanes:(m * C + j + 1) * lanes].astype(BF16)
     pl.semaphore_wait(barrier, N - 1)
 
     def gain_copy(d):
@@ -172,7 +178,6 @@
         remote(ref.at[block], ref.at[block], n_send.at[0], sems.at[block], grid.at(z, twin, f)).wait_recv()
 
     others = [lax.rem(f + d, F) for d in range(1, F)]
-    push_c(me, c_ref, grid.at(z, opposite, f))
 
     gain_buf[lin] = g_ref[...]
 
@@ -197,6 +202,7 @@
 
     for g in others:
         push_n(me, n_low, grid.at(z, q, g))
+    push_c(me, c_ref, grid.at(z, opposite, f))
     push_n(me, n_low, grid.at(z, opposite, f))
     for g in others:
         push_c(me, c_ref, grid.at(z, q, g))
@@ -270,124 +276,354 @@
 
 def gather_all(grid, hidden, gain_tile, cot, wi, small):
     F, C, Z, N = grid.fsdp, grid.members, grid.planes, grid.devices
-    tokens, rows = hidden.shape[0], wi.shape[1]
+    cut = wi.dtype == F32
+    rows, width = wi.shape[0 if cut else 1], 2 * DI // C
+    tokens = hidden.shape[0]
     dma = pltpu.SemaphoreType.DMA
     outs = [
         jax.ShapeDtypeStruct((C, tokens, D), BF16),
         jax.ShapeDtypeStruct((C, tokens, D), BF16),
-        jax.ShapeDtypeStruct((Z * C,) + wi.shape[1:], BF16),
+        jax.ShapeDtypeStruct((Z * C, rows, width), BF16),
         jax.ShapeDtypeStruct((Z,) + small.shape, BF16),
         jax.ShapeDtypeStruct((8, D), F32),
     ]
     count = (F - 1) + F + 2 * F
     scratch = [pltpu.VMEM((N, 8, 128), F32), pltpu.VMEM((8, D), F32), pltpu.VMEM((tokens, D), BF16)]
+    scratch += [pltpu.VMEM((C, rows, width) if cut else (1, 16, 128), BF16)]
     scratch += [dma((5,)), dma((N,)), dma((N,)), dma((count,)), dma((C,)), dma((count,)), dma((C,)), dma((C,)), dma((C,))]
     scratch += [dma((2, Z, C)), dma((2, Z, C)), dma((Z,)), dma((Z,))]
     return comm_call(
         functools.partial(gather_kernel, grid, rows), outs, scratch, 1, "gather_weights_and_tokens",
-        (hidden, gain_tile, cot, wi, small), in_vmem=(0, 1),
+        (hidden, gain_tile, cot, wi, small), vmem=32 * 2**20, in_vmem=(0, 1, 3) if cut else (0, 1),
     )
 
 
-def plane_sum_kernel(grid, part_ref, out_ref, send_buf, recv_buf, result, send, recv, out_send, out_recv, own):
+def plane_sum_kernel(grid, split, part_ref, *refs):
+    outs, (send_buf, recv_buf, result, landed, send, recv, out_send, out_recv) = refs[:1 + split], refs[1 + split:]
+    out_low, out_coef = outs if split else (outs[0].at[:, pl.ds(0, 128)], outs[0].at[:, pl.ds(128, 128)])
     z, q, f = grid.here()
     C = grid.members
     me = q * grid.fsdp + f
-    rows = recv_buf.shape[1]
+    rows = part_ref.shape[0] // C
+    quarter = rows // 4
     greet([grid.member(z, lax.rem(me + d, C)) for d in range(1, C)])
-    lane = lax.broadcasted_iota(jnp.int32, (rows, 128), 1)
-
-    def packed(v):
-        high = v.astype(BF16).astype(F32)
-        return high + pltpu.roll(v - high, 32, 1)
-
-    @pl.loop(0, C)
-    def _(k):
-        at = pl.ds(pl.multiple_of(k * rows, 16), rows)
-        send_buf[k, :, 0:128] = part_ref[at, 0:128].astype(BF16)
-        send_buf[k, :, 128:256] = packed(part_ref[at, 128:256]).astype(BF16)
+    lane = lax.broadcasted_iota(jnp.int32, (quarter, 128), 1)
+
+    def span(k, m, size):
+        return pl.ds(pl.multiple_of(k * rows + m * size, 16), size)
+
+    def pack(k):
+        send_buf[k, 0:rows, :] = part_ref[span(k, 0, rows), 0:128].astype(BF16)
+        mixed = part_ref[span(k, 0, quarter), 128:256]
+        for m in range(1, 4):
+            mixed = mixed + pltpu.roll(part_ref[span(k, m, quarter), 128:256], 32 * m, 1)
+        send_buf[k, rows:, :] = mixed.astype(BF16)
 
     copies = []
     for d in range(1, C):
         j = lax.rem(me + d, C)
+        pack(j)
         copy = remote(send_buf.at[j], recv_buf.at[d], send.at[d], recv.at[d], grid.member(z, j))
         copy.start()
         copies.append(copy)
-    low = send_buf[me, :, 0:128].astype(F32)
-    high = send_buf[me, :, 128:256].astype(F32)
+    pack(me)
+    total = send_buf[me].astype(F32)
     for d in range(1, C):
         copies[d - 1].wait_recv()
-        low = low + recv_buf[d, :, 0:128].astype(F32)
-        high = high + recv_buf[d, :, 128:256].astype(F32)
-    total = jnp.where(lane < 32, high + pltpu.roll(high, 96, 1), 0.0)
-    result[:, 0:128] = low.astype(BF16)
-    result[:, 128:256] = packed(total).astype(BF16)
-    for copy in copies:
-        copy.wait_send()
-    mine = pltpu.make_async_copy(result, out_ref.at[me], own)
-    mine.start()
-    copies = []
+        total = total + recv_buf[d].astype(F32)
+    result[...] = total.astype(BF16)
+    pushes = []
     for d in range(1, C):
-        j = lax.rem(me + d, C)
-        copy = remote(result, out_ref.at[me], out_send.at[d], out_recv.at[d], grid.member(z, j))
+        copy = remote(result, landed.at[me], out_send.at[d], out_recv.at[d], grid.member(z, lax.rem(me + d, C)))
         copy.start()
-        copies.append(copy)
-    mine.wait()
+        pushes.append(copy)
+
+    def unpack(k, block):
+        out_low[span(k, 0, rows), :] = block[0:rows, :]
+        mixed = block[rows:, :].astype(F32)
+        for m in range(4):
+            part = pltpu.roll(mixed, 128 - 32 * m, 1) if m else mixed
+            out_coef[span(k, m, quarter), :] = jnp.where(lane < 32, part, 0.0).astype(BF16)
+
+    unpack(me, result)
     for d in range(1, C):
         back = lax.rem(me + C - d, C)
-        remote(result, out_ref.at[back], out_send.at[d], out_recv.at[d], grid.member(z, back)).wait_recv()
-    for copy in copies:
+        remote(result, landed.at[back], out_send.at[d], out_recv.at[d], grid.member(z, back)).wait_recv()
+        unpack(back, landed.at[back])
+    for copy in copies + pushes:
         copy.wait_send()
 
 
-def plane_sum(grid, part, ident):
+def plane_sum(grid, part, split, ident):
     C = grid.members
-    rows = part.shape[0] // C
+    count = part.shape[0]
+    rows = count // C
+    packed = rows + rows // 4
     dma = pltpu.SemaphoreType.DMA
-    out = comm_call(
-        functools.partial(plane_sum_kernel, grid),
-        [jax.ShapeDtypeStruct((C, rows, 256), BF16)],
-        [pltpu.VMEM((C, rows, 256), BF16), pltpu.VMEM((C, rows, 256), BF16), pltpu.VMEM((rows, 256), BF16)]
-        + [dma((C,))] * 4 + [dma],
-        ident, "plane_sum", (part,), vmem=40 * 2**20, in_vmem=(0,),
-    )[0]
-    return out.reshape(C * rows, 256)
-
-
-def line_gather_kernel(grid, count, *refs):
+    return comm_call(
+        functools.partial(plane_sum_kernel, grid, split),
+        [jax.ShapeDtypeStruct((count, 128), BF16)] * 2 if split else [jax.ShapeDtypeStruct((count, 256), BF16)],
+        [pltpu.VMEM((C, packed, 128), BF16), pltpu.VMEM((C, packed, 128), BF16), pltpu.VMEM((packed, 128), BF16), pltpu.VMEM((C, packed, 128), BF16)]
+        + [dma((C,))] * 4,
+        ident, "plane_sum", (part,), vmem=40 * 2**20, in_vmem=(0,), out_vmem=True,
+    )
+
+
+def edges_kernel(grid, step, count, edge_ref, *refs):
+    z, q, f = grid.here()
+    C, Z = grid.members, grid.planes
+    me = q * grid.fsdp + f
+    ins, edge_out, outs = refs[:count], refs[count], refs[count + 1:2 * count + 1]
+    e_send, e_recv, local, send, recv = refs[2 * count + 1:]
+    above, below = z < Z - 1, z > 0
+    to, source = (above, below) if step > 0 else (below, above)
+    barrier = pltpu.get_barrier_semaphore()
+
+    @pl.when(above)
+    def _():
+        pl.semaphore_signal(barrier, inc=1, device_id=grid.at(z + 1, q, f), device_id_type=MESH)
+
+    @pl.when(below)
+    def _():
+        pl.semaphore_signal(barrier, inc=1, device_id=grid.at(z - 1, q, f), device_id_type=MESH)
+
+    members = [lax.rem(me + d, C) for d in range(1, C)] if count else []
+    for j in members:
+        pl.semaphore_signal(barrier, inc=1, device_id=grid.member(z, j), device_id_type=MESH)
+    pl.semaphore_wait(barrier, len(members) + jnp.where(above & below, 2, 1))
+    edge = remote(edge_ref, edge_out, e_send, e_recv, grid.at(z + step, q, f))
+
+    @pl.when(to)
+    def _():
+        edge.start()
+
+    pushes, waits = [], []
+    for i in range(count):
+        for d, j in enumerate(members, 1):
+            back = lax.rem(me + C - d, C)
+            pushes.append(remote(ins[i].at[j], outs[i].at[me], send.at[i, d], recv.at[i, d], grid.member(z, j)))
+            waits.append(remote(ins[i].at[me], outs[i].at[back], send.at[i, d], recv.at[i, d], grid.member(z, back)))
+    for copy in pushes:
+        copy.start()
+    for i in range(count):
+        own = pltpu.make_async_copy(ins[i].at[me], outs[i].at[me], local.at[i])
+        own.start()
+        own.wait()
+    for copy in waits:
+        copy.wait_recv()
+
+    @pl.when(source)
+    def _():
+        remote(edge_ref, edge_out, e_send, e_recv, grid.at(z - step, q, f)).wait_recv()
+
+    for copy in pushes:
+        copy.wait_send()
+
+    @pl.when(to)
+    def _():
+        edge.wait_send()
+
+
+def send_edges(grid, edge, step, arrays, ident, name):
+    dma = pltpu.SemaphoreType.DMA
+    n, C = len(arrays), grid.members
+    m = max(n, 1)
+    args = (edge,) + tuple(arrays)
+    return comm_call(
+        functools.partial(edges_kernel, grid, step, n), [jax.ShapeDtypeStruct(a.shape, a.dtype) for a in args],
+        [dma, dma, dma((m,)), dma((m, C)), dma((m, C))], ident, name, args,
+        in_vmem=tuple(range(n + 1)), out_vmem=True,
+    )
+
+
+def token_sums_kernel(grid, lines_in, part_ref, rows_ref, gate_ref, *refs):
+    ins, outs = refs[:lines_in], refs[3 + lines_in:3 + 2 * lines_in]
+    out_ref, row_out, gate_out = refs[lines_in:lines_in + 3]
+    (x_in, y_in, x_sum, y_sum, x_last, y_last, final, landed, row_in, row_sum, local, x_send, x_recv, y_send, y_recv, b_send,
+     b_recv, a_send, a_recv, t_send, t_recv, l_send, l_recv, f_send, f_recv, r_send, r_recv, g_send, g_recv) = refs[3 + 2 * lines_in:]
+    z, q, f = grid.here()
+    F, Z, C = grid.fsdp, grid.planes, grid.members
+    me = q * F + f
+    y, core = q // 2, lax.rem(q, 2)
+    rows = part_ref.shape[2] // 2
+    first, second = pl.ds(0, rows), pl.ds(rows, rows)
+    across, twin = grid.at(z, q ^ 2, f), grid.at(z, q ^ 1, f)
+    others = [lax.rem(f + d, F) for d in range(1, F)]
+    greet([grid.member(z, lax.rem(me + d, C)) for d in range(1, C)] + [grid.at(lax.rem(z + d, Z), q, f) for d in range(1, Z)])
+    far, near = pl.ds(2 * (1 - y), 2), pl.ds(2 * y, 2)
+
+    def add(target, sources):
+        @pl.loop(0, rows // 16)
+        def _(r):
+            at = pl.ds(pl.multiple_of(r * 16, 16), 16)
+            value = sources[0][at, :].astype(F32)
+            for source in sources[1:]:
+                value = value + source[at, :].astype(F32)
+            target[at, :] = value.astype(BF16)
+
+    x_copies = [
+        remote(part_ref.at[pl.ds(0, 4), g, first], x_in.at[d], x_send.at[d], x_recv.at[d], grid.at(z, q, g))
+        for d, g in enumerate(others, 1)
+    ]
+    y_copy = remote(part_ref.at[far, :, second], y_in, y_send, y_recv, across)
+    row_copies = []
+    for d in range(1, Z):
+        j = lax.rem(z + d, Z)
+        row_copies.append(remote(rows_ref.at[j], row_in.at[d], f_send.at[d], f_recv.at[d], grid.at(j, q, f)))
+    for copy in row_copies + x_copies + [y_copy]:
+        copy.start()
+    mine, pushes, waits = [], [], []
+    for d in range(1, C):
+        j, back = lax.rem(me + d, C), lax.rem(me + C - d, C)
+        pushes.append(remote(gate_ref.at[j], gate_out.at[me], g_send.at[d], g_recv.at[d], grid.member(z, j)))
+        waits.append(remote(gate_ref.at[me], gate_out.at[back], g_send.at[d], g_recv.at[d], grid.member(z, back)))
+    gate_out[me] = gate_ref[me]
+    for i in range(lines_in):
+        mine.append(pltpu.make_async_copy(ins[i].at[z], outs[i].at[z], local.at[i]))
+        for d in range(1, Z):
+            j, back = lax.rem(z + d, Z), lax.rem(z + Z - d, Z)
+            pushes.append(remote(ins[i].at[j], outs[i].at[z], l_send.at[i, d], l_recv.at[i, d], grid.at(j, q, f)))
+            waits.append(remote(ins[i].at[z], outs[i].at[back], l_send.at[i, d], l_recv.at[i, d], grid.at(back, q, f)))
+    for copy in pushes + mine:
+        copy.start()
+    for copy in x_copies:
+        copy.wait_recv()
+
+    def x_block(k):
+        add(x_sum.at[k], [part_ref.at[k, f, first]] + [x_in.at[d, k] for d in range(1, F)])
+
+    for c in range(2):
+        x_block(2 * (1 - y) + c)
+    a_copy = remote(x_sum.at[far], x_last, a_send, a_recv, across)
+    a_copy.start()
+    y_copy.wait_recv()
+    b_copies = []
+    for d, g in enumerate(others, 1):
+        for c in range(2):
+            add(y_sum.at[g, c], [part_ref.at[2 * y + c, g, second], y_in.at[c, g]])
+        copy = remote(y_sum.at[g], y_last.at[d], b_send.at[d], b_recv.at[d], grid.at(z, q, g))
+        copy.start()
+        b_copies.append(copy)
+    for c in range(2):
+        x_block(2 * y + c)
+        add(y_sum.at[f, c], [part_ref.at[2 * y + c, f, second], y_in.at[c, f]])
+    a_copy.wait_recv()
+    for c in range(2):
+        add(final.at[c, first], [x_sum.at[2 * y + c], x_last.at[c]])
+    for copy in b_copies:
+        copy.wait_recv()
+    for c in range(2):
+        add(final.at[c, second], [y_sum.at[f, c]] + [y_last.at[d, c] for d in range(1, F)])
+    t_copy = remote(final.at[1 - core], landed, t_send, t_recv, twin)
+    t_copy.start()
+    for copy in row_copies:
+        copy.wait_recv()
+
+    @pl.loop(0, C)
+    def _(j):
+        value = rows_ref[z, j].astype(F32)
+        for d in range(1, Z):
+            value = value + row_in[d, j].astype(F32)
+        row_sum[j] = value.astype(BF16)
+
+    for d in range(1, C):
+        j, back = lax.rem(me + d, C), lax.rem(me + C - d, C)
+        copy = remote(row_sum.at[j], row_out.at[me], r_send.at[d], r_recv.at[d], grid.member(z, j))
+        copy.start()
+        pushes.append(copy)
+        waits.append(remote(row_sum.at[me], row_out.at[back], r_send.at[d], r_recv.at[d], grid.member(z, back)))
+    row_out[me] = row_sum[me]
+    out_ref[core] = final[core]
+    t_copy.wait_recv()
+    out_ref[1 - core] = landed[...]
+    for copy in mine:
+        copy.wait()
+    for copy in waits:
+        copy.wait_recv()
+    for copy in x_copies + [y_copy, a_copy, t_copy] + b_copies + row_copies + pushes:
+        copy.wait_send()
+
+
+def token_sums(grid, part, weight_rows, gate_rows, line_arrays, ident):
+    dma = pltpu.SemaphoreType.DMA
+    F, Z, n = grid.fsdp, grid.planes, len(line_arrays)
+    tokens, half = part.shape[2:]
+    rows = tokens // 2
+    buf = lambda *shape: pltpu.VMEM(shape + (rows, half), BF16)
+    hbm, vmem = pl.BlockSpec(memory_space=pl.ANY), pl.BlockSpec(memory_space=pltpu.VMEM)
+    return pl.pallas_call(
+        functools.partial(token_sums_kernel, grid, n),
+        in_specs=[vmem] * 3 + [hbm] * n,
+        out_specs=[vmem] * 3 + [hbm] * n,
+        out_shape=[jax.ShapeDtypeStruct((2, tokens, half), BF16), jax.ShapeDtypeStruct(gate_rows.shape, BF16), jax.ShapeDtypeStruct(gate_rows.shape, BF16)] + [jax.ShapeDtypeStruct(a.shape, a.dtype) for a in line_arrays],
+        scratch_shapes=[buf(F, 4), buf(2, F), buf(4), buf(F, 2), buf(2), buf(F, 2), pltpu.VMEM((2, tokens, half), BF16), pltpu.VMEM((tokens, half), BF16), pltpu.VMEM(weight_rows.shape, BF16), pltpu.VMEM(weight_rows.shape[1:], BF16)]
+        + [dma((n,)), dma((F,)), dma((F,)), dma, dma, dma((F,)), dma((F,)), dma, dma, dma, dma, dma((n, Z)), dma((n, Z)), dma((Z,)), dma((Z,))] + [dma((grid.members,))] * 4,
+        compiler_params=pltpu.CompilerParams(collective_id=ident, has_side_effects=True, vmem_limit_bytes=56 * 2**20),
+        cost_estimate=pl.CostEstimate(flops=45 * 10**9, bytes_accessed=10**8, transcendentals=0),
+        name="token_sums",
+    )(part, weight_rows, gate_rows, *line_arrays)
+
+
+def pack_kernel(grid, out_ref, gate_ref, *outs):
+    z, _, _ = grid.here()
+    rows, chans = gate_ref.shape[1:]
+    block, width = out_ref.shape[1:]
+    for d in range(grid.planes):
+        p = lax.rem(z + d, grid.planes)
+        outs[d][0:rows, :] = gate_ref[p]
+        for i in range(width // chans):
+            outs[d][rows + i * block:rows + (i + 1) * block, :] = out_ref[p, :, i * chans:(i + 1) * chans]
+
+
+def packed_for_planes(grid, out_part, gate_part):
+    Z, rows, chans = gate_part.shape
+    shape = (rows + out_part.shape[1] * out_part.shape[2] // chans, chans)
+    vmem = pl.BlockSpec(memory_space=pltpu.VMEM)
+    return pl.pallas_call(
+        functools.partial(pack_kernel, grid),
+        in_specs=[vmem] * 2,
+        out_specs=[vmem] * Z,
+        out_shape=[jax.ShapeDtypeStruct(shape, BF16)] * Z,
+        compiler_params=pltpu.CompilerParams(vmem_limit_bytes=32 * 2**20),
+        name="packed_for_planes",
+    )(out_part, gate_part)
+
+
+def states_kernel(grid, up_ref, down_ref, up_all, down_all, send, recv):
     z, q, f = grid.here()
     Z = grid.planes
-    ins, outs = refs[:count], refs[count:2 * count]
-    local, send, recv = refs[2 * count:]
     greet([grid.at(lax.rem(z + d, Z), q, f) for d in range(1, Z)])
-    copies = []
-    for i in range(count):
-        mine = pltpu.make_async_copy(ins[i], outs[i].at[z], local.at[i])
-        mine.start()
-        copies.append(mine)
-    pushes = []
-    for i in range(count):
+
+    def each(act):
         for d in range(1, Z):
-            copy = remote(ins[i], outs[i].at[z], send.at[i, d], recv.at[i, d], grid.at(lax.rem(z + d, Z), q, f))
-            copy.start()
-            pushes.append(copy)
-    for mine in copies:
-        mine.wait()
-    for i in range(count):
-        for d in range(1, Z):
-            back = lax.rem(z + Z - d, Z)
-            remote(ins[i], outs[i].at[back], send.at[i, d], recv.at[i, d], grid.at(back, q, f)).wait_recv()
-    for copy in pushes:
-        copy.wait_send()
-
-
-def line_gather(grid, arrays, ident, name):
+            above, below = z + d, z - d
+
+            @pl.when(above <= Z - 1)
+            def _():
+                act(
+                    remote(up_ref, up_all.at[z], send.at[0, d], recv.at[0, d], grid.at(above, q, f)),
+                    remote(down_ref, down_all.at[above], send.at[1, d], recv.at[1, d], grid.at(above, q, f)),
+                )
+
+            @pl.when(below >= 0)
+            def _():
+                act(
+                    remote(down_ref, down_all.at[z], send.at[1, d], recv.at[1, d], grid.at(below, q, f)),
+                    remote(up_ref, up_all.at[below], send.at[0, d], recv.at[0, d], grid.at(below, q, f)),
+                )
+
+    each(lambda push, pull: push.start())
+    each(lambda push, pull: pull.wait_recv())
+    each(lambda push, pull: push.wait_send())
+
+
+def exchange_states(grid, up, down, ident):
     dma = pltpu.SemaphoreType.DMA
-    n, Z = len(arrays), grid.planes
+    Z = grid.planes
     return comm_call(
-        functools.partial(line_gather_kernel, grid, n),
-        [jax.ShapeDtypeStruct((Z,) + a.shape, a.dtype) for a in arrays],
-        [dma((n,)), dma((n, Z)), dma((n, Z))], ident, name, tuple(arrays),
+        functools.partial(states_kernel, grid),
+        [jax.ShapeDtypeStruct((Z,) + a.shape, a.dtype) for a in (up, down)],
+        [dma((2, Z)), dma((2, Z))], ident, "segment_states", (up, down),
     )
 
 
@@ -531,7 +767,7 @@
             return acc + delta_ref[t, :, lanes]
         tot_ref[0, :, lanes] = lax.fori_loop(0, tc, total, tot_ref[0, :, lanes], unroll=tc)
 
-def scan_ends(delta, w, ds, coef, rate, fan, tc=STEPS, vmem=48 * 2**20):
+def scan_ends(delta, w, ds, coef, rate, fan, tc=2 * STEPS, vmem=48 * 2**20):
     tokens, members, cd = delta.shape
     sg, nch = members // 8, tokens // tc
     rows = STATE * 8
@@ -594,7 +830,7 @@
     dc_ref[...] = sums.reshape(tc, 8, 128)
 
 
-def scan_forward(delta, w, ds, coef, rate, fan, fold, s_in, tc=STEPS, vmem=56 * 2**20):
+def scan_forward(delta, w, ds, coef, rate, fan, fold, s_in, tc=2 * STEPS, vmem=56 * 2**20):
     tokens, members, cd = delta.shape
     sg, nch = members // 8, tokens // tc
     rows = STATE * 8
@@ -687,7 +923,7 @@
         out_shape=[jax.ShapeDtypeStruct(delta.shape, F32)] * 2 + [jax.ShapeDtypeStruct((tokens, members, 128), F32), jax.ShapeDtypeStruct((sg, rows, cd), F32)],
         scratch_shapes=[pltpu.VMEM((rows, cd), F32), pltpu.VMEM((tc * 8, 2 * STATE * 128), F32), pltpu.VMEM((tc * 8, STATE * 128), F32)],
         compiler_params=pltpu.CompilerParams(vmem_limit_bytes=vmem),
-        cost_estimate=pl.CostEstimate(flops=45 * 10**9, bytes_accessed=90 * 10**6, transcendentals=0),
+        cost_estimate=pl.CostEstimate(flops=10**9, bytes_accessed=10**6, transcendentals=0),
         name="scan_backward",
     )(delta, w, ds, coef, rate, fan, fold, hist, dout, g_in)
 
@@ -751,11 +987,14 @@
     gain_tile = jnp.where(lax.broadcasted_iota(jnp.int32, (slots, 1), 0) == lin % slots, gain_rows[None, :], 0.0).reshape(1, 128)
     gain_tile = jnp.broadcast_to(gain_tile, (8, 128))
     out_low = out_proj.astype(BF16)
-    in_low = rounded(in_proj).astype(BF16)
-    wi = in_low.reshape(rows, 2, Z, C, block).transpose(3, 0, 1, 2, 4).reshape(C, rows, 2 * chans)
+    wi = in_proj
+    if block % 128:
+        wi = rounded(in_proj).astype(BF16)
+        wi = wi.reshape(rows, 2, Z, C, block).transpose(3, 0, 1, 2, 4).reshape(C, rows, 2 * chans)
     small = jnp.concatenate(
         [conv_weight, conv_bias[None], delta_bias[None], skip_gain[None], decay_log, jnp.zeros((9, block), F32), delta_proj, state_proj.T], axis=0
-    ).astype(BF16)
+    )
+    small = lax.optimization_barrier(small).astype(BF16)
     normed_all, cot_all, wi_all, small_all, gains = gather_all(grid, hidden_low, gain_tile, cot_rows, wi, small)
     gains = gains[0]
     count = C * tokens
@@ -778,15 +1017,18 @@
     def by_member(value):
         return value.transpose(1, 0, 2).reshape(count, -1)
 
-    mixed = by_step(dot(normed_all, w_in).astype(BF16))
+    mixed = lax.optimization_barrier(dot(normed_all, w_in).astype(BF16))
+    tail = mixed.reshape(C, tokens, -1)[C - F:, tokens - (KW - 1):, :chans].transpose(1, 0, 2)
+    tail = tail.reshape((KW - 1) * F, chans)
+    edge_rows = -(-(KW - 1) * F // 16) * 16
+    tails = send_edges(grid, jnp.pad(tail, ((0, edge_rows - (KW - 1) * F), (0, 0))), 1, [], 3, "conv_edges")[0]
+    out_low, tails = lax.optimization_barrier((out_low, tails))
+    w_out = [out_low] + [along_z(grid, out_low, d) for d in range(1, Z)]
+    mixed, tails = lax.optimization_barrier((mixed, tails))
+    mixed = by_step(mixed)
     conv_in = mixed[:, :, :chans]
     gate = mixed[:, :, chans:].astype(F32)
-    edge_rows = -(-(KW - 1) * F // 16) * 16
-    tail = conv_in[tokens - (KW - 1):, C - F:].reshape((KW - 1) * F, chans)
-    tails = line_gather(grid, [jnp.pad(tail, ((0, edge_rows - (KW - 1) * F), (0, 0)))], 3, "conv_edges")[0]
-    out_low, tails = lax.optimization_barrier((out_low, tails))
-    w_out = [out_low] + [along_z(grid, out_low, d) for d in range(1, Z)]
-    before = lax.dynamic_index_in_dim(tails, jnp.maximum(z - 1, 0), 0, False)[: (KW - 1) * F]
+    before = tails[: (KW - 1) * F]
     before = jnp.where(z > 0, before, jnp.zeros_like(before)).reshape(KW - 1, F, chans)
     edge = jnp.concatenate([before, conv_in[tokens - (KW - 1):, : C - F]], axis=1)
     padded = jnp.concatenate([edge, conv_in], axis=0).astype(F32)
@@ -796,16 +1038,18 @@
     act = rounded(jax.nn.silu(conv_out))
     act_rows = lax.optimization_barrier(act.astype(BF16).reshape(count, chans))
     pad_lanes = 256 - DT_RANK - 2 * STATE
-    selected = contract_cols(act_rows, jnp.pad(w_state, ((0, pad_lanes), (0, 0))))
-    selected, *w_out = lax.optimization_barrier((plane_sum(grid, selected, 4), *w_out))
-    delta_in = selected[:, :DT_RANK]
-    coef = selected[:, DT_RANK:].reshape(tokens, C, 128)
+    w_state = jnp.pad(w_state, ((0, pad_lanes), (0, 0)))
+    selected = contract_cols(act_rows, w_state)
+    delta_in, coef = plane_sum(grid, selected, True, 4)
+    coef = coef.reshape(tokens, C, 128)
     delta_pre = (dot(delta_in, w_delta) + delta_shift).reshape(tokens, C, chans)
     delta = jax.nn.softplus(delta_pre)
     drive = delta * act
+    delta, drive = lax.optimization_barrier((delta, drive))
+    w_out, _ = lax.optimization_barrier((w_out, delta))
     gate_act = jax.nn.silu(gate)
     w_out = in_place_order(grid, w_out).reshape(chans, D)
-    d_gated = lax.optimization_barrier(by_step(contract_cols(cot_all, w_out)))
+    d_gated = lax.optimization_barrier(by_step(lax.optimization_barrier(contract_cols(cot_all, w_out))))
     d_scanned = d_gated * gate_act
 
     fan, fold = spread_tables()
@@ -826,16 +1070,23 @@
     adj = adjoints[3]
     for c in reversed(range(3)):
         adj = kept[c] * adj + adjoints[c]
-    flat = [end.reshape(F * STATE, chans), adj.reshape(F * STATE, chans), jnp.broadcast_to(jnp.sum(totals, axis=0), (F, 8, chans)).reshape(F * 8, chans)]
-    all_end, all_adj, all_tot = line_gather(grid, flat, 5, "segment_states")
-    plane_kept = jnp.exp(decay_rate * all_tot.reshape(Z, F, 8, chans)[:, :, :1])
-    all_end, all_adj = all_end.reshape(Z, F, STATE, chans), all_adj.reshape(Z, F, STATE, chans)
+    plane_total = jnp.broadcast_to(jnp.sum(totals, axis=0), (F, 8, chans))
+
+    def with_total(value):
+        return jnp.concatenate([value, plane_total], axis=1).reshape(F * (STATE + 8), chans)
+
+    ups, downs = exchange_states(grid, with_total(end), with_total(adj), 5)
+    ups, downs = ups.reshape(Z, F, STATE + 8, chans), downs.reshape(Z, F, STATE + 8, chans)
+
+    def through(received, p, value):
+        return jnp.exp(decay_rate * received[p, :, STATE:STATE + 1]) * value + received[p, :, :STATE]
+
     state = jnp.zeros((F, STATE, chans), F32)
     adj = state
     for p in range(Z - 1):
-        state = jnp.where(p < z, plane_kept[p] * state + all_end[p], state)
+        state = jnp.where(p < z, through(ups, p, state), state)
     for p in reversed(range(1, Z)):
-        adj = jnp.where(p > z, plane_kept[p] * adj + all_adj[p], adj)
+        adj = jnp.where(p > z, through(downs, p, adj), adj)
     before_state, after_adj = [], []
     for c in range(4):
         before_state.append(state)
@@ -850,15 +1101,13 @@
     gated = (scanned * gate_act).astype(BF16)
     d_gate = d_gated * scanned * silu_slope(gate)
     gated, d_gate = lax.optimization_barrier((gated, d_gate.astype(BF16)))
-    gated, d_gate = by_member(gated), by_member(d_gate)
+    gated, d_gate = lax.optimization_barrier((by_member(gated), by_member(d_gate)))
     half = D // 2
     core = q % 2
     w_out_mine = lax.dynamic_slice_in_dim(w_out, core * half, half, 1)
     w_out_twin = lax.dynamic_slice_in_dim(w_out, (1 - core) * half, half, 1)
 
-    def sent_along_z(part):
-        pick = lambda d: lax.dynamic_index_in_dim(part, (z + d) % Z, 0, False)
-        return [pick(0)] + [along_z(grid, pick(d), d) for d in range(1, Z)]
+    near = [d for d in range(1, Z) if d != 2]
 
     def total(parts):
         return functools.reduce(lambda t, v: t + v.astype(F32), parts[1:], parts[0].astype(F32))
@@ -866,31 +1115,27 @@
     def twin_summed(mine, twin_part):
         return (mine + swap(grid, twin_part, 1).astype(F32)).astype(BF16).reshape(4, F, tokens, half)
 
-    def other_sequences(total):
-        pieces = [lax.dynamic_index_in_dim(total, (f + d) % F, 1, False) for d in range(F)]
-        return pieces[:1] + [lax.ppermute(pieces[d], "fsdp", [(g, (g + d) % F) for g in range(F)]) for d in range(1, F)]
-
-    def own_tokens(own):
-        own = own.reshape(2, 2, tokens, half)
-        keep = lax.dynamic_index_in_dim(own, q // 2, 0, False)
-        give = lax.dynamic_index_in_dim(own, 1 - q // 2, 0, False).astype(BF16)
-        keep = keep + swap(grid, give, 2).astype(F32)
-        final = lax.dynamic_index_in_dim(keep, core, 0, False)
-        give = lax.dynamic_index_in_dim(keep, 1 - core, 0, False).astype(BF16)
-        return final, swap(grid, give, 1)
+    def over_x(pick):
+        return [pick(f)] + [lax.ppermute(pick((f + d) % F), "fsdp", [(g, (g + d) % F) for g in range(F)]) for d in range(1, F)]
+
+    def over_y(low):
+        cut = lambda y: lax.dynamic_slice_in_dim(low, 2 * y, 2, 0)
+        return [cut(q // 2), swap(grid, cut(1 - q // 2), 2)]
+
+    early = tokens // 2
 
     twin_part = dot(gated, w_out_twin).astype(BF16)
     out_part = contract_rows(gated, cot_all).astype(BF16).reshape(Z, block, D)
     gate_part = contract_rows(normed_all, d_gate).astype(BF16).reshape(Z, C * rows, chans)
-    out_part, gate_part, chip_out = lax.optimization_barrier((out_part, gate_part, twin_summed(dot(gated, w_out_mine), twin_part)))
-    sent_out, sent_gate, sent_tokens = sent_along_z(out_part), sent_along_z(gate_part), other_sequences(chip_out)
+    out_part, gate_part = lax.optimization_barrier((out_part, gate_part))
+    chip_out = twin_summed(dot(gated, w_out_mine), twin_part)
+    packed = packed_for_planes(grid, out_part, gate_part)
+    sent_weights = [packed[0]] + [along_z(grid, packed[d], d) for d in range(1, Z)]
+    sent_tokens = [over_x(lambda g: lax.dynamic_index_in_dim(chip_out[:, :, :early], g, 1, False)), over_y(chip_out[:, :, early:])]
     history, _ = lax.optimization_barrier((history, (out_part, gate_part, chip_out)))
     swept = scan_backward(delta, drive, d_scanned, coef, rate8, fan, fold, history, d_out_coef, by_sublane(jnp.stack(after_adj)))
-    near = [d for d in range(1, Z) if d != 2]
-    (d_delta_a, coef_sum, d_coef, rate_sum), arrived_out, arrived_gate, sent_tokens = lax.optimization_barrier(
-        (swept, [sent_out[d] for d in near], [sent_gate[d] for d in near], sent_tokens)
-    )
-    mixer_own, mixer_twin = own_tokens(total(sent_tokens))
+    (d_delta_a, coef_sum, d_coef, rate_sum), arrived_weights, sent_tokens = lax.optimization_barrier((swept, [sent_weights[d] for d in near], sent_tokens))
+    first, second = (total(parts).astype(BF16) for parts in sent_tokens)
     decay_grad = rate_sum.reshape(C // 8, STATE, 8, chans).sum(axis=(0, 2)) * decay_rate
     skip_grad = jnp.sum(d_scanned * act, axis=(0, 1))
     d_delta_pre = (d_delta_a * (1.0 / LOG2E) + act * coef_sum) * jax.nn.sigmoid(delta_pre)
@@ -899,51 +1144,54 @@
     dproj_grad = contract_rows(delta_in, d_delta_low)
     d_delta_in = contract_cols(d_delta_low, w_delta)
     partial = jnp.concatenate([d_delta_in, d_coef.reshape(count, 128)], axis=1)
-    d_selected, far_out = lax.optimization_barrier((plane_sum(grid, partial, 6), sent_out[2]))
-    d_selected = d_selected[:, :DT_RANK + 2 * STATE]
-    sproj_grad = contract_rows(d_selected, act_rows)
+    d_selected, far_weights = lax.optimization_barrier((plane_sum(grid, partial, False, 6)[0], sent_weights[2]))
+    sproj_grad = contract_rows(act_rows, d_selected).T[:DT_RANK + 2 * STATE]
     d_activated = delta * coef_sum + skip * d_scanned + dot(d_selected, w_state).reshape(tokens, C, chans)
     d_conv = d_activated * silu_slope(conv_out)
     cbias_grad = jnp.sum(d_conv, axis=(0, 1))
     kernel_grad = jnp.stack([jnp.sum(d_conv * padded[k:k + tokens], axis=(0, 1)) for k in range(KW)])
     head = d_conv[:KW - 1, :F].reshape((KW - 1) * F, chans)
     head_rows = -(-(KW - 1) * F // 8) * 8
-    heads = line_gather(grid, [jnp.pad(head, ((0, head_rows - (KW - 1) * F), (0, 0)))], 7, "conv_grad_edges")[0]
-    after = lax.dynamic_index_in_dim(heads, jnp.minimum(z + 1, Z - 1), 0, False)[: (KW - 1) * F]
+    weight_sum = total([sent_weights[0], far_weights] + arrived_weights)
+    gate_sum = weight_sum[:C * rows].astype(BF16).reshape(C, rows, chans)
+    out_grad = weight_sum[C * rows:].reshape(D // chans, block, chans).transpose(1, 0, 2).reshape(block, D)
+    first, second = over_y(first), over_x(lambda g: lax.dynamic_index_in_dim(second, g, 1, False))
+    heads = send_edges(grid, jnp.pad(head, ((0, head_rows - (KW - 1) * F), (0, 0))), -1, [], 7, "conv_grad_edges")[0]
+    after = heads[: (KW - 1) * F]
     after = jnp.where(z < Z - 1, after, jnp.zeros_like(after)).reshape(KW - 1, F, chans)
     edge_grad = jnp.concatenate([d_conv[:KW - 1, F:], after], axis=1)
     grad_padded = jnp.concatenate([d_conv, edge_grad], axis=0)
     d_conv_in = jnp.zeros((tokens, C, chans), F32)
     for k in range(KW):
         d_conv_in = d_conv_in + taps[k] * grad_padded[KW - 1 - k:KW - 1 - k + tokens]
-    d_conv_in, far_gate, mixer_own, mixer_twin = lax.optimization_barrier((d_conv_in.astype(BF16), sent_gate[2], mixer_own, mixer_twin))
-    d_conv_in = by_member(d_conv_in)
-    out_grad = total([sent_out[0], far_out] + arrived_out)
-    gate_sum = total([sent_gate[0], far_gate] + arrived_gate).astype(BF16).reshape(C, rows, chans)
-    mixer_twin = mixer_twin.astype(F32)
-    mixer_out = jnp.where(core == 0, jnp.concatenate([mixer_own, mixer_twin], 1), jnp.concatenate([mixer_twin, mixer_own], 1))
+    d_conv_in = by_member(lax.optimization_barrier(d_conv_in.astype(BF16)))
+    conv_part = contract_rows(normed_all, d_conv_in).astype(BF16).reshape(Z, C, rows, chans)
     d_mixed = jnp.concatenate([d_conv_in, d_gate], axis=1)
     w_in_mine = lax.dynamic_slice_in_dim(w_in, core * half, half, 0)
     w_in_twin = lax.dynamic_slice_in_dim(w_in, (1 - core) * half, half, 0)
     from_twin = swap(grid, contract_cols(d_mixed, w_in_twin).astype(BF16), 1)
-    conv_part = contract_rows(normed_all, d_conv_in).astype(BF16).reshape(Z, C, rows, chans)
-    part_in = (contract_cols(d_mixed, w_in_mine) + from_twin.astype(F32)).astype(BF16).reshape(C, tokens, half)
+    part_in = (contract_cols(d_mixed, w_in_mine) + from_twin.astype(F32)).astype(BF16).reshape(4, F, tokens, half)
 
     fine = jnp.concatenate([kernel_grad, cbias_grad[None], shift_grad[None], skip_grad[None], decay_grad, jnp.zeros((9, chans), F32)], axis=0)
-    fine = fine.reshape(32, Z, block).transpose(1, 0, 2)
+    fine = lax.optimization_barrier(fine).reshape(32, Z, block).transpose(1, 0, 2)
     coarse = jnp.concatenate([dproj_grad, sproj_grad], axis=0).astype(BF16)
     coarse = coarse.reshape(-1, Z, block).transpose(1, 0, 2)
-    got = to_owners(grid, conv_part, [gate_sum, part_in], [coarse, fine], 9)
-    in_grad = jnp.stack([got[0], got[1]], axis=0).reshape(2, C, rows, Z, block).transpose(2, 0, 3, 1, 4)
+    part_in, first, second = lax.optimization_barrier((part_in, first, second))
+    own = jnp.concatenate([total(first), total(second)], axis=1)
+    mixer_own = lax.dynamic_index_in_dim(own, core, 0, False)
+    mixer_twin = swap(grid, lax.dynamic_index_in_dim(own, 1 - core, 0, False).astype(BF16), 1)
+    mixer_twin = mixer_twin.astype(F32)
+    mixer_out = jnp.where(core == 0, jnp.concatenate([mixer_own, mixer_twin], 1), jnp.concatenate([mixer_twin, mixer_own], 1))
+    d_normed, conv_rows, gate_rows, coarse, fine = token_sums(grid, part_in, conv_part, gate_sum, [coarse, fine], 9)
+    in_grad = jnp.stack([conv_rows, gate_rows], axis=0).reshape(2, C, rows, Z, block).transpose(2, 0, 3, 1, 4)
     in_grad = in_grad.reshape(rows, 2 * DI).astype(F32)
-    d_normed = got[2].astype(F32).reshape(2, 2, F, tokens, half).sum(axis=(0, 2))
-    d_unit = jnp.concatenate([d_normed[0], d_normed[1]], axis=1) * gains[None, :]
+    d_unit = jnp.concatenate([d_normed[0], d_normed[1]], axis=1).astype(F32) * gains[None, :]
     hidden = hidden_low.astype(F32)
     inv_rms = lax.rsqrt(jnp.mean(hidden * hidden, axis=1, keepdims=True) + EPS)
     unit = hidden * inv_rms
     block_out = (hidden + mixer_out).astype(BF16)
-    coarse = got[3].astype(F32).sum(axis=0)
-    fine = got[4].sum(axis=0)
+    coarse = coarse.astype(F32).sum(axis=0)
+    fine = fine.sum(axis=0)
     gain_grad = jnp.sum(rounded(in_proj) * in_grad, axis=1) / gain_rows
     mean_term = jnp.mean(d_unit * unit, axis=1, keepdims=True)
     input_grad = (cot_rows.astype(F32) + inv_rms * (d_unit - unit * mean_term)).astype(BF16)

time: 609 us -> 537 us (0.88)
  Pallas kernels: 352 us -> 315 us
  matrix products: 96.6 us -> 84.2 us
  other arithmetic: 61.1 us -> 50.2 us
    pallas_call x7 -> x6, Pallas kernels: 247 us -> 153 us  [comm_call(): pl.pallas_call(kernel, in_specs=spaces, out_specs=[pl.BlockSpec(memory_sp...]
    pallas_call x0 -> x2, Pallas kernels: none -> 62.9 us  [the longest x1 61 us: token_sums(): pl.pallas_call(functools.partial(token_sums_kernel, grid, n), in_specs=[v...]
    ppermute x4 -> x5, waiting for transfers between devices: 10.6 us -> 0.01 us  [swap(): return lax.ppermute(value, 'ctx', [(c, c ^ bit) for c in range(grid.ctx)])]
    ppermute x9 -> x6, starting transfers between devices: 12.5 us -> 8.97 us  [along_z(): lax.ppermute(value, 'ctx', [(c, (c + 4 * d) % ctx) for c in range(ctx)])]
    unnamed x168 -> x154, local copies, waits for them, and re-layouts: 20.8 us -> 17.5 us
  transfers between devices with their start and end apart: 14 -> 13, of which waited for: 1 -> 2; matrix products, arithmetic and copies ran while one was open for 16% -> 18% of each run, Pallas kernels for 18% -> 16%
where the time goes in v3:
time: 537 us; the launch traced here: 528 us
  Pallas kernels  315 us (59%)
  matrix products  84.2 us (16%)
  local copies, waits for them, and re-layouts  56.9 us (11%)
  other arithmetic  50.2 us (9%)
  starting transfers between devices  13.2 us (2%)
  waiting for transfers between devices  5.61 us (1%)
    pallas_call x6, Pallas kernels, comm_call(): pl.pallas_call(kernel, in_specs=spaces, out_specs=[pl.BlockSpec(memory_sp...  153 us
    pallas_call x1, Pallas kernels, token_sums(): pl.pallas_call(functools.partial(token_sums_kernel, grid, n), in_specs=[v...  61 us
    pallas_call x1, Pallas kernels, scan_backward(): pl.pallas_call(functools.partial(backward_kernel, cd, tc), grid=(sg, nch)...  44.8 us
    dot_general x5, matrix products, contract_rows(): lax.dot_general(left, right, (((0,), (0,)), ((), ())), preferred_element_...  30.9 us
    pallas_call x1, Pallas kernels, scan_forward(): pl.pallas_call(functools.partial(forward_kernel, cd, tc), grid=(sg, nch),...  29.8 us
    dot_general x5, matrix products, dot(): return jnp.dot(left, right, preferred_element_type=F32)  28 us
    dot_general x5, matrix products, contract_cols(): lax.dot_general(left, right, (((1,), (1,)), ((), ())), preferred_element_...  25.2 us
    pallas_call x1, Pallas kernels, scan_ends(): pl.pallas_call(functools.partial(ends_kernel, cd, tc), grid=(sg, nch), in...  24 us
  transfers between devices with their start and end apart: 13, of which 2 were waited for; matrix products, arithmetic and copies ran while one was open for 18% of the time, Pallas kernels for 16%

profile of v3, /device:TPU:0, one launch (start us, length us, event | category | flops | bytes accessed | tf_op | source)
XLA Modules:
  0.0 527.6 jit_solution(4614518138318937449)
XLA Ops:
  1.5 3.4 concatenate.77.sm_ref
  4.9 1.3 convert_element_type.206.refs_0_
  6.2 1.2 copy-done
  7.4 1.6 copy-done.2
  9.0 1.2 copy-done.5
  10.2 95.2 %gather_weights_and_tokens.1 = (bf16[8,256,2048]{2,1,0:T(8,128)(2,1)S(1)}, bf16[8,256,2048]{2,1,0:T(8,128)(2,1)}, bf16[32,64,1024]{2,1,0:T(8,128)(2,1)S(1)}, bf1...) custom-call(bf16[256,2048]{1,0:T(8,128)(2,1)S(1)} %bitcast.285, f32[8,128]{1,0:T(8,128)S(1)} %broadcast_in_dim.85.g_ref, ...), custom_call_target="tpu_custom_call" | custom-call | tf_op jit(solution)/shard_map/gather_weights_and_tokens/pallas_call | solution.py:57
  105.4 9.0 %convolution_convert_fusion.1 = bf16[2048,1024]{1,0:T(8,128)(2,1)S(1)} fusion(bf16[2048,2048]{1,0:T(8,128)(2,1)S(1)} %bitcast.310, bf16[2048,1024]{1,0:T(8,128)(2,1)S(1)} %bitcast.312), kind=kOutput, calls=%fused_computation.49 | convolution fusion | flops 8592031744 | bytes 16777216 | tf_op jit(solution)/shard_map/dot_general | solution.py:949
  114.5 2.0 copy-done.35
  116.5 2.5 conv_edges.1
  119.0 3.2 collective-permute-start.2
  122.9 1.2 collective-permute-start
  124.1 4.6 copy.115
  128.7 1.9 copy-done.25
  130.7 1.6 slice.316
  132.4 2.2 maximum_convert_fusion
  134.7 2.6 convert_bitcast_fusion.1
  137.4 1.3 copy-done.31
  139.4 20.3 %plane_sum.2 = (bf16[2048,128]{1,0:T(8,128)(2,1)S(1)}, bf16[2048,128]{1,0:T(8,128)(2,1)S(1)}) custom-call(f32[2048,256]{1,0:T(8,128)S(1)} %fusion.47.part_ref), custom_call_target="tpu_custom_call" | custom-call | tf_op jit(solution)/shard_map/plane_sum/pallas_call | solution.py:57
  159.7 6.4 %fusion.72 = (f32[256,8,512]{2,1,0:T(8,128)}, f32[256,8,512]{2,1,0:T(8,128)}, f32[2048,512]{1,0:T(8,128)}) fusion(f32[256,8,512]{2,1,0:T(8,128)S(1)} %get-tuple-element.158, f32[512]{0:T(512)S(1)} %bitcast.378, bf16[2048,128]{1,0:T(8,128)(2,1)S(1)} %get-tuple-element.80, bf16[128,512]{0,1:T(8,128)(2,1)S(1)} %bitcast.348), kind=kOutput, calls=%fused_computation.200 | convolution fusion | flops 282066944 | bytes 17434624 | tf_op jit(solution)/shard_map/dot_general | solution.py:949
  166.2 1.4 collective-permute-done.1.refs_2_
  167.8 7.8 %fusion.82 = f32[2048,512]{1,0:T(8,128)S(1)} fusion(bf16[2048,2048]{1,0:T(8,128)(2,1)} %bitcast.385, bf16[512,2048]{1,0:T(8,128)(2,1)S(1)} %bitcast.290), kind=kOutput, calls=%fused_computation.206 | convolution fusion | flops 4294967296 | bytes 14680064 | tf_op jit(solution)/shard_map/dot_general | solution.py:945
  175.6 2.4 copy.114
  179.1 3.7 multiply_reduce_fusion
  182.8 24.0 %segment_ends.1 = (f32[1,128,512]{2,1,0:T(8,128)S(1)}, f32[1,128,512]{2,1,0:T(8,128)S(1)}, f32[1,8,512]{2,1,0:T(8,128)S(1)}) custom-call(f32[256,8,512]{2,1,0:T(8,128)} %get-tuple-element.81.delta_ref, f32[256,8,512]{2,1,0:T(8,128)} %get-tuple-element.82.w_ref, f32[256,8,512]{2,1,0:T(8,128)} %get-tuple-element.144.ds_ref, ...), custom_call_target="tpu_custom_call" | custom-call | tf_op jit(solution)/shard_map/segment_ends/pallas_call | solution.py:776
  208.0 11.8 %segment_states.1 = (f32[4,48,512]{2,1,0:T(8,128)S(1)}, f32[4,48,512]{2,1,0:T(8,128)S(1)}) custom-call(f32[48,512]{1,0:T(8,128)S(1)} %bitcast.296, f32[48,512]{1,0:T(8,128)S(1)} %bitcast.295), custom_call_target="tpu_custom_call" | custom-call | tf_op jit(solution)/shard_map/segment_states/pallas_call | solution.py:57
  220.8 29.8 %scan_forward.1 = (f32[256,8,512]{2,1,0:T(8,128)}, f32[1,256,128,512]{3,2,1,0:T(8,128)}, f32[256,8,128]{2,1,0:T(8,128)}) custom-call(f32[256,8,512]{2,1,0:T(8,128)} %get-tuple-element.81.delta_ref, f32[256,8,512]{2,1,0:T(8,128)} %get-tuple-element.82.w_ref, f32[256,8,512]{2,1,0:T(8,128)} %get-tuple-element.144.ds_ref, bf16[256,8,128]{2,1,0:T(8,128)(2,1)} %bitcast.288, ...), custom_call_target="tpu_custom_call" | custom-call | flops 30000001024 | bytes 90000000 | tf_op jit(solution)/shard_map/scan_forward/pallas_call | solution.py:840
  250.6 6.2 %fusion.6 = (bf16[256,8,512]{2,1,0:T(8,128)(2,1)S(1)}, bf16[256,8,512]{2,1,0:T(8,128)(2,1)S(1)}) fusion(f32[256,8,512]{2,1,0:T(8,128)} %bitcast.318, bf16[256,8,1024]{2,1,0:T(8,128)(2,1)} %bitcast.321, f32[256,8,512]{2,1,0:T(8,128)} %get-tuple-element.95, f32[512]{0:T(512)S(1)} %bitcast.376, f32[256,8,512]{2,1,0:T(8,128)S(1)} %copy-done.21), kind=kLoop, calls=%fused_computation.13 | loop fusion | flops 22020096 | bytes 18876416 | tf_op jit(solution)/shard_map/convert_element_type | solution.py:1103
  257.5 2.0 copy.50
  259.5 4.3 convolution_convert_fusion
  264.4 8.7 %convolution_convert_fusion.4 = bf16[512,2048]{1,0:T(8,128)(2,1)S(1)} fusion(bf16[2048,512]{1,0:T(8,128)(2,1)} %bitcast.339, bf16[2048,2048]{1,0:T(8,128)(2,1)} %bitcast.386), kind=kOutput, calls=%fused_computation.52 | convolution fusion | flops 4296015872 | bytes 12582912 | tf_op jit(solution)/shard_map/dot_general | solution.py:941
  273.2 8.5 %convolution_convert_fusion.3 = bf16[2048,512]{1,0:T(8,128)(2,1)S(1)} fusion(bf16[2048,2048]{1,0:T(8,128)(2,1)} %bitcast.311, bf16[2048,512]{1,0:T(8,128)(2,1)S(1)} %bitcast.336), kind=kOutput, calls=%fused_computation.51 | convolution fusion | flops 4296015872 | bytes 12582912 | tf_op jit(solution)/shard_map/dot_general | solution.py:941
  281.7 1.9 packed_for_planes.1
  283.6 4.0 collective-permute-start.5
  287.5 4.5 add_convert_fusion.1
  292.8 1.1 copy.82
  293.8 1.4 collective-permute-start.7
  295.2 1.2 dynamic-slice_bitcast_fusion
  298.4 1.1 copy.81
  299.6 44.8 %scan_backward.1 = (f32[256,8,512]{2,1,0:T(8,128)}, f32[256,8,512]{2,1,0:T(8,128)}, f32[256,8,128]{2,1,0:T(8,128)}, f32[1,128,512]{2,1,0:T(8,128)}) custom-call(f32[256,8,512]{2,1,0:T(8,128)} %get-tuple-element.81.delta_ref, f32[256,8,512]{2,1,0:T(8,128)} %get-tuple-element.82.w_ref, f32[256,8,512]{2,1,0:T(8,128)} %get-tuple-element.144.ds_ref, ...), custom_call_target="tpu_custom_call" | custom-call | flops 1000000000 | bytes 1000000 | tf_op jit(solution)/shard_map/scan_backward/pallas_call | solution.py:917
  345.5 7.6 %fusion.74 = (f32[512]{0:T(512)S(1)}, bf16[256,8,512]{2,1,0:T(8,128)(2,1)S(1)}) fusion(f32[2048,512]{1,0:T(8,128)} %get-tuple-element.198, f32[512]{0:T(512)S(1)} %bitcast.379, f32[256,8,512]{2,1,0:T(8,128)} %get-tuple-element.111, f32[256,8,512]{2,1,0:T(8,128)} %copy-done.19, f32[256,8,512]{2,1,0:T(8,128)} %get-tuple-element.112), kind=kLoop, calls=%fused_computation.201 | loop fusion | flops 15728128 | bytes 18878464 | tf_op jit(solution)/shard_map/reduce_sum | solution.py:1142
  354.5 19.5 %plane_sum.3 = bf16[2048,256]{1,0:T(8,128)(2,1)S(1)} custom-call(f32[2048,256]{1,0:T(8,128)S(1)} %pad_maximum_fusion.5.part_ref), custom_call_target="tpu_custom_call" | custom-call | tf_op jit(solution)/shard_map/plane_sum/pallas_call | solution.py:57
  374.0 4.2 collective-permute-done.8
  378.2 3.7 fusion.11
  382.0 3.9 convert_add_fusion.1
  387.9 4.0 conv_grad_edges.1
  391.9 2.4 copy.87
  394.3 2.8 maximum_maximum_fusion
  397.8 4.5 multiply_reduce_fusion.1
  403.1 3.0 copy-done.16
  406.1 7.8 %convolution_convert_fusion.2 = bf16[2048,1024]{1,0:T(8,128)(2,1)} fusion(bf16[2048,512]{1,0:T(8,128)(2,1)} %bitcast.335, bf16[2048,512]{1,0:T(8,128)(2,1)S(1)} %bitcast.341, bf16[2048,1024]{1,0:T(8,128)(2,1)S(1)} %bitcast.313, s32[]{:T(128)S(6)} %select_n.189), kind=kOutput, calls=%fused_computation.50 | convolution fusion | flops 4305453056 | bytes 10485764 | tf_op jit(solution)/shard_map/dot_general | solution.py:945
  415.4 1.4 collective-permute-start.10
  417.2 1.1 dynamic-slice_bitcast_fusion.2
  418.9 4.0 copy.58
  424.1 2.5 fusion.83
  428.9 10.5 %bitcast_convert_fusion = bf16[2048,512]{1,0:T(8,128)(2,1)} fusion(bf16[8,256,2048]{2,1,0:T(8,128)(2,1)} %copy-done.14, bf16[8,256,512]{2,0,1:T(8,128)(2,1)S(1)} %bitcast.325), kind=kOutput, calls=%fused_computation.22 | convolution fusion | flops 4296015872 | bytes 12582912 | tf_op jit(solution)/shard_map/dot_general | solution.py:941
  439.3 8.2 %add_convert_fusion = bf16[2048,1024]{1,0:T(8,128)(2,1)} fusion(bf16[2048,1024]{1,0:T(8,128)(2,1)} %collective-permute-done.9, bf16[2048,512]{1,0:T(8,128)(2,1)S(1)} %bitcast.337, bf16[2048,512]{1,0:T(8,128)(2,1)S(1)} %bitcast.342, bf16[2048,1024]{1,0:T(8,128)(2,1)S(1)} %bitcast.314, s32[]{:T(128)S(6)} %select_n.188), kind=kOutput, calls=%fused_computation.1 | convolution fusion | flops 4309647360 | bytes 14680068 | tf_op jit(solution)/shard_map/dot_general | solution.py:945
  447.6 61.0 %token_sums.1 = (bf16[2,256,1024]{2,1,0:T(8,128)(2,1)}, bf16[8,64,512]{2,1,0:T(8,128)(2,1)}, bf16[8,64,512]{2,1,0:T(8,128)(2,1)}, bf16[4,288,128]{2,1,0:T(8,128)(2,1)}, f32[4,32,128]{2,1,0:T(8,128)}) custom-call(bf16[4,2,256,1024]{3,2,1,0:T(8,128)(2,1)} %bitcast.387, bf16[4,8,64,512]{3,2,1,0:T(8,128)(2,1)} %bitcast.388, bf16[8,64,512]{2,1,0:T(8,128)(2,1)} %bitcast.350, ...), custom_call_target="tpu_custom_call" | custom-call | flops 44999999488 | bytes 100000000 | tf_op jit(solution)/shard_map/token_sums/pallas_call | solution.py:554
  512.3 1.2 stack.41
  513.5 1.2 stack.42
  514.7 1.2 convert_add_fusion.3
  515.9 1.2 convert_add_fusion.2
  518.0 1.2 copy.62
  519.3 2.9 multiply_reduce_fusion.5
  524.9 2.2 fusion.26
  (247 shorter events, 28.6 us)
Async XLA Ops:
  105.4 9.1 %copy-start.14 = (bf16[8,256,2048]{2,1,0:T(8,128)(2,1)}, bf16[8,256,2048]{2,1,0:T(8,128)(2,1)S(1)}, u32[]{:S(2)}) copy-start(bf16[8,256,2048]{2,1,0:T(8,128)(2,1)S(1)} %get-tuple-element.75) | copy-start | bytes 25165828
  105.4 9.1 %copy-start.15 = (bf16[32,64,1024]{2,1,0:T(8,128)(2,1)}, bf16[32,64,1024]{2,1,0:T(8,128)(2,1)S(1)}, u32[]{:S(2)}) copy-start(bf16[32,64,1024]{2,1,0:T(8,128)(2,1)S(1)} %get-tuple-element.76) | copy-start | bytes 12582916
  105.4 60.7 %copy-start.13 = (bf16[4,320,128]{2,1,0:T(8,128)(2,1)}, bf16[4,320,128]{2,1,0:T(8,128)(2,1)S(1)}, u32[]{:S(2)}) copy-start(bf16[4,320,128]{2,1,0:T(8,128)(2,1)S(1)} %get-tuple-element.74) | copy-start | bytes 983044
  119.0 47.2 %collective-permute-start.2 = (bf16[128,2048]{1,0:T(8,128)(2,1)S(1)}, bf16[128,2048]{1,0:T(8,128)(2,1)S(1)}, u32[]{:S(2)}, u32[]{:S(2)}) collective-permute-start(bf16[128,2048]{1,0:T(8,128)(2,1)S(1)} %convert_element_type.206.refs_0_), channel_id=1, source_target_pairs={{0,24},{2,26},{4,28},{6,30},{8,0},{10,2},{12,4},{14,6},{16,8},{18,... | collective-permute-start | bytes 1572872 | tf_op jit(solution)/shard_map/ppermute | solution.py:954
  122.3 45.4 %collective-permute-start.1 = (bf16[128,2048]{1,0:T(8,128)(2,1)S(1)}, bf16[128,2048]{1,0:T(8,128)(2,1)S(1)}, u32[]{:S(2)}, u32[]{:S(2)}) collective-permute-start(bf16[128,2048]{1,0:T(8,128)(2,1)S(1)} %convert_element_type.206.refs_0_), channel_id=1, source_target_pairs={{0,16},{2,18},{4,20},{6,22},{8,24},{10,26},{12,28},{14,30},{16,0},... | collective-permute-start | bytes 1572872 | tf_op jit(solution)/shard_map/ppermute | solution.py:954
  122.9 44.8 %collective-permute-start = (bf16[128,2048]{1,0:T(8,128)(2,1)S(1)}, bf16[128,2048]{1,0:T(8,128)(2,1)S(1)}, u32[]{:S(2)}, u32[]{:S(2)}) collective-permute-start(bf16[128,2048]{1,0:T(8,128)(2,1)S(1)} %convert_element_type.206.refs_0_), channel_id=1, source_target_pairs={{0,8},{2,10},{4,12},{6,14},{8,16},{10,18},{12,20},{14,22},{16,24},... | collective-permute-start | bytes 1572872 | tf_op jit(solution)/shard_map/ppermute | solution.py:954
  124.1 13.3 %copy-start.54 = (bf16[160,512]{1,0:T(8,128)(2,1)}, bf16[160,512]{1,0:T(8,128)(2,1)S(1)}, u32[]{:S(2)}) copy-start(bf16[160,512]{1,0:T(8,128)(2,1)S(1)} %copy_bitcast_fusion.7) | copy-start | bytes 491524
  132.2 5.1 copy-start.62
  132.2 5.1 copy-start.64
  132.2 5.1 copy-start.66
  132.3 5.1 copy-start.68
  132.4 27.3 %copy-start.56 = (bf16[128,4,128]{0,2,1:T(8,128)(2,1)}, bf16[128,4,128]{0,2,1:T(8,128)(2,1)S(1)}, u32[]{:S(2)}) copy-start(bf16[128,4,128]{0,2,1:T(8,128)(2,1)S(1)} %copy.43) | copy-start | bytes 393220
  137.4 22.3 %copy-start.19 = (f32[256,8,512]{2,1,0:T(8,128)}, f32[256,8,512]{2,1,0:T(8,128)S(1)}, u32[]{:S(2)}) copy-start(f32[256,8,512]{2,1,0:T(8,128)S(1)} %get-tuple-element.158) | copy-start | bytes 12582916
  159.7 6.4 %copy-start.11 = (bf16[2048,128]{1,0:T(8,128)(2,1)}, bf16[2048,128]{1,0:T(8,128)(2,1)S(1)}, u32[]{:S(2)}) copy-start(bf16[2048,128]{1,0:T(8,128)(2,1)S(1)} %get-tuple-element.80) | copy-start | bytes 1572868
  159.7 23.1 %copy-start.8 = (bf16[2048,128]{1,0:T(8,128)(2,1)}, bf16[2048,128]{1,0:T(8,128)(2,1)S(1)}, u32[]{:S(2)}) copy-start(bf16[2048,128]{1,0:T(8,128)(2,1)S(1)} %get-tuple-element.89) | copy-start | bytes 1572868
  166.1 53.7 %copy-start.58 = (f32[16,512]{1,0:T(8,128)}, f32[16,512]{1,0:T(8,128)S(1)}, u32[]{:S(2)}) copy-start(f32[16,512]{1,0:T(8,128)S(1)} %copy_bitcast_fusion.9) | copy-start | bytes 98308
  166.2 16.6 %copy-start.7 = (f32[128,512]{1,0:T(8,128)}, f32[128,512]{1,0:T(8,128)S(1)}, u32[]{:S(2)}) copy-start(f32[128,512]{1,0:T(8,128)S(1)} %broadcast_bitcast_fusion.rate_ref) | copy-start | bytes 786436
  167.8 7.8 %copy-start.9 = (bf16[4,128,2048]{2,1,0:T(8,128)(2,1)}, bf16[4,128,2048]{2,1,0:T(8,128)(2,1)S(1)}, u32[]{:S(2)}) copy-start(bf16[4,128,2048]{2,1,0:T(8,128)(2,1)S(1)} %in_place_order.1) | copy-start | bytes 6291460
  178.1 4.7 copy-start.24
  179.1 3.7 copy-start.4
  206.9 43.6 %copy-start.37 = (f32[4,2,16,512]{3,2,1,0:T(8,128)}, f32[4,2,16,512]{3,2,1,0:T(8,128)S(1)}, u32[]{:S(2)}) copy-start(f32[4,2,16,512]{3,2,1,0:T(8,128)S(1)} %multiply_exponential_fusion) | copy-start | bytes 786436
  220.8 29.8 %copy-start.21 = (f32[256,8,512]{2,1,0:T(8,128)S(1)}, f32[256,8,512]{2,1,0:T(8,128)}, u32[]{:S(2)}) copy-start(f32[256,8,512]{2,1,0:T(8,128)} %copy-done.19) | copy-start | bytes 12582916
  257.5 6.4 %copy-start.41 = (bf16[8,256,512]{2,1,0:T(8,128)(2,1)}, bf16[8,256,512]{2,1,0:T(8,128)(2,1)S(1)}, u32[]{:S(2)}) copy-start(bf16[8,256,512]{2,1,0:T(8,128)(2,1)S(1)} %copy.49) | copy-start | bytes 6291460
  263.8 23.7 %collective-permute-start.3 = (bf16[2048,1024]{1,0:T(8,128)(2,1)}, bf16[2048,1024]{1,0:T(8,128)(2,1)}, u32[]{:S(2)}, u32[]{:S(2)}) collective-permute-start(bf16[2048,1024]{1,0:T(8,128)(2,1)} %convolution_convert_fusion), channel_id=1, source_target_pairs={{0,2},{2,0},{4,6},{6,4},{8,10},{10,8},{12,14},{14,12},{16,18},{18,... | collective-permute-start | bytes 12582920 | tf_op jit(solution)/shard_map/ppermute | solution.py:958
  264.4 8.7 %copy-start.39 = (bf16[8,256,512]{2,1,0:T(8,128)(2,1)S(1)}, bf16[8,256,512]{2,1,0:T(8,128)(2,1)}, u32[]{:S(2)}) copy-start(bf16[8,256,512]{2,1,0:T(8,128)(2,1)} %copy.50) | copy-start | bytes 6291460
  281.6 5.9 %copy-start.42 = (bf16[8,256,512]{2,1,0:T(8,128)(2,1)S(1)}, bf16[8,256,512]{2,1,0:T(8,128)(2,1)}, u32[]{:S(2)}) copy-start(bf16[8,256,512]{2,1,0:T(8,128)(2,1)} %copy-done.41) | copy-start | bytes 6291460
  283.5 60.9 %collective-permute-start.4 = (bf16[1024,512]{1,0:T(8,128)(2,1)}, bf16[1024,512]{1,0:T(8,128)(2,1)}, u32[]{:S(2)}, u32[]{:S(2)}) collective-permute-start(bf16[1024,512]{1,0:T(8,128)(2,1)} %get-tuple-element.109), channel_id=1, source_target_pairs={{0,8},{2,10},{4,12},{6,14},{8,16},{10,18},{12,20},{14,22},{16,24},... | collective-permute-start | bytes 3145736 | tf_op jit(solution)/shard_map/ppermute | solution.py:954
  283.6 60.9 %collective-permute-start.5 = (bf16[1024,512]{1,0:T(8,128)(2,1)}, bf16[1024,512]{1,0:T(8,128)(2,1)}, u32[]{:S(2)}, u32[]{:S(2)}) collective-permute-start(bf16[1024,512]{1,0:T(8,128)(2,1)} %get-tuple-element.110), channel_id=1, source_target_pairs={{0,24},{2,26},{4,28},{6,30},{8,0},{10,2},{12,4},{14,6},{16,8},{18,... | collective-permute-start | bytes 3145736 | tf_op jit(solution)/shard_map/ppermute | solution.py:954
  292.7 4.4 copy-start.1
  292.7 4.7 copy-start.38
  292.8 4.7 copy-start.47
  292.8 4.7 copy-start.59
  293.8 50.6 %collective-permute-start.7 = (bf16[2,2,128,1024]{3,2,0,1:T(8,128)(2,1)}, bf16[2,2,128,1024]{3,2,0,1:T(8,128)(2,1)S(1)}, u32[]{:S(2)}, u32[]{:S(2)}) collective-permute-start(bf16[2,2,128,1024]{3,2,0,1:T(8,128)(2,1)} %copy.82), channel_id=1, source_target_pairs={{0,4},{2,6},{4,0},{6,2},{8,12},{10,14},{12,8},{14,10},{16,20},{18,... | collective-permute-start | bytes 3145736 | tf_op jit(solution)/shard_map/ppermute | solution.py:958
  296.4 48.0 %collective-permute-start.6 = (bf16[4,128,1024]{2,1,0:T(8,128)(2,1)}, bf16[4,128,1024]{2,1,0:T(8,128)(2,1)S(1)}, u32[]{:S(2)}, u32[]{:S(2)}) collective-permute-start(bf16[4,128,1024]{2,1,0:T(8,128)(2,1)} %get-tuple-element.166), channel_id=1, source_target_pairs={{0,1},{1,0},{2,3},{3,2},{4,5},{5,4},{6,7},{7,6},{8,9},{9,8},{10,11... | collective-permute-start | bytes 3145736 | tf_op jit(solution)/shard_map/ppermute | solution.py:1119
  298.4 79.7 %collective-permute-start.8 = (bf16[1024,512]{1,0:T(8,128)(2,1)}, bf16[1024,512]{1,0:T(8,128)(2,1)}, u32[]{:S(2)}, u32[]{:S(2)}) collective-permute-start(bf16[1024,512]{1,0:T(8,128)(2,1)} %get-tuple-element.114), channel_id=1, source_target_pairs={{0,16},{2,18},{4,20},{6,22},{8,24},{10,26},{12,28},{14,30},{16,0},... | collective-permute-start | bytes 3145736 | tf_op jit(solution)/shard_map/ppermute | solution.py:954
  344.4 8.6 %copy-start.48 = (bf16[2,2,128,1024]{3,2,0,1:T(8,128)(2,1)}, bf16[2,2,128,1024]{3,2,0,1:T(8,128)(2,1)S(1)}, u32[]{:S(2)}) copy-start(bf16[2,2,128,1024]{3,2,0,1:T(8,128)(2,1)S(1)} %collective-permute-done.7) | copy-start | bytes 3145732
  345.5 7.6 %copy-start.57 = (bf16[128,4,128]{0,2,1:T(8,128)(2,1)S(1)}, bf16[128,4,128]{0,2,1:T(8,128)(2,1)}, u32[]{:S(2)}) copy-start(bf16[128,4,128]{0,2,1:T(8,128)(2,1)} %copy-done.56) | copy-start | bytes 393220
  345.5 8.9 %copy-start.53 = (f32[256,8,128]{2,1,0:T(8,128)S(1)}, f32[256,8,128]{2,1,0:T(8,128)}, u32[]{:S(2)}) copy-start(f32[256,8,128]{2,1,0:T(8,128)} %get-tuple-element.113) | copy-start | bytes 3145732
  345.5 32.7 %copy-start.30 = (f32[256,8,512]{2,1,0:T(8,128)S(1)}, f32[256,8,512]{2,1,0:T(8,128)}, u32[]{:S(2)}) copy-start(f32[256,8,512]{2,1,0:T(8,128)} %get-tuple-element.81.delta_ref) | copy-start | bytes 12582916
  353.1 25.1 %copy-start.23 = (f32[256,8,512]{2,1,0:T(8,128)S(1)}, f32[256,8,512]{2,1,0:T(8,128)}, u32[]{:S(2)}) copy-start(f32[256,8,512]{2,1,0:T(8,128)} %get-tuple-element.144.ds_ref) | copy-start | bytes 12582916
  354.4 23.8 %copy-start.22 = (f32[256,8,512]{2,1,0:T(8,128)S(1)}, f32[256,8,512]{2,1,0:T(8,128)}, u32[]{:S(2)}) copy-start(f32[256,8,512]{2,1,0:T(8,128)} %copy-done.19) | copy-start | bytes 12582916
  354.4 23.8 %copy-start.55 = (bf16[160,512]{1,0:T(8,128)(2,1)S(1)}, bf16[160,512]{1,0:T(8,128)(2,1)}, u32[]{:S(2)}) copy-start(bf16[160,512]{1,0:T(8,128)(2,1)} %copy-done.54) | copy-start | bytes 491524
  381.9 3.9 copy-start.28
  391.8 5.3 %slice-start = ((s8[4243456]{0:T(1024)(128)(4,1)}), s8[4194304]{0:T(1024)(128)(4,1)S(1)}, s32[]{:S(2)}) async-start(s8[4243456]{0:T(1024)(128)(4,1)} %bitcast.315), calls=%async_computation | async-start | bytes 8388608
  394.3 3.5 copy-start.29
  394.3 3.5 copy-start.63
  394.3 3.5 copy-start.65
  394.3 3.5 copy-start.67
  402.4 11.5 %copy-start.32 = (bf16[256,8,512]{2,1,0:T(8,128)(2,1)}, bf16[256,8,512]{2,1,0:T(8,128)(2,1)S(1)}, u32[]{:S(2)}) copy-start(bf16[256,8,512]{2,1,0:T(8,128)(2,1)S(1)} %get-tuple-element.161) | copy-start | bytes 6291460
  402.4 3.7 copy-start.16
  403.1 10.9 %copy-start.43 = (bf16[8,256,512]{2,1,0:T(8,128)(2,1)}, bf16[8,256,512]{2,1,0:T(8,128)(2,1)S(1)}, u32[]{:S(2)}) copy-start(bf16[8,256,512]{2,1,0:T(8,128)(2,1)S(1)} %copy.55) | copy-start | bytes 6291460
  406.1 7.9 %copy-start.51 = (bf16[4,128,1024]{2,1,0:T(8,128)(2,1)S(1)}, bf16[4,128,1024]{2,1,0:T(8,128)(2,1)}, u32[]{:S(2)}) copy-start(bf16[4,128,1024]{2,1,0:T(8,128)(2,1)} %copy-done.50) | copy-start | bytes 3145732
  414.0 25.4 %collective-permute-start.9 = (bf16[2048,1024]{1,0:T(8,128)(2,1)}, bf16[2048,1024]{1,0:T(8,128)(2,1)}, u32[]{:S(2)}, u32[]{:S(2)}) collective-permute-start(bf16[2048,1024]{1,0:T(8,128)(2,1)} %convolution_convert_fusion.2), channel_id=1, source_target_pairs={{0,2},{2,0},{4,6},{6,4},{8,10},{10,8},{12,14},{14,12},{16,18},{18,... | collective-permute-start | bytes 12582920 | tf_op jit(solution)/shard_map/ppermute | solution.py:958
  415.4 7.6 %copy-start.60 = (f32[1,128,512]{2,1,0:T(8,128)S(1)}, f32[1,128,512]{2,1,0:T(8,128)}, u32[]{:S(2)}) copy-start(f32[1,128,512]{2,1,0:T(8,128)} %get-tuple-element.129) | copy-start | bytes 786436
  415.4 32.2 %collective-permute-start.10 = (bf16[2,128,1024]{2,1,0:T(8,128)(2,1)}, bf16[2,128,1024]{2,1,0:T(8,128)(2,1)}, u32[]{:S(2)}, u32[]{:S(2)}) collective-permute-start(bf16[2,128,1024]{2,1,0:T(8,128)(2,1)} %get-tuple-element.176), channel_id=1, source_target_pairs={{0,4},{2,6},{4,0},{6,2},{8,12},{10,14},{12,8},{14,10},{16,20},{18,... | collective-permute-start | bytes 1572872 | tf_op jit(solution)/shard_map/ppermute | solution.py:958
  418.3 29.3 %collective-permute-start.11 = (bf16[2,128,1024]{2,1,0:T(8,128)(2,1)}, bf16[2,128,1024]{2,1,0:T(8,128)(2,1)}, u32[]{:S(2)}, u32[]{:S(2)}) collective-permute-start(bf16[2,128,1024]{2,1,0:T(8,128)(2,1)} %get-tuple-element.174), channel_id=1, source_target_pairs={{0,1},{1,0},{2,3},{3,2},{4,5},{5,4},{6,7},{7,6},{8,9},{9,8},{10,11... | collective-permute-start | bytes 1572872 | tf_op jit(solution)/shard_map/ppermute | solution.py:1119
  418.9 7.7 %copy-start.12 = (bf16[2048,128]{1,0:T(8,128)(2,1)S(1)}, bf16[2048,128]{1,0:T(8,128)(2,1)}, u32[]{:S(2)}) copy-start(bf16[2048,128]{1,0:T(8,128)(2,1)} %copy-done.11) | copy-start | bytes 1572868
  424.1 4.7 copy-start.33
  428.8 10.5 %copy-start.17 = (bf16[32,64,1024]{2,1,0:T(8,128)(2,1)S(1)}, bf16[32,64,1024]{2,1,0:T(8,128)(2,1)}, u32[]{:S(2)}) copy-start(bf16[32,64,1024]{2,1,0:T(8,128)(2,1)} %copy-done.15) | copy-start | bytes 12582916
  428.8 10.5 %copy-start.40 = (bf16[8,256,512]{2,1,0:T(8,128)(2,1)S(1)}, bf16[8,256,512]{2,1,0:T(8,128)(2,1)}, u32[]{:S(2)}) copy-start(bf16[8,256,512]{2,1,0:T(8,128)(2,1)} %copy.50) | copy-start | bytes 6291460
  428.8 10.5 %copy-start.44 = (bf16[8,256,512]{2,1,0:T(8,128)(2,1)S(1)}, bf16[8,256,512]{2,1,0:T(8,128)(2,1)}, u32[]{:S(2)}) copy-start(bf16[8,256,512]{2,1,0:T(8,128)(2,1)} %copy-done.43) | copy-start | bytes 6291460
  508.6 7.3 %copy-start.45 = (bf16[2,128,1024]{2,1,0:T(8,128)(2,1)S(1)}, bf16[2,128,1024]{2,1,0:T(8,128)(2,1)}, u32[]{:S(2)}) copy-start(bf16[2,128,1024]{2,1,0:T(8,128)(2,1)} %get-tuple-element.122) | copy-start | bytes 1572868
  517.2 7.6 %collective-permute-start.12 = (bf16[256,1024]{1,0:T(8,128)(2,1)S(1)}, bf16[256,1024]{1,0:T(8,128)(2,1)S(1)}, u32[]{:S(2)}, u32[]{:S(2)}) collective-permute-start(bf16[256,1024]{1,0:T(8,128)(2,1)S(1)} %fusion.44), channel_id=1, source_target_pairs={{0,2},{2,0},{4,6},{6,4},{8,10},{10,8},{12,14},{14,12},{16,18},{18,... | collective-permute-start | bytes 1572872 | tf_op jit(solution)/shard_map/ppermute | solution.py:958
  519.2 3.7 copy-start.61
  (22 other events, 48.6 us)

commit v4 on v3

--- a/solution.py
+++ b/solution.py
@@ -472,7 +472,7 @@
         row_copies.append(remote(rows_ref.at[j], row_in.at[d], f_send.at[d], f_recv.at[d], grid.at(j, q, f)))
     for copy in row_copies + x_copies + [y_copy]:
         copy.start()
-    mine, pushes, waits = [], [], []
+    mine, pushes, waits, late = [], [], [], []
     for d in range(1, C):
         j, back = lax.rem(me + d, C), lax.rem(me + C - d, C)
         pushes.append(remote(gate_ref.at[j], gate_out.at[me], g_send.at[d], g_recv.at[d], grid.member(z, j)))
@@ -482,7 +482,7 @@
         mine.append(pltpu.make_async_copy(ins[i].at[z], outs[i].at[z], local.at[i]))
         for d in range(1, Z):
             j, back = lax.rem(z + d, Z), lax.rem(z + Z - d, Z)
-            pushes.append(remote(ins[i].at[j], outs[i].at[z], l_send.at[i, d], l_recv.at[i, d], grid.at(j, q, f)))
+            late.append(remote(ins[i].at[j], outs[i].at[z], l_send.at[i, d], l_recv.at[i, d], grid.at(j, q, f)))
             waits.append(remote(ins[i].at[z], outs[i].at[back], l_send.at[i, d], l_recv.at[i, d], grid.at(back, q, f)))
     for copy in pushes + mine:
         copy.start()
@@ -518,6 +518,8 @@
     t_copy.start()
     for copy in row_copies:
         copy.wait_recv()
+    for copy in late:
+        copy.start()
 
     @pl.loop(0, C)
     def _(j):
@@ -540,7 +542,7 @@
         copy.wait()
     for copy in waits:
         copy.wait_recv()
-    for copy in x_copies + [y_copy, a_copy, t_copy] + b_copies + row_copies + pushes:
+    for copy in x_copies + [y_copy, a_copy, t_copy] + b_copies + row_copies + pushes + late:
         copy.wait_send()
 
 
@@ -1070,16 +1072,16 @@
     adj = adjoints[3]
     for c in reversed(range(3)):
         adj = kept[c] * adj + adjoints[c]
-    plane_total = jnp.broadcast_to(jnp.sum(totals, axis=0), (F, 8, chans))
+    plane_total = jnp.pad(jnp.sum(totals, axis=0).reshape(F, chans), ((0, -F % 8), (0, 0)))
 
     def with_total(value):
-        return jnp.concatenate([value, plane_total], axis=1).reshape(F * (STATE + 8), chans)
+        return jnp.concatenate([value.reshape(F * STATE, chans), plane_total], axis=0)
 
     ups, downs = exchange_states(grid, with_total(end), with_total(adj), 5)
-    ups, downs = ups.reshape(Z, F, STATE + 8, chans), downs.reshape(Z, F, STATE + 8, chans)
 
     def through(received, p, value):
-        return jnp.exp(decay_rate * received[p, :, STATE:STATE + 1]) * value + received[p, :, :STATE]
+        total_steps = received[p, F * STATE:F * STATE + F].reshape(F, 1, chans)
+        return jnp.exp(decay_rate * total_steps) * value + received[p, :F * STATE].reshape(F, STATE, chans)
 
     state = jnp.zeros((F, STATE, chans), F32)
     adj = state

time: 537 us -> 534 us (level)
    unnamed x154 -> x146, local copies, waits for them, and re-layouts: 17.5 us -> 16.1 us
where the time goes in v4:
time: 534 us; the launch traced here: 527 us
  Pallas kernels  315 us (59%)
  matrix products  82.6 us (15%)
  local copies, waits for them, and re-layouts  54.1 us (10%)
  other arithmetic  51.7 us (10%)
  starting transfers between devices  13.2 us (2%)
  waiting for transfers between devices  7.9 us (1%)
    pallas_call x6, Pallas kernels, comm_call(): pl.pallas_call(kernel, in_specs=spaces, out_specs=[pl.BlockSpec(memory_sp...  152 us
    pallas_call x1, Pallas kernels, token_sums(): pl.pallas_call(functools.partial(token_sums_kernel, grid, n), in_specs=[v...  62.7 us
    pallas_call x1, Pallas kernels, scan_backward(): pl.pallas_call(functools.partial(backward_kernel, cd, tc), grid=(sg, nch)...  45 us
    dot_general x5, matrix products, contract_rows(): lax.dot_general(left, right, (((0,), (0,)), ((), ())), preferred_element_...  31 us
    pallas_call x1, Pallas kernels, scan_forward(): pl.pallas_call(functools.partial(forward_kernel, cd, tc), grid=(sg, nch),...  29.7 us
    dot_general x5, matrix products, dot(): return jnp.dot(left, right, preferred_element_type=F32)  28 us
    pallas_call x1, Pallas kernels, scan_ends(): pl.pallas_call(functools.partial(ends_kernel, cd, tc), grid=(sg, nch), in...  24 us
    dot_general x5, matrix products, contract_cols(): lax.dot_general(left, right, (((1,), (1,)), ((), ())), preferred_element_...  23.6 us
  transfers between devices with their start and end apart: 13, of which 2 were waited for; matrix products, arithmetic and copies ran while one was open for 18% of the time, Pallas kernels for 16%

profile of v4, /device:TPU:0, one launch (start us, length us, event | category | flops | bytes accessed | tf_op | source)
XLA Modules:
  0.0 526.9 jit_solution(1894934447229826601)
XLA Ops:
  1.5 3.4 concatenate.77.sm_ref
  4.9 1.3 convert_element_type.208.refs_0_
  6.2 1.2 copy-done
  7.4 1.6 copy-done.3
  9.0 1.2 copy-done.6
  10.2 95.2 %gather_weights_and_tokens.1 = (bf16[8,256,2048]{2,1,0:T(8,128)(2,1)S(1)}, bf16[8,256,2048]{2,1,0:T(8,128)(2,1)}, bf16[32,64,1024]{2,1,0:T(8,128)(2,1)S(1)}, bf1...) custom-call(bf16[256,2048]{1,0:T(8,128)(2,1)S(1)} %bitcast.279, f32[8,128]{1,0:T(8,128)S(1)} %broadcast_in_dim.80.g_ref, ...), custom_call_target="tpu_custom_call" | custom-call | tf_op jit(solution)/shard_map/gather_weights_and_tokens/pallas_call | solution.py:57
  105.4 9.0 %convolution_convert_fusion.1 = bf16[2048,1024]{1,0:T(8,128)(2,1)S(1)} fusion(bf16[2048,2048]{1,0:T(8,128)(2,1)S(1)} %bitcast.298, bf16[2048,1024]{1,0:T(8,128)(2,1)S(1)} %bitcast.300), kind=kOutput, calls=%fused_computation.49 | convolution fusion | flops 8592031744 | bytes 16777216 | tf_op jit(solution)/shard_map/dot_general | solution.py:951
  114.5 2.0 copy-done.37
  116.5 2.5 conv_edges.1
  119.1 3.2 collective-permute-start.2
  122.9 1.2 collective-permute-start
  124.1 4.6 copy.103
  128.7 2.0 copy-done.27
  130.7 1.6 slice.316
  132.5 2.2 maximum_convert_fusion
  134.7 2.6 convert_bitcast_fusion.1
  137.4 1.3 copy-done.33
  139.4 20.3 %plane_sum.2 = (bf16[2048,128]{1,0:T(8,128)(2,1)S(1)}, bf16[2048,128]{1,0:T(8,128)(2,1)S(1)}) custom-call(f32[2048,256]{1,0:T(8,128)S(1)} %fusion.47.part_ref), custom_call_target="tpu_custom_call" | custom-call | tf_op jit(solution)/shard_map/plane_sum/pallas_call | solution.py:57
  159.7 6.4 %fusion.66 = (f32[256,8,512]{2,1,0:T(8,128)}, f32[256,8,512]{2,1,0:T(8,128)}, f32[2048,512]{1,0:T(8,128)}) fusion(f32[256,8,512]{2,1,0:T(8,128)S(1)} %get-tuple-element.158, f32[512]{0:T(512)S(1)} %bitcast.370, bf16[2048,128]{1,0:T(8,128)(2,1)S(1)} %get-tuple-element.80, bf16[128,512]{0,1:T(8,128)(2,1)S(1)} %bitcast.340), kind=kOutput, calls=%fused_computation.190 | convolution fusion | flops 282066944 | bytes 17434624 | tf_op jit(solution)/shard_map/dot_general | solution.py:951
  166.2 1.4 collective-permute-done.1.refs_2_
  167.8 7.8 %fusion.77 = f32[2048,512]{1,0:T(8,128)S(1)} fusion(bf16[2048,2048]{1,0:T(8,128)(2,1)} %bitcast.377, bf16[512,2048]{1,0:T(8,128)(2,1)S(1)} %bitcast.284), kind=kOutput, calls=%fused_computation.199 | convolution fusion | flops 4294967296 | bytes 14680064 | tf_op jit(solution)/shard_map/dot_general | solution.py:947
  175.6 2.4 copy.102
  179.1 4.3 multiply_reduce_fusion
  183.4 24.0 %segment_ends.1 = (f32[1,128,512]{2,1,0:T(8,128)S(1)}, f32[1,128,512]{2,1,0:T(8,128)S(1)}, f32[1,8,512]{2,1,0:T(8,128)S(1)}) custom-call(f32[256,8,512]{2,1,0:T(8,128)} %get-tuple-element.81.delta_ref, f32[256,8,512]{2,1,0:T(8,128)} %get-tuple-element.82.w_ref, f32[256,8,512]{2,1,0:T(8,128)} %get-tuple-element.144.ds_ref, ...), custom_call_target="tpu_custom_call" | custom-call | tf_op jit(solution)/shard_map/segment_ends/pallas_call | solution.py:778
  208.0 10.5 %segment_states.1 = (f32[4,40,512]{2,1,0:T(8,128)S(1)}, f32[4,40,512]{2,1,0:T(8,128)S(1)}) custom-call(f32[40,512]{1,0:T(8,128)S(1)} %get-tuple-element.215.up_ref, f32[40,512]{1,0:T(8,128)S(1)} %get-tuple-element.214.down_ref), custom_call_target="tpu_custom_call" | custom-call | tf_op jit(solution)/shard_map/segment_states/pallas_call | solution.py:57
  219.5 29.7 %scan_forward.1 = (f32[256,8,512]{2,1,0:T(8,128)}, f32[1,256,128,512]{3,2,1,0:T(8,128)}, f32[256,8,128]{2,1,0:T(8,128)}) custom-call(f32[256,8,512]{2,1,0:T(8,128)} %get-tuple-element.81.delta_ref, f32[256,8,512]{2,1,0:T(8,128)} %get-tuple-element.82.w_ref, f32[256,8,512]{2,1,0:T(8,128)} %get-tuple-element.144.ds_ref, bf16[256,8,128]{2,1,0:T(8,128)(2,1)} %bitcast.282, ...), custom_call_target="tpu_custom_call" | custom-call | flops 30000001024 | bytes 90000000 | tf_op jit(solution)/shard_map/scan_forward/pallas_call | solution.py:842
  249.3 6.2 %fusion.6 = (bf16[256,8,512]{2,1,0:T(8,128)(2,1)S(1)}, bf16[256,8,512]{2,1,0:T(8,128)(2,1)S(1)}) fusion(f32[256,8,512]{2,1,0:T(8,128)} %bitcast.306, bf16[256,8,1024]{2,1,0:T(8,128)(2,1)} %bitcast.309, f32[256,8,512]{2,1,0:T(8,128)} %get-tuple-element.95, f32[512]{0:T(512)S(1)} %bitcast.368, f32[256,8,512]{2,1,0:T(8,128)S(1)} %copy-done.22), kind=kLoop, calls=%fused_computation.13 | loop fusion | flops 22020096 | bytes 18876416 | tf_op jit(solution)/shard_map/convert_element_type | solution.py:1105
  256.2 2.0 copy.50
  258.2 4.3 convolution_convert_fusion
  263.4 8.7 %convolution_convert_fusion.4 = bf16[512,2048]{1,0:T(8,128)(2,1)S(1)} fusion(bf16[2048,512]{1,0:T(8,128)(2,1)} %bitcast.327, bf16[2048,2048]{1,0:T(8,128)(2,1)} %bitcast.378), kind=kOutput, calls=%fused_computation.52 | convolution fusion | flops 4296015872 | bytes 12582912 | tf_op jit(solution)/shard_map/dot_general | solution.py:943
  272.1 8.5 %convolution_convert_fusion.3 = bf16[2048,512]{1,0:T(8,128)(2,1)S(1)} fusion(bf16[2048,2048]{1,0:T(8,128)(2,1)} %bitcast.299, bf16[2048,512]{1,0:T(8,128)(2,1)S(1)} %bitcast.323), kind=kOutput, calls=%fused_computation.51 | convolution fusion | flops 4296015872 | bytes 12582912 | tf_op jit(solution)/shard_map/dot_general | solution.py:943
  280.6 1.3 packed_for_planes.1
  281.9 4.0 collective-permute-start.5
  285.9 4.6 add_convert_fusion.1
  291.4 1.1 copy.76
  292.4 1.4 collective-permute-start.7
  293.8 1.5 dynamic-slice_bitcast_fusion
  297.0 1.1 copy.75
  298.0 45.0 %scan_backward.1 = (f32[256,8,512]{2,1,0:T(8,128)}, f32[256,8,512]{2,1,0:T(8,128)}, f32[256,8,128]{2,1,0:T(8,128)}, f32[1,128,512]{2,1,0:T(8,128)}) custom-call(f32[256,8,512]{2,1,0:T(8,128)} %get-tuple-element.81.delta_ref, f32[256,8,512]{2,1,0:T(8,128)} %get-tuple-element.82.w_ref, f32[256,8,512]{2,1,0:T(8,128)} %get-tuple-element.144.ds_ref, ...), custom_call_target="tpu_custom_call" | custom-call | flops 1000000000 | bytes 1000000 | tf_op jit(solution)/shard_map/scan_backward/pallas_call | solution.py:919
  343.1 6.1 %fusion.68 = (f32[512]{0:T(512)S(1)}, bf16[256,8,512]{2,1,0:T(8,128)(2,1)S(1)}) fusion(f32[2048,512]{1,0:T(8,128)} %get-tuple-element.216, f32[512]{0:T(512)S(1)} %bitcast.371, f32[256,8,512]{2,1,0:T(8,128)} %get-tuple-element.111, f32[256,8,512]{2,1,0:T(8,128)S(1)} %copy-done.23, f32[256,8,512]{2,1,0:T(8,128)} %get-tuple-element.112), kind=kLoop, calls=%fused_computation.191 | loop fusion | flops 15728128 | bytes 18878464 | tf_op jit(solution)/shard_map/reduce_sum | solution.py:1144
  350.6 19.5 %plane_sum.3 = bf16[2048,256]{1,0:T(8,128)(2,1)S(1)} custom-call(f32[2048,256]{1,0:T(8,128)S(1)} %pad_maximum_fusion.5.part_ref), custom_call_target="tpu_custom_call" | custom-call | tf_op jit(solution)/shard_map/plane_sum/pallas_call | solution.py:57
  370.1 6.4 %collective-permute-done.8 = bf16[1024,512]{1,0:T(8,128)(2,1)} collective-permute-done((bf16[1024,512]{1,0:T(8,128)(2,1)S(1)}, bf16[1024,512]{1,0:T(8,128)(2,1)}, u32[]{:S(2)}, u32[]{:S(2)}) %collective-permute-start.8) | collective-permute-done | bytes 1048608 | tf_op jit(solution)/shard_map/ppermute | solution.py:956
  376.5 3.7 fusion.11
  380.3 3.9 convert_add_fusion.1
  385.2 4.0 conv_grad_edges.1
  389.2 1.1 copy.81
  390.3 3.2 maximum_maximum_fusion
  394.5 5.2 multiply_reduce_fusion.1
  400.4 3.0 copy-done.17
  403.4 6.2 %convolution_convert_fusion.2 = bf16[2048,1024]{1,0:T(8,128)(2,1)} fusion(bf16[2048,512]{1,0:T(8,128)(2,1)S(1)} %bitcast.324, bf16[2048,512]{1,0:T(8,128)(2,1)S(1)} %bitcast.329, bf16[2048,1024]{1,0:T(8,128)(2,1)S(1)} %bitcast.301, s32[]{:T(128)S(6)} %select_n.225), kind=kOutput, calls=%fused_computation.50 | convolution fusion | flops 4305453056 | bytes 10485764 | tf_op jit(solution)/shard_map/dot_general | solution.py:947
  409.7 1.7 add_convert_fusion.3
  412.3 1.4 collective-permute-start.10
  413.7 1.6 add_convert_fusion.2
  416.9 4.0 copy.58
  422.7 2.5 fusion.78
  427.5 10.5 %bitcast_convert_fusion = bf16[2048,512]{1,0:T(8,128)(2,1)} fusion(bf16[8,256,2048]{2,1,0:T(8,128)(2,1)} %copy-done.15, bf16[8,256,512]{2,0,1:T(8,128)(2,1)S(1)} %bitcast.313), kind=kOutput, calls=%fused_computation.22 | convolution fusion | flops 4296015872 | bytes 12582912 | tf_op jit(solution)/shard_map/dot_general | solution.py:943
  438.0 8.2 %add_convert_fusion = bf16[2048,1024]{1,0:T(8,128)(2,1)} fusion(bf16[2048,1024]{1,0:T(8,128)(2,1)} %collective-permute-done.9, bf16[2048,512]{1,0:T(8,128)(2,1)S(1)} %bitcast.325, bf16[2048,512]{1,0:T(8,128)(2,1)S(1)} %bitcast.330, bf16[2048,1024]{1,0:T(8,128)(2,1)S(1)} %bitcast.302, s32[]{:T(128)S(6)} %select_n.224), kind=kOutput, calls=%fused_computation.1 | convolution fusion | flops 4309647360 | bytes 14680068 | tf_op jit(solution)/shard_map/dot_general | solution.py:947
  446.2 62.7 %token_sums.1 = (bf16[2,256,1024]{2,1,0:T(8,128)(2,1)}, bf16[8,64,512]{2,1,0:T(8,128)(2,1)}, bf16[8,64,512]{2,1,0:T(8,128)(2,1)}, bf16[4,288,128]{2,1,0:T(8,128)(2,1)}, f32[4,32,128]{2,1,0:T(8,128)}) custom-call(bf16[4,2,256,1024]{3,2,1,0:T(8,128)(2,1)} %bitcast.379, bf16[4,8,64,512]{3,2,1,0:T(8,128)(2,1)} %bitcast.380, bf16[8,64,512]{2,1,0:T(8,128)(2,1)} %bitcast.342, ...), custom_call_target="tpu_custom_call" | custom-call | flops 44999999488 | bytes 100000000 | tf_op jit(solution)/shard_map/token_sums/pallas_call | solution.py:556
  512.7 1.2 stack.41
  513.8 1.2 stack.42
  515.2 1.2 convert_add_fusion.2
  517.3 1.2 copy.62
  518.5 2.9 multiply_reduce_fusion.5
  524.2 2.2 fusion.26
  (243 shorter events, 27.3 us)
Async XLA Ops:
  105.4 9.1 %copy-start.15 = (bf16[8,256,2048]{2,1,0:T(8,128)(2,1)}, bf16[8,256,2048]{2,1,0:T(8,128)(2,1)S(1)}, u32[]{:S(2)}) copy-start(bf16[8,256,2048]{2,1,0:T(8,128)(2,1)S(1)} %get-tuple-element.75) | copy-start | bytes 25165828
  105.4 9.1 %copy-start.16 = (bf16[32,64,1024]{2,1,0:T(8,128)(2,1)}, bf16[32,64,1024]{2,1,0:T(8,128)(2,1)S(1)}, u32[]{:S(2)}) copy-start(bf16[32,64,1024]{2,1,0:T(8,128)(2,1)S(1)} %get-tuple-element.76) | copy-start | bytes 12582916
  105.4 60.7 %copy-start.14 = (bf16[4,320,128]{2,1,0:T(8,128)(2,1)}, bf16[4,320,128]{2,1,0:T(8,128)(2,1)S(1)}, u32[]{:S(2)}) copy-start(bf16[4,320,128]{2,1,0:T(8,128)(2,1)S(1)} %get-tuple-element.74) | copy-start | bytes 983044
  119.1 47.2 %collective-permute-start.2 = (bf16[128,2048]{1,0:T(8,128)(2,1)S(1)}, bf16[128,2048]{1,0:T(8,128)(2,1)S(1)}, u32[]{:S(2)}, u32[]{:S(2)}) collective-permute-start(bf16[128,2048]{1,0:T(8,128)(2,1)S(1)} %convert_element_type.208.refs_0_), channel_id=1, source_target_pairs={{0,24},{2,26},{4,28},{6,30},{8,0},{10,2},{12,4},{14,6},{16,8},{18,... | collective-permute-start | bytes 1572872 | tf_op jit(solution)/shard_map/ppermute | solution.py:956
  122.3 45.4 %collective-permute-start.1 = (bf16[128,2048]{1,0:T(8,128)(2,1)S(1)}, bf16[128,2048]{1,0:T(8,128)(2,1)S(1)}, u32[]{:S(2)}, u32[]{:S(2)}) collective-permute-start(bf16[128,2048]{1,0:T(8,128)(2,1)S(1)} %convert_element_type.208.refs_0_), channel_id=1, source_target_pairs={{0,16},{2,18},{4,20},{6,22},{8,24},{10,26},{12,28},{14,30},{16,0},... | collective-permute-start | bytes 1572872 | tf_op jit(solution)/shard_map/ppermute | solution.py:956
  122.9 44.8 %collective-permute-start = (bf16[128,2048]{1,0:T(8,128)(2,1)S(1)}, bf16[128,2048]{1,0:T(8,128)(2,1)S(1)}, u32[]{:S(2)}, u32[]{:S(2)}) collective-permute-start(bf16[128,2048]{1,0:T(8,128)(2,1)S(1)} %convert_element_type.208.refs_0_), channel_id=1, source_target_pairs={{0,8},{2,10},{4,12},{6,14},{8,16},{10,18},{12,20},{14,22},{16,24},... | collective-permute-start | bytes 1572872 | tf_op jit(solution)/shard_map/ppermute | solution.py:956
  124.1 13.3 %copy-start.53 = (bf16[160,512]{1,0:T(8,128)(2,1)}, bf16[160,512]{1,0:T(8,128)(2,1)S(1)}, u32[]{:S(2)}) copy-start(bf16[160,512]{1,0:T(8,128)(2,1)S(1)} %copy_bitcast_fusion.7) | copy-start | bytes 491524
  132.2 5.1 copy-start.61
  132.3 5.1 copy-start.63
  132.3 5.1 copy-start.65
  132.3 5.1 copy-start.67
  132.4 27.3 %copy-start.55 = (bf16[128,4,128]{0,2,1:T(8,128)(2,1)}, bf16[128,4,128]{0,2,1:T(8,128)(2,1)S(1)}, u32[]{:S(2)}) copy-start(bf16[128,4,128]{0,2,1:T(8,128)(2,1)S(1)} %copy.43) | copy-start | bytes 393220
  137.4 22.3 %copy-start.20 = (f32[256,8,512]{2,1,0:T(8,128)}, f32[256,8,512]{2,1,0:T(8,128)S(1)}, u32[]{:S(2)}) copy-start(f32[256,8,512]{2,1,0:T(8,128)S(1)} %get-tuple-element.158) | copy-start | bytes 12582916
  159.7 6.4 %copy-start.12 = (bf16[2048,128]{1,0:T(8,128)(2,1)}, bf16[2048,128]{1,0:T(8,128)(2,1)S(1)}, u32[]{:S(2)}) copy-start(bf16[2048,128]{1,0:T(8,128)(2,1)S(1)} %get-tuple-element.80) | copy-start | bytes 1572868
  159.7 23.7 %copy-start.9 = (bf16[2048,128]{1,0:T(8,128)(2,1)}, bf16[2048,128]{1,0:T(8,128)(2,1)S(1)}, u32[]{:S(2)}) copy-start(bf16[2048,128]{1,0:T(8,128)(2,1)S(1)} %get-tuple-element.89) | copy-start | bytes 1572868
  166.1 52.4 %copy-start.57 = (f32[16,512]{1,0:T(8,128)}, f32[16,512]{1,0:T(8,128)S(1)}, u32[]{:S(2)}) copy-start(f32[16,512]{1,0:T(8,128)S(1)} %copy_bitcast_fusion.9) | copy-start | bytes 98308
  166.2 17.2 %copy-start.8 = (f32[128,512]{1,0:T(8,128)}, f32[128,512]{1,0:T(8,128)S(1)}, u32[]{:S(2)}) copy-start(f32[128,512]{1,0:T(8,128)S(1)} %broadcast_bitcast_fusion.rate_ref) | copy-start | bytes 786436
  167.8 7.8 %copy-start.10 = (bf16[4,128,2048]{2,1,0:T(8,128)(2,1)}, bf16[4,128,2048]{2,1,0:T(8,128)(2,1)S(1)}, u32[]{:S(2)}) copy-start(bf16[4,128,2048]{2,1,0:T(8,128)(2,1)S(1)} %in_place_order.1) | copy-start | bytes 6291460
  178.1 5.3 %copy-start.26 = (f32[8,256,512]{2,0,1:T(8,128)}, f32[8,256,512]{2,0,1:T(8,128)S(1)}, u32[]{:S(2)}) copy-start(f32[8,256,512]{2,0,1:T(8,128)S(1)} %copy.102) | copy-start | bytes 12582916
  179.1 4.3 copy-start.5
  207.6 11.9 %copy-start.40 = (f32[4,2,16,512]{3,2,1,0:T(8,128)}, f32[4,2,16,512]{3,2,1,0:T(8,128)S(1)}, u32[]{:S(2)}) copy-start(f32[4,2,16,512]{3,2,1,0:T(8,128)S(1)} %multiply_exponential_fusion) | copy-start | bytes 786436
  207.8 41.4 %copy-start.49 = (f32[1,16,8,512]{3,1,2,0:T(8,128)}, f32[1,16,8,512]{3,1,2,0:T(8,128)S(1)}, u32[]{:S(2)}) copy-start(f32[1,16,8,512]{3,1,2,0:T(8,128)S(1)} %copy.106) | copy-start | bytes 786436
  219.5 29.8 %copy-start.22 = (f32[256,8,512]{2,1,0:T(8,128)S(1)}, f32[256,8,512]{2,1,0:T(8,128)}, u32[]{:S(2)}) copy-start(f32[256,8,512]{2,1,0:T(8,128)} %copy-done.20) | copy-start | bytes 12582916
  256.1 6.4 %copy-start.45 = (bf16[8,256,512]{2,1,0:T(8,128)(2,1)}, bf16[8,256,512]{2,1,0:T(8,128)(2,1)S(1)}, u32[]{:S(2)}) copy-start(bf16[8,256,512]{2,1,0:T(8,128)(2,1)S(1)} %copy.49) | copy-start | bytes 6291460
  258.2 4.9 copy-start.1
  262.5 23.4 %collective-permute-start.3 = (bf16[2048,1024]{1,0:T(8,128)(2,1)}, bf16[2048,1024]{1,0:T(8,128)(2,1)}, u32[]{:S(2)}, u32[]{:S(2)}) collective-permute-start(bf16[2048,1024]{1,0:T(8,128)(2,1)} %convolution_convert_fusion), channel_id=1, source_target_pairs={{0,2},{2,0},{4,6},{6,4},{8,10},{10,8},{12,14},{14,12},{16,18},{18,... | collective-permute-start | bytes 12582920 | tf_op jit(solution)/shard_map/ppermute | solution.py:960
  263.4 8.7 %copy-start.42 = (bf16[8,256,512]{2,1,0:T(8,128)(2,1)S(1)}, bf16[8,256,512]{2,1,0:T(8,128)(2,1)}, u32[]{:S(2)}) copy-start(bf16[8,256,512]{2,1,0:T(8,128)(2,1)} %copy.50) | copy-start | bytes 6291460
  280.6 5.3 copy-start.46
  281.9 61.1 %collective-permute-start.4 = (bf16[1024,512]{1,0:T(8,128)(2,1)S(1)}, bf16[1024,512]{1,0:T(8,128)(2,1)}, u32[]{:S(2)}, u32[]{:S(2)}) collective-permute-start(bf16[1024,512]{1,0:T(8,128)(2,1)S(1)} %get-tuple-element.109), channel_id=1, source_target_pairs={{0,8},{2,10},{4,12},{6,14},{8,16},{10,18},{12,20},{14,22},{16,24},... | collective-permute-start | bytes 3145736 | tf_op jit(solution)/shard_map/ppermute | solution.py:956
  281.9 61.1 %collective-permute-start.5 = (bf16[1024,512]{1,0:T(8,128)(2,1)}, bf16[1024,512]{1,0:T(8,128)(2,1)}, u32[]{:S(2)}, u32[]{:S(2)}) collective-permute-start(bf16[1024,512]{1,0:T(8,128)(2,1)} %get-tuple-element.110), channel_id=1, source_target_pairs={{0,24},{2,26},{4,28},{6,30},{8,0},{10,2},{12,4},{14,6},{16,8},{18,... | collective-permute-start | bytes 3145736 | tf_op jit(solution)/shard_map/ppermute | solution.py:956
  291.3 4.6 copy-start.41
  291.3 4.6 copy-start.50
  291.4 4.6 copy-start.58
  292.4 50.6 %collective-permute-start.7 = (bf16[2,2,128,1024]{3,2,0,1:T(8,128)(2,1)}, bf16[2,2,128,1024]{3,2,0,1:T(8,128)(2,1)}, u32[]{:S(2)}, u32[]{:S(2)}) collective-permute-start(bf16[2,2,128,1024]{3,2,0,1:T(8,128)(2,1)} %copy.76), channel_id=1, source_target_pairs={{0,4},{2,6},{4,0},{6,2},{8,12},{10,14},{12,8},{14,10},{16,20},{18,... | collective-permute-start | bytes 3145736 | tf_op jit(solution)/shard_map/ppermute | solution.py:960
  295.3 47.7 %collective-permute-start.6 = (bf16[4,128,1024]{2,1,0:T(8,128)(2,1)}, bf16[4,128,1024]{2,1,0:T(8,128)(2,1)}, u32[]{:S(2)}, u32[]{:S(2)}) collective-permute-start(bf16[4,128,1024]{2,1,0:T(8,128)(2,1)} %get-tuple-element.166), channel_id=1, source_target_pairs={{0,1},{1,0},{2,3},{3,2},{4,5},{5,4},{6,7},{7,6},{8,9},{9,8},{10,11... | collective-permute-start | bytes 3145736 | tf_op jit(solution)/shard_map/ppermute | solution.py:1121
  297.0 79.6 %collective-permute-start.8 = (bf16[1024,512]{1,0:T(8,128)(2,1)S(1)}, bf16[1024,512]{1,0:T(8,128)(2,1)}, u32[]{:S(2)}, u32[]{:S(2)}) collective-permute-start(bf16[1024,512]{1,0:T(8,128)(2,1)S(1)} %get-tuple-element.114), channel_id=1, source_target_pairs={{0,16},{2,18},{4,20},{6,22},{8,24},{10,26},{12,28},{14,30},{16,0},... | collective-permute-start | bytes 3145736 | tf_op jit(solution)/shard_map/ppermute | solution.py:956
  298.0 45.0 %copy-start.23 = (f32[256,8,512]{2,1,0:T(8,128)S(1)}, f32[256,8,512]{2,1,0:T(8,128)}, u32[]{:S(2)}) copy-start(f32[256,8,512]{2,1,0:T(8,128)} %copy-done.20) | copy-start | bytes 12582916
  343.1 6.1 %copy-start.56 = (bf16[128,4,128]{0,2,1:T(8,128)(2,1)S(1)}, bf16[128,4,128]{0,2,1:T(8,128)(2,1)}, u32[]{:S(2)}) copy-start(bf16[128,4,128]{0,2,1:T(8,128)(2,1)} %copy-done.55) | copy-start | bytes 393220
  343.1 7.4 %copy-start.52 = (f32[256,8,128]{2,1,0:T(8,128)S(1)}, f32[256,8,128]{2,1,0:T(8,128)}, u32[]{:S(2)}) copy-start(f32[256,8,128]{2,1,0:T(8,128)} %get-tuple-element.113) | copy-start | bytes 3145732
  343.1 33.5 %copy-start.32 = (f32[256,8,512]{2,1,0:T(8,128)S(1)}, f32[256,8,512]{2,1,0:T(8,128)}, u32[]{:S(2)}) copy-start(f32[256,8,512]{2,1,0:T(8,128)} %get-tuple-element.81.delta_ref) | copy-start | bytes 12582916
  349.2 27.4 %copy-start.25 = (f32[256,8,512]{2,1,0:T(8,128)S(1)}, f32[256,8,512]{2,1,0:T(8,128)}, u32[]{:S(2)}) copy-start(f32[256,8,512]{2,1,0:T(8,128)} %get-tuple-element.144.ds_ref) | copy-start | bytes 12582916
  349.9 26.6 %copy-start.24 = (f32[256,8,512]{2,1,0:T(8,128)S(1)}, f32[256,8,512]{2,1,0:T(8,128)}, u32[]{:S(2)}) copy-start(f32[256,8,512]{2,1,0:T(8,128)} %copy-done.20) | copy-start | bytes 12582916
  349.9 26.6 %copy-start.54 = (bf16[160,512]{1,0:T(8,128)(2,1)S(1)}, bf16[160,512]{1,0:T(8,128)(2,1)}, u32[]{:S(2)}) copy-start(bf16[160,512]{1,0:T(8,128)(2,1)} %copy-done.53) | copy-start | bytes 491524
  389.2 4.3 slice-start
  390.3 4.2 copy-start.31
  390.3 4.2 copy-start.62
  390.3 4.2 copy-start.64
  390.3 4.2 copy-start.66
  390.3 4.2 copy-start.68
  394.5 5.9 %copy-start.43 = (bf16[8,256,512]{2,1,0:T(8,128)(2,1)S(1)}, bf16[8,256,512]{2,1,0:T(8,128)(2,1)}, u32[]{:S(2)}) copy-start(bf16[8,256,512]{2,1,0:T(8,128)(2,1)} %copy.50) | copy-start | bytes 6291460
  399.7 9.9 %copy-start.34 = (bf16[256,8,512]{2,1,0:T(8,128)(2,1)}, bf16[256,8,512]{2,1,0:T(8,128)(2,1)S(1)}, u32[]{:S(2)}) copy-start(bf16[256,8,512]{2,1,0:T(8,128)(2,1)S(1)} %get-tuple-element.161) | copy-start | bytes 6291460
  400.4 9.2 %copy-start.47 = (bf16[8,256,512]{2,1,0:T(8,128)(2,1)}, bf16[8,256,512]{2,1,0:T(8,128)(2,1)S(1)}, u32[]{:S(2)}) copy-start(bf16[8,256,512]{2,1,0:T(8,128)(2,1)S(1)} %copy.55) | copy-start | bytes 6291460
  403.4 6.3 %copy-start.38 = (bf16[4,128,1024]{2,1,0:T(8,128)(2,1)S(1)}, bf16[4,128,1024]{2,1,0:T(8,128)(2,1)}, u32[]{:S(2)}) copy-start(bf16[4,128,1024]{2,1,0:T(8,128)(2,1)} %get-tuple-element.116) | copy-start | bytes 3145732
  409.6 4.1 copy-start.39
  409.6 28.4 %collective-permute-start.9 = (bf16[2048,1024]{1,0:T(8,128)(2,1)}, bf16[2048,1024]{1,0:T(8,128)(2,1)}, u32[]{:S(2)}, u32[]{:S(2)}) collective-permute-start(bf16[2048,1024]{1,0:T(8,128)(2,1)} %convolution_convert_fusion.2), channel_id=1, source_target_pairs={{0,2},{2,0},{4,6},{6,4},{8,10},{10,8},{12,14},{14,12},{16,18},{18,... | collective-permute-start | bytes 12582920 | tf_op jit(solution)/shard_map/ppermute | solution.py:960
  412.3 8.6 %copy-start.59 = (f32[1,128,512]{2,1,0:T(8,128)S(1)}, f32[1,128,512]{2,1,0:T(8,128)}, u32[]{:S(2)}) copy-start(f32[1,128,512]{2,1,0:T(8,128)} %get-tuple-element.129) | copy-start | bytes 786436
  412.3 34.0 %collective-permute-start.10 = (bf16[2,128,1024]{2,1,0:T(8,128)(2,1)}, bf16[2,128,1024]{2,1,0:T(8,128)(2,1)S(1)}, u32[]{:S(2)}, u32[]{:S(2)}) collective-permute-start(bf16[2,128,1024]{2,1,0:T(8,128)(2,1)} %get-tuple-element.176), channel_id=1, source_target_pairs={{0,4},{2,6},{4,0},{6,2},{8,12},{10,14},{12,8},{14,10},{16,20},{18,... | collective-permute-start | bytes 1572872 | tf_op jit(solution)/shard_map/ppermute | solution.py:960
  416.2 30.0 %collective-permute-start.11 = (bf16[2,128,1024]{2,1,0:T(8,128)(2,1)}, bf16[2,128,1024]{2,1,0:T(8,128)(2,1)}, u32[]{:S(2)}, u32[]{:S(2)}) collective-permute-start(bf16[2,128,1024]{2,1,0:T(8,128)(2,1)} %get-tuple-element.174), channel_id=1, source_target_pairs={{0,1},{1,0},{2,3},{3,2},{4,5},{5,4},{6,7},{7,6},{8,9},{9,8},{10,11... | collective-permute-start | bytes 1572872 | tf_op jit(solution)/shard_map/ppermute | solution.py:1121
  416.9 8.4 %copy-start.13 = (bf16[2048,128]{1,0:T(8,128)(2,1)S(1)}, bf16[2048,128]{1,0:T(8,128)(2,1)}, u32[]{:S(2)}) copy-start(bf16[2048,128]{1,0:T(8,128)(2,1)} %copy-done.12) | copy-start | bytes 1572868
  422.7 4.8 copy-start.35
  427.5 10.5 %copy-start.18 = (bf16[32,64,1024]{2,1,0:T(8,128)(2,1)S(1)}, bf16[32,64,1024]{2,1,0:T(8,128)(2,1)}, u32[]{:S(2)}) copy-start(bf16[32,64,1024]{2,1,0:T(8,128)(2,1)} %copy-done.16) | copy-start | bytes 12582916
  427.5 10.5 %copy-start.44 = (bf16[8,256,512]{2,1,0:T(8,128)(2,1)S(1)}, bf16[8,256,512]{2,1,0:T(8,128)(2,1)}, u32[]{:S(2)}) copy-start(bf16[8,256,512]{2,1,0:T(8,128)(2,1)} %copy.50) | copy-start | bytes 6291460
  427.5 10.5 %copy-start.48 = (bf16[8,256,512]{2,1,0:T(8,128)(2,1)S(1)}, bf16[8,256,512]{2,1,0:T(8,128)(2,1)}, u32[]{:S(2)}) copy-start(bf16[8,256,512]{2,1,0:T(8,128)(2,1)} %copy-done.47) | copy-start | bytes 6291460
  516.5 7.6 %collective-permute-start.12 = (bf16[256,1024]{1,0:T(8,128)(2,1)S(1)}, bf16[256,1024]{1,0:T(8,128)(2,1)S(1)}, u32[]{:S(2)}, u32[]{:S(2)}) collective-permute-start(bf16[256,1024]{1,0:T(8,128)(2,1)S(1)} %fusion.44), channel_id=1, source_target_pairs={{0,2},{2,0},{4,6},{6,4},{8,10},{10,8},{12,14},{14,12},{16,18},{18,... | collective-permute-start | bytes 1572872 | tf_op jit(solution)/shard_map/ppermute | solution.py:960
  (21 other events, 53.3 us)
